TPU v7x, 32 devices: a whole 2x2x4 slice. The times are simulated.
32 devices in a mesh: cls: 16 (over z, y, x), dp: 2 (over core).
Axes of the slice: x: 2, y: 2, z: 4, core: 2. Of those that a mesh axis runs over, the one named last changes fastest.
Arguments:
- features: bfloat16 [4096, 512], P(('cls', 'dp')), may hold values from -6 to 6
- labels: int32 [4096], P(('cls', 'dp')), may hold values from 0 to 4095, as said below
- weights: float32 [16384, 512], P('cls'), may hold values from -0.25 to 0.25
- sampled: int32 [4096], P('cls'), may hold values from 0 to 1023, as said below
Outputs:
- sample_loss: float32 [4096], P(('cls', 'dp'))
- weight_grad: float32 [4096, 512], P(('cls', 'dp'))
Inputs may be any that keep to these rules, and one draw needn't show every extreme that they name: The owner of a label is label // 256. In the rows of one device (aligned blocks of 128 rows) exactly one owner receives 10 of the labels and every other owner fewer. `sampled`: each aligned block of 256 entries holds distinct rows of the owner's bank.
All inputs are finite; a program needn't handle non-finite values.
Results may differ from a plain program's by a relative error of at most 0.0038.
Values may be sent and summed in bfloat16 or wider, within the bound.
No kernel may reach another device: no remote copies, remote signals or barrier semaphores. Data moves between devices by JAX's collectives and lax.ppermute only.
A program may use at most 64 MiB of HBM per device.

v0:
```python
import functools

import jax
import jax.numpy as jnp
from jax import lax
from jax.experimental import pallas as pl
from jax.experimental.pallas import tpu as pltpu
from jax.sharding import PartitionSpec as P

logit_scale = 64.0
margin = 0.35
epsilon = 1e-06
digit = 256
extra = 8
square = 4

vmem_spec = pl.BlockSpec(memory_space=pltpu.VMEM)
smem_spec = pl.BlockSpec(memory_space=pltpu.SMEM)
hbm_spec = pl.BlockSpec(memory_space=pltpu.HBM)


vmem_bytes = 64 * 1024 * 1024


def params(room):
    return pltpu.CompilerParams(vmem_limit_bytes=vmem_bytes - room * 1024)


def normalized(feat_ref):
    wide = feat_ref[...].astype(jnp.float32)
    squares = jnp.sum(wide * wide, axis=1, keepdims=True)
    return (wide * lax.rsqrt(squares + epsilon)).astype(jnp.bfloat16)


def normalize_kernel(*refs):
    rows = refs[0].shape[0]
    for index, feat_ref in enumerate(refs[:-1]):
        refs[-1][index * rows : (index + 1) * rows, :] = normalized(feat_ref)


def pack_kernel(feat_ref, label_ref, out_ref):
    rows, width = feat_ref.shape
    sets = label_ref.shape[0]
    out_ref[:rows, :] = normalized(feat_ref)
    labels = label_ref[...]
    digits = [labels // digit, labels % digit]
    line = lax.broadcasted_iota(jnp.int32, (extra, width), 0)
    packed = jnp.zeros((extra, width), jnp.float32)
    per_row = width // (2 * rows)
    for first in range(0, sets, per_row):
        pieces = [
            part[index : index + 1, :]
            for index in range(first, min(first + per_row, sets))
            for part in digits
        ]
        if len(pieces) * rows < width:
            pieces.append(jnp.zeros((1, width - len(pieces) * rows), jnp.int32))
        row = jnp.concatenate(pieces, axis=1).astype(jnp.float32)
        packed = jnp.where(line == first // per_row, row, packed)
    out_ref[rows:, :] = packed.astype(jnp.bfloat16)


def labels_of(packed_ref, index):
    rows = packed_ref.shape[0] - extra
    per_row = packed_ref.shape[1] // (2 * rows)
    line, start = index // per_row, index % per_row * 2 * rows
    digits = packed_ref[rows:, :].astype(jnp.float32)[line : line + 1, :].astype(jnp.int32)
    return digits[:, start : start + rows] * digit + digits[:, start + rows : start + 2 * rows]


def choose_kernel(place_ref, sampled_hbm, weight_hbm, low_ref, chosen_ref, sampled_ref, sems):
    part = chosen_ref.shape[0]
    first = place_ref[square] * part
    copy = pltpu.make_async_copy(sampled_hbm, sampled_ref, sems.at[0])
    copy.start()
    copy.wait()

    def start_row(row, carry):
        pltpu.make_async_copy(
            weight_hbm.at[pl.ds(sampled_ref[first + row], 1), :],
            chosen_ref.at[pl.ds(row, 1), :],
            sems.at[1],
        ).start()
        return carry

    lax.fori_loop(0, part, start_row, 0, unroll=32)
    pltpu.make_async_copy(weight_hbm.at[pl.ds(0, part), :], chosen_ref, sems.at[1]).wait()
    rows = chosen_ref[...]
    inverse = lax.rsqrt(jnp.sum(rows * rows, axis=1, keepdims=True) + epsilon)
    low_ref[:part, :] = (rows * inverse).astype(jnp.bfloat16) * logit_scale
    low_ref[part:, :] = jnp.zeros_like(low_ref[part:, :])


def logits_kernel(count, span, held, joined, place_ref, *refs):
    feats = refs[:held]
    if joined:
        rows, earlier_ref = refs[held : held + 2]
        exp_ref, stat_ref, every_ref, label_ref = refs[-4:]
        stat_ref[...] = earlier_ref[...]
    else:
        classes = refs[held : held + square]
        exp_ref, stat_ref, every_ref, label_ref, rows = refs[-5:]
        part = rows.shape[0] // square
        for side in range(square):
            rows[side * part : (side + 1) * part, :] = classes[side][:part, :]
    part = rows.shape[0] // square
    lanes = label_ref.shape[1]
    for index, (_, place, first, source, label_set) in enumerate(span):
        every_ref[index * lanes : (index + 1) * lanes, :] = feats[place][first : first + lanes, :]
        label_ref[index : index + 1, :] = labels_of(feats[source], label_set)
    line = lax.broadcasted_iota(jnp.int32, (part, lanes), 0)
    for pair in range(0, len(span), 2):
        scaled = lax.dot_general(
            rows[...],
            every_ref[pair * lanes : (pair + 2) * lanes, :],
            (((1,), (1,)), ((), ())),
            preferred_element_type=jnp.float32,
        )
        for index in (pair, pair + 1):
            start = (index - pair) * lanes
            labels = label_ref[index : index + 1, :]
            total = jnp.zeros((1, lanes), jnp.float32)
            target = jnp.zeros((1, lanes), jnp.float32)
            for side in range(square):
                lines = slice(side * part, (side + 1) * part)
                hit = labels - place_ref[side] == line
                tile = scaled[lines, start : start + lanes]
                exps = jnp.exp(
                    tile - jnp.where(hit, logit_scale + logit_scale * margin, logit_scale)
                )
                exp_ref[lines, index * lanes : (index + 1) * lanes] = exps
                total = total + jnp.sum(exps, axis=0, keepdims=True)
                target = target + jnp.sum(jnp.where(hit, tile, 0.0), axis=0, keepdims=True)
            group = place_ref[square + 1] ^ span[index][0]
            stat_ref[pl.ds(group, 1), :] = total
            stat_ref[pl.ds(count + group, 1), :] = target


def grads_kernel(count, replicas, spans, sides, place_ref, stat_ref, *refs):
    chunks = [refs[3 * index : 3 * index + 3] for index in range(len(spans))]
    refs = refs[3 * len(spans) :]
    outs, scratch = refs[: len(sides)], refs[-len(spans) :]
    part = chunks[0][0].shape[0] // square
    lanes = stat_ref.shape[1]
    scale = logit_scale / replicas
    group = place_ref[square + 1]
    if 0 in sides:
        refs[len(sides)][...] = (
            logit_scale
            + jnp.log(stat_ref[pl.ds(group, 1), :])
            - (stat_ref[pl.ds(count + group, 1), :] - logit_scale * margin)
        )
    line = lax.broadcasted_iota(jnp.int32, (part, lanes), 0)
    total = None
    for span, (exp_ref, every_ref, label_ref), grads in zip(spans, chunks, scratch):
        for index in range(len(span)):
            inverse = 1.0 / stat_ref[pl.ds(group ^ span[index][0], 1), :]
            columns = slice(index * lanes, (index + 1) * lanes)
            labels = label_ref[index : index + 1, :]
            for place, side in enumerate(sides):
                hit = labels - place_ref[side] == line
                exps = exp_ref[side * part : (side + 1) * part, columns]
                grads[place * part : (place + 1) * part, columns] = (
                    exps * inverse - jnp.where(hit, 1.0, 0.0)
                ).astype(jnp.bfloat16)
        product = jnp.dot(grads[...], every_ref[...], preferred_element_type=jnp.float32)
        total = product if total is None else total + product
    for index, out in enumerate(outs):
        out[...] = (total[index * part : (index + 1) * part, :] * scale).astype(out.dtype)


def finish_kernel(chosen_ref, own_ref, *refs):
    others, out_ref = refs[:-1], refs[-1]
    summed = own_ref[...]
    for other in others:
        summed = summed + other[...].astype(jnp.float32)
    rows = chosen_ref[...]
    inverse = lax.rsqrt(jnp.sum(rows * rows, axis=1, keepdims=True) + epsilon)
    unit = rows * inverse
    radial = jnp.sum(unit * summed, axis=1, keepdims=True)
    out_ref[...] = inverse * (summed - unit * radial)


def per_device(features, labels, weights, sampled):
    groups = lax.axis_size("cls")
    replicas = lax.axis_size("dp")
    local_rows, width = features.shape
    classes = sampled.shape[0]
    part = classes // replicas
    position = lax.axis_index("cls").astype(jnp.int32)
    replica = lax.axis_index("dp").astype(jnp.int32)
    place = jnp.stack(
        [(position ^ side) * classes + replica * part for side in range(square)]
        + [replica, position // square * replicas + replica]
    )

    def swap(value, chip_mask, core_mask):
        mask = chip_mask * replicas + core_mask
        return lax.ppermute(
            value, ("cls", "dp"), [(i, i ^ mask) for i in range(groups * replicas)]
        )

    bits = [(0, 1 << bit) for bit in range(replicas.bit_length() - 1)]
    far_bits = [(1 << bit, 0) for bit in range(2, groups.bit_length() - 1)]

    upper, marks = {0: features}, labels.reshape(1, local_rows)
    for bit, _ in far_bits[1:]:
        upper.update({mask | bit: swap(block, bit, 0) for mask, block in list(upper.items())})
        marks = jnp.concatenate([marks, swap(marks, bit, 0)], axis=0)
    near_raw = swap(features, square, 0)
    low_rows, chosen = pl.pallas_call(
        choose_kernel,
        out_shape=[
            jax.ShapeDtypeStruct((part + extra, width), jnp.bfloat16),
            jax.ShapeDtypeStruct((part, width), jnp.float32),
        ],
        in_specs=[smem_spec, hbm_spec, hbm_spec],
        out_specs=[vmem_spec] * 2,
        scratch_shapes=[pltpu.SMEM((classes,), jnp.int32), pltpu.SemaphoreType.DMA((2,))],
        compiler_params=params(11264),
        name="choose",
    )(place, sampled, weights)
    def spread(block):
        near = [block]
        for _, bit in bits:
            near = near + [swap(value, 0, bit) for value in near]
        return near

    tie = lax.optimization_barrier
    corner_rows, marks = tie((low_rows, marks))
    rows = [low_rows, swap(low_rows, 1, 0), swap(low_rows, 2, 0), swap(corner_rows, 3, 0)]
    tied, near_raw = tie(({mask: block for mask, block in upper.items() if mask}, near_raw))
    upper.update(tied)
    packed = {
        mask: pl.pallas_call(
            pack_kernel,
            out_shape=jax.ShapeDtypeStruct((local_rows + extra, width), jnp.bfloat16),
            in_specs=[vmem_spec] * 2,
            out_specs=vmem_spec,
            compiler_params=params(56 * 1024),
            name="pack",
        )(block, marks)
        for mask, block in upper.items()
        if mask
    }
    pair = pl.pallas_call(
        normalize_kernel,
        out_shape=jax.ShapeDtypeStruct((2 * local_rows, width), jnp.bfloat16),
        in_specs=[vmem_spec] * 2,
        out_specs=vmem_spec,
        compiler_params=params(56 * 1024),
        name="normalize",
    )(features, near_raw)
    passed = {mask | square: swap(block, square, 0) for mask, block in packed.items()}
    rows = tie(rows[::-1])[::-1]
    passed, rows, pair = tie((passed, rows, pair))
    ups = list(packed)
    held = [pair, *packed.values(), *passed.values()]
    spread_out = [spread(array) for array in held]
    count = groups // square * replicas
    order = list(upper)

    def entry(index, first_replica):
        mask, replica_bit = index // replicas * square, index % replicas
        up, beside = mask & ~square, bool(mask & square)
        base = (replica_bit - first_replica) * len(held) + 1 + beside * len(ups)
        source = base + ups.index(groups // 2)
        if up:
            return (index, base + ups.index(up), 0, source, order.index(up))
        return (index, base - 1 - beside * len(ups), beside * local_rows, source, 0)

    spans, arrays = [], []
    for some in (range(1), range(1, replicas)):
        spans.append(
            tuple(entry(index, some[0]) for index in range(count) if index % replicas in some)
        )
        arrays.append([copies[bit] for bit in some for copies in spread_out])
    chunks, carried = [], rows
    for joined, span in enumerate(spans):
        shapes = [
            jax.ShapeDtypeStruct((square * part, len(span) * local_rows), jnp.float32),
            jax.ShapeDtypeStruct((2 * count, local_rows), jnp.float32),
            jax.ShapeDtypeStruct((len(span) * local_rows, width), jnp.bfloat16),
            jax.ShapeDtypeStruct((len(span), local_rows), jnp.int32),
            jax.ShapeDtypeStruct((square * part, width), jnp.bfloat16),
        ][: 5 - joined]
        exps, stats, every, marks, *together = pl.pallas_call(
            functools.partial(logits_kernel, count, span, len(arrays[joined]), joined),
            out_shape=shapes,
            in_specs=[smem_spec] + [vmem_spec] * (len(arrays[joined]) + len(carried)),
            out_specs=[vmem_spec] * len(shapes),
            compiler_params=params(16 * 1024),
            name="logits",
        )(place, *arrays[joined], *carried)
        chunks, carried = chunks + [exps, every, marks], together + [stats]
    near = [(0, 0)]
    for chip_bit, core_bit in bits[:1] + far_bits[:1]:
        near = near + [(chip_mask | chip_bit, core_mask | core_bit) for chip_mask, core_mask in near]
    stats = sum((swap(stats, *masks) for masks in near[1:]), stats)
    for chip_mask, core_mask in bits[1:] + far_bits[1:]:
        stats = stats + swap(stats, chip_mask, core_mask)

    def grads(sides):
        kinds = [jnp.bfloat16 if side else jnp.float32 for side in sides]
        shapes = [jax.ShapeDtypeStruct((part, width), kind) for kind in kinds]
        if 0 in sides:
            shapes.append(jax.ShapeDtypeStruct((1, local_rows), jnp.float32))
        return pl.pallas_call(
            functools.partial(grads_kernel, count, replicas, spans, sides),
            out_shape=shapes,
            in_specs=[smem_spec] + [vmem_spec] * (1 + len(chunks)),
            out_specs=[vmem_spec] * len(shapes),
            scratch_shapes=[
                pltpu.VMEM((len(sides) * part, len(span) * local_rows), jnp.bfloat16)
                for span in spans
            ],
            compiler_params=params(16 * 1024),
            name="grads",
        )(place, stats, *chunks)

    away = [swap(block, side, 0) for side, block in enumerate(grads((1, 2, 3)), 1)]
    mine, loss = grads((0,))
    weight_grad = pl.pallas_call(
        finish_kernel,
        out_shape=jax.ShapeDtypeStruct((part, width), jnp.float32),
        in_specs=[vmem_spec] * (2 + len(away)),
        out_specs=vmem_spec,
        compiler_params=params(56 * 1024),
        name="finish",
    )(chosen, mine, *away)
    return (loss.reshape(local_rows), weight_grad)


def solution(mesh):
    in_specs = (P(("cls", "dp"), None), P(("cls", "dp")), P("cls", None), P("cls"))
    out_specs = (P(("cls", "dp")), P(("cls", "dp"), None))
    return jax.shard_map(
        per_device, mesh=mesh, in_specs=in_specs, out_specs=out_specs, check_vma=False
    )
```

profile of v0, /device:TPU:0, one launch (start us, length us, event | category | flops | bytes accessed | tf_op | source)
XLA Modules:
  0.0 41.9 jit_solution(3750076643215185118)
XLA Ops:
  0.6 0.0 copy-start
  0.6 4.1 %collective-permute-start = (bf16[128,512]{1,0:T(8,128)(2,1)}, bf16[128,512]{1,0:T(8,128)(2,1)S(1)}, u32[]{:S(2)}, u32[]{:S(2)}) collective-permute-start(bf16[128,512]{1,0:T(8,128)(2,1)} %refs_0_.1), channel_id=1, source_target_pairs={{0,16},{1,17},{2,18},{3,19},{4,20},{5,21},{6,22},{7,23},{8,24},{9,... | collective-permute-start | bytes 393224 | tf_op jit(solution)/shard_map/ppermute | solution.py:199
  4.7 1.6 %collective-permute-start.1 = (bf16[128,512]{1,0:T(8,128)(2,1)}, bf16[128,512]{1,0:T(8,128)(2,1)S(1)}, u32[]{:S(2)}, u32[]{:S(2)}) collective-permute-start(bf16[128,512]{1,0:T(8,128)(2,1)} %refs_0_.1), channel_id=1, source_target_pairs={{0,8},{1,9},{2,10},{3,11},{4,12},{5,13},{6,14},{7,15},{8,0},{9,1},... | collective-permute-start | bytes 393224 | tf_op jit(solution)/shard_map/ppermute | solution.py:199
  6.3 0.3 collective-permute-start.2
  6.7 0.1 stack.27.place_ref
  6.7 0.0 copy-start.1
  6.7 0.7 %copy-done.1 = s32[256]{0:T(256)S(1)} copy-done((s32[256]{0:T(256)S(1)}, s32[256]{0:T(256)}, u32[]{:S(2)}) %copy-start.1) | copy-done | bytes 1048
  7.4 2.7 %choose.1 = (bf16[136,512]{1,0:T(8,128)(2,1)S(1)}, f32[128,512]{1,0:T(8,128)S(1)}) custom-call(s32[6]{0:T(128)S(1)} %stack.27.place_ref, s32[256]{0:T(256)S(1)} %copy-done.1, f32[1024,512]{1,0:T(8,128)} %weight_hbm.1), custom_call_target="tpu_custom_call" | custom-call | tf_op jit(solution)/shard_map/choose/pallas_call | solution.py:211
  10.1 1.6 %collective-permute-start.6 = (bf16[136,512]{1,0:T(8,128)(2,1)S(1)}, bf16[136,512]{1,0:T(8,128)(2,1)S(1)}, u32[]{:S(2)}, u32[]{:S(2)}) collective-permute-start(bf16[136,512]{1,0:T(8,128)(2,1)S(1)} %get-tuple-element.43.refs_3_), channel_id=1, source_target_pairs={{0,2},{1,3},{2,0},{3,1},{4,6},{5,7},{6,4},{7,5},{8,10},{9,11},{10,... | collective-permute-start | bytes 417800 | tf_op jit(solution)/shard_map/ppermute | solution.py:199
  11.6 1.5 %collective-permute-start.5 = (bf16[136,512]{1,0:T(8,128)(2,1)S(1)}, bf16[136,512]{1,0:T(8,128)(2,1)S(1)}, u32[]{:S(2)}, u32[]{:S(2)}) collective-permute-start(bf16[136,512]{1,0:T(8,128)(2,1)S(1)} %get-tuple-element.43.refs_3_), channel_id=1, source_target_pairs={{0,4},{1,5},{2,6},{3,7},{4,0},{5,1},{6,2},{7,3},{8,12},{9,13},{10,... | collective-permute-start | bytes 417800 | tf_op jit(solution)/shard_map/ppermute | solution.py:199
  13.2 0.0 collective-permute-done.2
  13.2 0.0 copy-done.2
  13.2 0.8 %collective-permute-start.4 = (bf16[136,512]{1,0:T(8,128)(2,1)S(1)}, bf16[136,512]{1,0:T(8,128)(2,1)S(1)}, u32[]{:S(2)}, u32[]{:S(2)}) collective-permute-start(bf16[136,512]{1,0:T(8,128)(2,1)S(1)} %get-tuple-element.43.refs_3_), channel_id=1, source_target_pairs={{0,6},{1,7},{2,4},{3,5},{4,2},{5,3},{6,0},{7,1},{8,14},{9,15},{10,... | collective-permute-start | bytes 417800 | tf_op jit(solution)/shard_map/ppermute | solution.py:199
  14.0 0.0 collective-permute-done.feat_ref
  14.0 0.0 collective-permute-done.1.refs_1_
  14.0 0.1 pack.1.refs_1_
  14.1 1.5 %collective-permute-start.3 = (bf16[136,512]{1,0:T(8,128)(2,1)S(1)}, bf16[136,512]{1,0:T(8,128)(2,1)S(1)}, u32[]{:S(2)}, u32[]{:S(2)}) collective-permute-start(bf16[136,512]{1,0:T(8,128)(2,1)S(1)} %pack.1.refs_1_), channel_id=1, source_target_pairs={{0,8},{1,9},{2,10},{3,11},{4,12},{5,13},{6,14},{7,15},{8,0},{9,1},... | collective-permute-start | bytes 417800 | tf_op jit(solution)/shard_map/ppermute | solution.py:199
  15.6 0.0 copy-done
  15.6 0.1 normalize.1.refs_0_
  15.8 0.5 %collective-permute-done.6.refs_4_ = bf16[136,512]{1,0:T(8,128)(2,1)S(1)} collective-permute-done((bf16[136,512]{1,0:T(8,128)(2,1)S(1)}, bf16[136,512]{1,0:T(8,128)(2,1)S(1)}, u32[]{:S(2)}, u32[]{:S(2)}) %collective-permute-start.6) | collective-permute-done | bytes 139296 | tf_op jit(solution)/shard_map/ppermute | solution.py:199
  16.2 3.4 %collective-permute-done.5.refs_5_ = bf16[136,512]{1,0:T(8,128)(2,1)S(1)} collective-permute-done((bf16[136,512]{1,0:T(8,128)(2,1)S(1)}, bf16[136,512]{1,0:T(8,128)(2,1)S(1)}, u32[]{:S(2)}, u32[]{:S(2)}) %collective-permute-start.5) | collective-permute-done | bytes 139296 | tf_op jit(solution)/shard_map/ppermute | solution.py:199
  19.7 0.0 collective-permute-done.4.refs_6_
  19.7 0.0 collective-permute-done.3.refs_2_
  19.7 0.0 collective-permute-start.7
  19.7 0.5 %collective-permute-start.8 = (bf16[136,512]{1,0:T(8,128)(2,1)S(1)}, bf16[136,512]{1,0:T(8,128)(2,1)S(1)}, u32[]{:S(2)}, u32[]{:S(2)}) collective-permute-start(bf16[136,512]{1,0:T(8,128)(2,1)S(1)} %pack.1.refs_1_), channel_id=1, source_target_pairs={{0,1},{1,0},{2,3},{3,2},{4,5},{5,4},{6,7},{7,6},{8,9},{9,8},{10,11... | collective-permute-start | bytes 417800 | tf_op jit(solution)/shard_map/ppermute | solution.py:199
  20.2 0.1 collective-permute-start.9
  20.3 1.2 %logits.2 = (f32[512,512]{1,0:T(8,128)S(1)}, f32[16,128]{1,0:T(8,128)S(1)}, bf16[512,512]{1,0:T(8,128)(2,1)S(1)}, s32[4,128]{1,0:T(4,128)S(1)}, bf16[512,512]{1,0:T(8,128)(2,1)S(1)}) custom-call(s32[6]{0:T(128)S(1)} %stack.27.place_ref, bf16[256,512]{1,0:T(8,128)(2,1)S(1)} %normalize.1.refs_0_, bf16[136,512]{1,0:T(8,128)(2,1)S(1)} %pack.1.refs_1_, ...), custom_call_target="tpu_custom_call" | custom-call | tf_op jit(solution)/shard_map/logits/pallas_call | solution.py:287
  21.5 0.0 collective-permute-done.8.refs_1_
  21.5 0.1 collective-permute-done.9.refs_2_
  21.6 0.0 collective-permute-done.7.refs_0_
  21.6 1.2 %logits.3 = (f32[512,512]{1,0:T(8,128)S(1)}, f32[16,128]{1,0:T(8,128)S(1)}, bf16[512,512]{1,0:T(8,128)(2,1)S(1)}, s32[4,128]{1,0:T(4,128)S(1)}) custom-call(s32[6]{0:T(128)S(1)} %stack.27.place_ref, bf16[256,512]{1,0:T(8,128)(2,1)S(1)} %collective-permute-done.7.refs_0_, bf16[136,512]{1,0:T(8,128)(2,1)S(1)} %collective-permute-done.8.refs_1_, ...), custom_call_target="tpu_custom_call" | custom-call | tf_op jit(solution)/shard_map/logits/pallas_call | solution.py:287
  22.8 1.0 %collective-permute-start.12 = (f32[16,128]{1,0:T(8,128)S(1)}, f32[16,128]{1,0:T(8,128)S(1)}, u32[]{:S(2)}, u32[]{:S(2)}) collective-permute-start(f32[16,128]{1,0:T(8,128)S(1)} %get-tuple-element.49), channel_id=1, source_target_pairs={{0,9},{1,8},{2,11},{3,10},{4,13},{5,12},{6,15},{7,14},{8,1},{9,0},... | collective-permute-start | bytes 24584 | tf_op jit(solution)/shard_map/ppermute | solution.py:199
  23.9 1.0 %collective-permute-start.11 = (f32[16,128]{1,0:T(8,128)S(1)}, f32[16,128]{1,0:T(8,128)S(1)}, u32[]{:S(2)}, u32[]{:S(2)}) collective-permute-start(f32[16,128]{1,0:T(8,128)S(1)} %get-tuple-element.49), channel_id=1, source_target_pairs={{0,8},{1,9},{2,10},{3,11},{4,12},{5,13},{6,14},{7,15},{8,0},{9,1},... | collective-permute-start | bytes 24584 | tf_op jit(solution)/shard_map/ppermute | solution.py:199
  24.9 0.0 collective-permute-start.10
  24.9 1.1 %collective-permute-done.12 = f32[16,128]{1,0:T(8,128)S(1)} collective-permute-done((f32[16,128]{1,0:T(8,128)S(1)}, f32[16,128]{1,0:T(8,128)S(1)}, u32[]{:S(2)}, u32[]{:S(2)}) %collective-permute-start.12) | collective-permute-done | bytes 8224 | tf_op jit(solution)/shard_map/ppermute | solution.py:199
  26.0 1.5 %collective-permute-done.11 = f32[16,128]{1,0:T(8,128)S(1)} collective-permute-done((f32[16,128]{1,0:T(8,128)S(1)}, f32[16,128]{1,0:T(8,128)S(1)}, u32[]{:S(2)}, u32[]{:S(2)}) %collective-permute-start.11) | collective-permute-done | bytes 8224 | tf_op jit(solution)/shard_map/ppermute | solution.py:199
  27.5 0.0 collective-permute-done.10
  27.5 2.8 %collective-permute-start.13 = (f32[16,128]{1,0:T(8,128)S(1)}, f32[16,128]{1,0:T(8,128)S(1)}, u32[]{:S(2)}, u32[]{:S(2)}) collective-permute-start(f32[16,128]{1,0:T(8,128)S(1)} %add_add_fusion), channel_id=1, source_target_pairs={{0,16},{1,17},{2,18},{3,19},{4,20},{5,21},{6,22},{7,23},{8,24},{9,... | collective-permute-start | bytes 24584 | tf_op jit(solution)/shard_map/ppermute | solution.py:199
  30.3 1.8 %collective-permute-done.13 = f32[16,128]{1,0:T(8,128)S(1)} collective-permute-done((f32[16,128]{1,0:T(8,128)S(1)}, f32[16,128]{1,0:T(8,128)S(1)}, u32[]{:S(2)}, u32[]{:S(2)}) %collective-permute-start.13) | collective-permute-done | bytes 8224 | tf_op jit(solution)/shard_map/ppermute | solution.py:199
  32.1 1.2 %grads.3 = (bf16[128,512]{1,0:T(8,128)(2,1)S(1)}, bf16[128,512]{1,0:T(8,128)(2,1)S(1)}, bf16[128,512]{1,0:T(8,128)(2,1)S(1)}) custom-call(s32[6]{0:T(128)S(1)} %stack.27.place_ref, f32[16,128]{1,0:T(8,128)S(1)} %add.36.stat_ref, f32[512,512]{1,0:T(8,128)S(1)} %get-tuple-element.50.refs_0_, bf16[512,512]{1,0:T(8,128)(2,1)S(1)} %get-tuple-element.51.refs_1_, ...), custom_call_target="tpu_custom_call" | custom-call | tf_op jit(solution)/shard_map/grads/pallas_call | solution.py:308
  33.3 0.6 %collective-permute-start.14 = (bf16[128,512]{1,0:T(8,128)(2,1)S(1)}, bf16[128,512]{1,0:T(8,128)(2,1)S(1)}, u32[]{:S(2)}, u32[]{:S(2)}) collective-permute-start(bf16[128,512]{1,0:T(8,128)(2,1)S(1)} %get-tuple-element.59), channel_id=1, source_target_pairs={{0,2},{1,3},{2,0},{3,1},{4,6},{5,7},{6,4},{7,5},{8,10},{9,11},{10,... | collective-permute-start | bytes 393224 | tf_op jit(solution)/shard_map/ppermute | solution.py:199
  33.9 1.2 %collective-permute-start.15 = (bf16[128,512]{1,0:T(8,128)(2,1)S(1)}, bf16[128,512]{1,0:T(8,128)(2,1)S(1)}, u32[]{:S(2)}, u32[]{:S(2)}) collective-permute-start(bf16[128,512]{1,0:T(8,128)(2,1)S(1)} %get-tuple-element.60), channel_id=1, source_target_pairs={{0,4},{1,5},{2,6},{3,7},{4,0},{5,1},{6,2},{7,3},{8,12},{9,13},{10,... | collective-permute-start | bytes 393224 | tf_op jit(solution)/shard_map/ppermute | solution.py:199
  35.1 1.7 %collective-permute-start.16 = (bf16[128,512]{1,0:T(8,128)(2,1)S(1)}, bf16[128,512]{1,0:T(8,128)(2,1)S(1)}, u32[]{:S(2)}, u32[]{:S(2)}) collective-permute-start(bf16[128,512]{1,0:T(8,128)(2,1)S(1)} %get-tuple-element.61), channel_id=1, source_target_pairs={{0,6},{1,7},{2,4},{3,5},{4,2},{5,3},{6,0},{7,1},{8,14},{9,15},{10,... | collective-permute-start | bytes 393224 | tf_op jit(solution)/shard_map/ppermute | solution.py:199
  36.9 1.3 %grads.2 = (f32[128,512]{1,0:T(8,128)S(1)}, f32[1,128]{1,0:T(1,128)}) custom-call(s32[6]{0:T(128)S(1)} %stack.27.place_ref, f32[16,128]{1,0:T(8,128)S(1)} %add.36.stat_ref, f32[512,512]{1,0:T(8,128)S(1)} %get-tuple-element.50.refs_0_, bf16[512,512]{1,0:T(8,128)(2,1)S(1)} %get-tuple-element.51.refs_1_, s32[4,128]{1,0:T(4,128)S(1)} %get-tuple-element.52.refs_2_, ...), custom_call_target="tpu_custom_call" | custom-call | tf_op jit(solution)/shard_map/grads/pallas_call | solution.py:308
  38.1 0.2 collective-permute-done.14.refs_0_
  38.4 0.8 %collective-permute-done.15.refs_1_ = bf16[128,512]{1,0:T(8,128)(2,1)S(1)} collective-permute-done((bf16[128,512]{1,0:T(8,128)(2,1)S(1)}, bf16[128,512]{1,0:T(8,128)(2,1)S(1)}, u32[]{:S(2)}, u32[]{:S(2)}) %collective-permute-start.15) | collective-permute-done | bytes 131104 | tf_op jit(solution)/shard_map/ppermute | solution.py:199
  39.2 1.9 %collective-permute-done.16.refs_2_ = bf16[128,512]{1,0:T(8,128)(2,1)S(1)} collective-permute-done((bf16[128,512]{1,0:T(8,128)(2,1)S(1)}, bf16[128,512]{1,0:T(8,128)(2,1)S(1)}, u32[]{:S(2)}, u32[]{:S(2)}) %collective-permute-start.16) | collective-permute-done | bytes 131104 | tf_op jit(solution)/shard_map/ppermute | solution.py:199
  41.0 0.9 %finish.1 = f32[128,512]{1,0:T(8,128)} custom-call(f32[128,512]{1,0:T(8,128)S(1)} %get-tuple-element.57.chosen_ref, f32[128,512]{1,0:T(8,128)S(1)} %get-tuple-element.58.own_ref, bf16[128,512]{1,0:T(8,128)(2,1)S(1)} %collective-permute-done.14.refs_0_, bf16[128,512]{1,0:T(8,128)(2,1)S(1)} %collective-permute-done.15.refs_1_, ...), custom_call_target="tpu_custom_call" | custom-call | tf_op jit(solution)/shard_map/finish/pallas_call | solution.py:323
  (4 shorter events, 0.0 us)
Async XLA Ops:
  0.6 15.0 %copy-start = (bf16[128,512]{1,0:T(8,128)(2,1)S(1)}, bf16[128,512]{1,0:T(8,128)(2,1)}, u32[]{:S(2)}) copy-start(bf16[128,512]{1,0:T(8,128)(2,1)} %refs_0_.1) | copy-start | bytes 393220
  0.6 13.4 %collective-permute-start = (bf16[128,512]{1,0:T(8,128)(2,1)}, bf16[128,512]{1,0:T(8,128)(2,1)S(1)}, u32[]{:S(2)}, u32[]{:S(2)}) collective-permute-start(bf16[128,512]{1,0:T(8,128)(2,1)} %refs_0_.1), channel_id=1, source_target_pairs={{0,16},{1,17},{2,18},{3,19},{4,20},{5,21},{6,22},{7,23},{8,24},{9,... | collective-permute-start | bytes 393224 | tf_op jit(solution)/shard_map/ppermute | solution.py:199
  4.7 9.3 %collective-permute-start.1 = (bf16[128,512]{1,0:T(8,128)(2,1)}, bf16[128,512]{1,0:T(8,128)(2,1)S(1)}, u32[]{:S(2)}, u32[]{:S(2)}) collective-permute-start(bf16[128,512]{1,0:T(8,128)(2,1)} %refs_0_.1), channel_id=1, source_target_pairs={{0,8},{1,9},{2,10},{3,11},{4,12},{5,13},{6,14},{7,15},{8,0},{9,1},... | collective-permute-start | bytes 393224 | tf_op jit(solution)/shard_map/ppermute | solution.py:199
  6.3 6.9 %collective-permute-start.2 = (s32[1,128]{1,0:T(1,128)}, s32[1,128]{1,0:T(1,128)S(1)}, u32[]{:S(2)}, u32[]{:S(2)}) collective-permute-start(s32[1,128]{1,0:T(1,128)} %bitcast.8), channel_id=1, source_target_pairs={{0,16},{1,17},{2,18},{3,19},{4,20},{5,21},{6,22},{7,23},{8,24},{9,... | collective-permute-start | bytes 1544 | tf_op jit(solution)/shard_map/ppermute | solution.py:199
  6.7 0.7 %copy-start.1 = (s32[256]{0:T(256)S(1)}, s32[256]{0:T(256)}, u32[]{:S(2)}) copy-start(s32[256]{0:T(256)} %sampled_hbm.1) | copy-start | bytes 3076
  7.4 5.8 %copy-start.2 = (s32[128]{0:T(128)S(1)}, s32[128]{0:T(128)}, u32[]{:S(2)}) copy-start(s32[128]{0:T(128)} %param.5) | copy-start | bytes 1540
  10.1 6.2 %collective-permute-start.6 = (bf16[136,512]{1,0:T(8,128)(2,1)S(1)}, bf16[136,512]{1,0:T(8,128)(2,1)S(1)}, u32[]{:S(2)}, u32[]{:S(2)}) collective-permute-start(bf16[136,512]{1,0:T(8,128)(2,1)S(1)} %get-tuple-element.43.refs_3_), channel_id=1, source_target_pairs={{0,2},{1,3},{2,0},{3,1},{4,6},{5,7},{6,4},{7,5},{8,10},{9,11},{10,... | collective-permute-start | bytes 417800 | tf_op jit(solution)/shard_map/ppermute | solution.py:199
  11.6 8.0 %collective-permute-start.5 = (bf16[136,512]{1,0:T(8,128)(2,1)S(1)}, bf16[136,512]{1,0:T(8,128)(2,1)S(1)}, u32[]{:S(2)}, u32[]{:S(2)}) collective-permute-start(bf16[136,512]{1,0:T(8,128)(2,1)S(1)} %get-tuple-element.43.refs_3_), channel_id=1, source_target_pairs={{0,4},{1,5},{2,6},{3,7},{4,0},{5,1},{6,2},{7,3},{8,12},{9,13},{10,... | collective-permute-start | bytes 417800 | tf_op jit(solution)/shard_map/ppermute | solution.py:199
  13.2 6.5 %collective-permute-start.4 = (bf16[136,512]{1,0:T(8,128)(2,1)S(1)}, bf16[136,512]{1,0:T(8,128)(2,1)S(1)}, u32[]{:S(2)}, u32[]{:S(2)}) collective-permute-start(bf16[136,512]{1,0:T(8,128)(2,1)S(1)} %get-tuple-element.43.refs_3_), channel_id=1, source_target_pairs={{0,6},{1,7},{2,4},{3,5},{4,2},{5,3},{6,0},{7,1},{8,14},{9,15},{10,... | collective-permute-start | bytes 417800 | tf_op jit(solution)/shard_map/ppermute | solution.py:199
  14.1 5.6 %collective-permute-start.3 = (bf16[136,512]{1,0:T(8,128)(2,1)S(1)}, bf16[136,512]{1,0:T(8,128)(2,1)S(1)}, u32[]{:S(2)}, u32[]{:S(2)}) collective-permute-start(bf16[136,512]{1,0:T(8,128)(2,1)S(1)} %pack.1.refs_1_), channel_id=1, source_target_pairs={{0,8},{1,9},{2,10},{3,11},{4,12},{5,13},{6,14},{7,15},{8,0},{9,1},... | collective-permute-start | bytes 417800 | tf_op jit(solution)/shard_map/ppermute | solution.py:199
  19.7 1.9 %collective-permute-start.7 = (bf16[256,512]{1,0:T(8,128)(2,1)S(1)}, bf16[256,512]{1,0:T(8,128)(2,1)S(1)}, u32[]{:S(2)}, u32[]{:S(2)}) collective-permute-start(bf16[256,512]{1,0:T(8,128)(2,1)S(1)} %normalize.1.refs_0_), channel_id=1, source_target_pairs={{0,1},{1,0},{2,3},{3,2},{4,5},{5,4},{6,7},{7,6},{8,9},{9,8},{10,11... | collective-permute-start | bytes 786440 | tf_op jit(solution)/shard_map/ppermute | solution.py:199
  19.7 1.8 %collective-permute-start.8 = (bf16[136,512]{1,0:T(8,128)(2,1)S(1)}, bf16[136,512]{1,0:T(8,128)(2,1)S(1)}, u32[]{:S(2)}, u32[]{:S(2)}) collective-permute-start(bf16[136,512]{1,0:T(8,128)(2,1)S(1)} %pack.1.refs_1_), channel_id=1, source_target_pairs={{0,1},{1,0},{2,3},{3,2},{4,5},{5,4},{6,7},{7,6},{8,9},{9,8},{10,11... | collective-permute-start | bytes 417800 | tf_op jit(solution)/shard_map/ppermute | solution.py:199
  20.2 1.4 %collective-permute-start.9 = (bf16[136,512]{1,0:T(8,128)(2,1)S(1)}, bf16[136,512]{1,0:T(8,128)(2,1)S(1)}, u32[]{:S(2)}, u32[]{:S(2)}) collective-permute-start(bf16[136,512]{1,0:T(8,128)(2,1)S(1)} %collective-permute-done.3.refs_2_), channel_id=1, source_target_pairs={{0,1},{1,0},{2,3},{3,2},{4,5},{5,4},{6,7},{7,6},{8,9},{9,8},{10,11... | collective-permute-start | bytes 417800 | tf_op jit(solution)/shard_map/ppermute | solution.py:199
  22.8 3.1 %collective-permute-start.12 = (f32[16,128]{1,0:T(8,128)S(1)}, f32[16,128]{1,0:T(8,128)S(1)}, u32[]{:S(2)}, u32[]{:S(2)}) collective-permute-start(f32[16,128]{1,0:T(8,128)S(1)} %get-tuple-element.49), channel_id=1, source_target_pairs={{0,9},{1,8},{2,11},{3,10},{4,13},{5,12},{6,15},{7,14},{8,1},{9,0},... | collective-permute-start | bytes 24584 | tf_op jit(solution)/shard_map/ppermute | solution.py:199
  23.9 3.7 %collective-permute-start.11 = (f32[16,128]{1,0:T(8,128)S(1)}, f32[16,128]{1,0:T(8,128)S(1)}, u32[]{:S(2)}, u32[]{:S(2)}) collective-permute-start(f32[16,128]{1,0:T(8,128)S(1)} %get-tuple-element.49), channel_id=1, source_target_pairs={{0,8},{1,9},{2,10},{3,11},{4,12},{5,13},{6,14},{7,15},{8,0},{9,1},... | collective-permute-start | bytes 24584 | tf_op jit(solution)/shard_map/ppermute | solution.py:199
  24.9 2.6 %collective-permute-start.10 = (f32[16,128]{1,0:T(8,128)S(1)}, f32[16,128]{1,0:T(8,128)S(1)}, u32[]{:S(2)}, u32[]{:S(2)}) collective-permute-start(f32[16,128]{1,0:T(8,128)S(1)} %get-tuple-element.49), channel_id=1, source_target_pairs={{0,1},{1,0},{2,3},{3,2},{4,5},{5,4},{6,7},{7,6},{8,9},{9,8},{10,11... | collective-permute-start | bytes 24584 | tf_op jit(solution)/shard_map/ppermute | solution.py:199
  27.5 4.6 %collective-permute-start.13 = (f32[16,128]{1,0:T(8,128)S(1)}, f32[16,128]{1,0:T(8,128)S(1)}, u32[]{:S(2)}, u32[]{:S(2)}) collective-permute-start(f32[16,128]{1,0:T(8,128)S(1)} %add_add_fusion), channel_id=1, source_target_pairs={{0,16},{1,17},{2,18},{3,19},{4,20},{5,21},{6,22},{7,23},{8,24},{9,... | collective-permute-start | bytes 24584 | tf_op jit(solution)/shard_map/ppermute | solution.py:199
  33.3 5.0 %collective-permute-start.14 = (bf16[128,512]{1,0:T(8,128)(2,1)S(1)}, bf16[128,512]{1,0:T(8,128)(2,1)S(1)}, u32[]{:S(2)}, u32[]{:S(2)}) collective-permute-start(bf16[128,512]{1,0:T(8,128)(2,1)S(1)} %get-tuple-element.59), channel_id=1, source_target_pairs={{0,2},{1,3},{2,0},{3,1},{4,6},{5,7},{6,4},{7,5},{8,10},{9,11},{10,... | collective-permute-start | bytes 393224 | tf_op jit(solution)/shard_map/ppermute | solution.py:199
  33.9 5.2 %collective-permute-start.15 = (bf16[128,512]{1,0:T(8,128)(2,1)S(1)}, bf16[128,512]{1,0:T(8,128)(2,1)S(1)}, u32[]{:S(2)}, u32[]{:S(2)}) collective-permute-start(bf16[128,512]{1,0:T(8,128)(2,1)S(1)} %get-tuple-element.60), channel_id=1, source_target_pairs={{0,4},{1,5},{2,6},{3,7},{4,0},{5,1},{6,2},{7,3},{8,12},{9,13},{10,... | collective-permute-start | bytes 393224 | tf_op jit(solution)/shard_map/ppermute | solution.py:199
  35.1 5.9 %collective-permute-start.16 = (bf16[128,512]{1,0:T(8,128)(2,1)S(1)}, bf16[128,512]{1,0:T(8,128)(2,1)S(1)}, u32[]{:S(2)}, u32[]{:S(2)}) collective-permute-start(bf16[128,512]{1,0:T(8,128)(2,1)S(1)} %get-tuple-element.61), channel_id=1, source_target_pairs={{0,6},{1,7},{2,4},{3,5},{4,2},{5,3},{6,0},{7,1},{8,14},{9,15},{10,... | collective-permute-start | bytes 393224 | tf_op jit(solution)/shard_map/ppermute | solution.py:199
where the time goes:
time: 42.1 us; the launch traced here: 41.9 us
  starting transfers between devices  20.3 us (48%)
  waiting for transfers between devices  11.4 us (27%)
  Pallas kernels  8.68 us (21%)
  local copies, waits for them, and re-layouts  0.77 us (2%)
  between operations  0.72 us (2%)
    ppermute x17, starting transfers between devices, swap(): lax.ppermute(value, ('cls', 'dp'), [(i, i ^ mask) for i in range(groups *...  20.3 us
    ppermute x17, waiting for transfers between devices, swap(): lax.ppermute(value, ('cls', 'dp'), [(i, i ^ mask) for i in range(groups *...  11.4 us
    pallas_call x1, Pallas kernels, per_device(): pl.pallas_call(choose_kernel, out_shape=[jax.ShapeDtypeStruct((part + ext...  2.66 us
    pallas_call x2, Pallas kernels, per_device(): pl.pallas_call(functools.partial(logits_kernel, count, span, len(arrays[j...  2.44 us
    pallas_call x2, Pallas kernels, grads(): pl.pallas_call(functools.partial(grads_kernel, count, replicas, spans, si...  2.42 us
    pallas_call x1, Pallas kernels, per_device(): pl.pallas_call(finish_kernel, out_shape=jax.ShapeDtypeStruct((part, width...  0.91 us
  transfers between devices with their start and end apart: 17, of which 9 were waited for; matrix products, arithmetic and copies ran while one was open for 0% of the time, Pallas kernels for 13%

commit v1 on v0

--- a/solution.py
+++ b/solution.py
@@ -68,23 +68,8 @@
     return digits[:, start : start + rows] * digit + digits[:, start + rows : start + 2 * rows]
 
 
-def choose_kernel(place_ref, sampled_hbm, weight_hbm, low_ref, chosen_ref, sampled_ref, sems):
+def choose_kernel(chosen_ref, low_ref):
     part = chosen_ref.shape[0]
-    first = place_ref[square] * part
-    copy = pltpu.make_async_copy(sampled_hbm, sampled_ref, sems.at[0])
-    copy.start()
-    copy.wait()
-
-    def start_row(row, carry):
-        pltpu.make_async_copy(
-            weight_hbm.at[pl.ds(sampled_ref[first + row], 1), :],
-            chosen_ref.at[pl.ds(row, 1), :],
-            sems.at[1],
-        ).start()
-        return carry
-
-    lax.fori_loop(0, part, start_row, 0, unroll=32)
-    pltpu.make_async_copy(weight_hbm.at[pl.ds(0, part), :], chosen_ref, sems.at[1]).wait()
     rows = chosen_ref[...]
     inverse = lax.rsqrt(jnp.sum(rows * rows, axis=1, keepdims=True) + epsilon)
     low_ref[:part, :] = (rows * inverse).astype(jnp.bfloat16) * logit_scale
@@ -208,18 +193,16 @@
         upper.update({mask | bit: swap(block, bit, 0) for mask, block in list(upper.items())})
         marks = jnp.concatenate([marks, swap(marks, bit, 0)], axis=0)
     near_raw = swap(features, square, 0)
-    low_rows, chosen = pl.pallas_call(
+    mine = lax.dynamic_slice_in_dim(sampled, replica * part, part)
+    chosen = weights.at[mine].get(mode="promise_in_bounds", unique_indices=True)
+    low_rows = pl.pallas_call(
         choose_kernel,
-        out_shape=[
-            jax.ShapeDtypeStruct((part + extra, width), jnp.bfloat16),
-            jax.ShapeDtypeStruct((part, width), jnp.float32),
-        ],
-        in_specs=[smem_spec, hbm_spec, hbm_spec],
-        out_specs=[vmem_spec] * 2,
-        scratch_shapes=[pltpu.SMEM((classes,), jnp.int32), pltpu.SemaphoreType.DMA((2,))],
-        compiler_params=params(11264),
+        out_shape=jax.ShapeDtypeStruct((part + extra, width), jnp.bfloat16),
+        in_specs=[vmem_spec],
+        out_specs=vmem_spec,
+        compiler_params=params(16 * 1024),
         name="choose",
-    )(place, sampled, weights)
+    )(chosen)
     def spread(block):
         near = [block]
         for _, bit in bits:
@@ -319,7 +302,7 @@
         )(place, stats, *chunks)
 
     away = [swap(block, side, 0) for side, block in enumerate(grads((1, 2, 3)), 1)]
-    mine, loss = grads((0,))
+    own_part, loss = grads((0,))
     weight_grad = pl.pallas_call(
         finish_kernel,
         out_shape=jax.ShapeDtypeStruct((part, width), jnp.float32),
@@ -327,7 +310,7 @@
         out_specs=vmem_spec,
         compiler_params=params(56 * 1024),
         name="finish",
-    )(chosen, mine, *away)
+    )(chosen, own_part, *away)
     return (loss.reshape(local_rows), weight_grad)
 
 

time: 42.1 us -> 44.3 us (1.052)
  local copies, waits for them, and re-layouts: 0.77 us -> 4.76 us
  waiting for transfers between devices: 11.4 us -> 8.66 us
  starting transfers between devices: 20.3 us -> 22.1 us
  Pallas kernels: 8.68 us -> 6.94 us
  other arithmetic: 0.02 us -> 0.78 us
    unnamed x6 -> x14, local copies, waits for them, and re-layouts: 0.69 us -> 3.92 us
    ppermute x17, waiting for transfers between devices: 11.4 us -> 8.66 us  [swap(): lax.ppermute(value, ('cls', 'dp'), [(i, i ^ mask) for i in range(groups *...]
    pallas_call x1, Pallas kernels: 2.66 us -> 0.12 us  [per_device(): pl.pallas_call(choose_kernel, out_shape=jax.ShapeDtypeStruct((part + extr...]
    ppermute x17, starting transfers between devices: 20.3 us -> 22.1 us  [swap(): lax.ppermute(value, ('cls', 'dp'), [(i, i ^ mask) for i in range(groups *...]
    pallas_call x2, Pallas kernels: 2.44 us -> 3.26 us  [per_device(): pl.pallas_call(functools.partial(logits_kernel, count, span, len(arrays[j...]
    gather x0 -> x1, local copies, waits for them, and re-layouts: none -> 0.76 us  [per_device(): chosen = weights.at[mine].get(mode='promise_in_bounds', unique_indices=True)]
    select_n x0 -> x1, other arithmetic: none -> 0.75 us  [per_device(): chosen = weights.at[mine].get(mode='promise_in_bounds', unique_indices=True)]
  transfers between devices with their start and end apart: 17 -> 17, of which waited for: 9 -> 8; matrix products, arithmetic and copies ran while one was open for 0% -> 4% of each run, Pallas kernels for 13% -> 7%
where the time goes in v1:
time: 44.3 us; the launch traced here: 44 us
  starting transfers between devices  22.1 us (50%)
  waiting for transfers between devices  8.66 us (20%)
  Pallas kernels  6.94 us (16%)
  local copies, waits for them, and re-layouts  4.76 us (11%)
  other arithmetic  0.78 us (2%)
  between operations  0.77 us (2%)
    ppermute x17, starting transfers between devices, swap(): lax.ppermute(value, ('cls', 'dp'), [(i, i ^ mask) for i in range(groups *...  22.1 us
    ppermute x17, waiting for transfers between devices, swap(): lax.ppermute(value, ('cls', 'dp'), [(i, i ^ mask) for i in range(groups *...  8.66 us
    unnamed x14, local copies, waits for them, and re-layouts  3.92 us
    pallas_call x2, Pallas kernels, per_device(): pl.pallas_call(functools.partial(logits_kernel, count, span, len(arrays[j...  3.26 us
    pallas_call x2, Pallas kernels, grads(): pl.pallas_call(functools.partial(grads_kernel, count, replicas, spans, si...  2.41 us
    pallas_call x1, Pallas kernels, per_device(): pl.pallas_call(finish_kernel, out_shape=jax.ShapeDtypeStruct((part, width...  0.9 us
  transfers between devices with their start and end apart: 17, of which 8 were waited for; matrix products, arithmetic and copies ran while one was open for 4% of the time, Pallas kernels for 7%

profile of v1, /device:TPU:0, one launch (start us, length us, event | category | flops | bytes accessed | tf_op | source)
XLA Modules:
  0.0 44.0 jit_solution(5147373309216244694)
XLA Ops:
  0.6 0.0 copy-start
  0.7 4.1 %collective-permute-start = (bf16[128,512]{1,0:T(8,128)(2,1)}, bf16[128,512]{1,0:T(8,128)(2,1)S(1)}, u32[]{:S(2)}, u32[]{:S(2)}) collective-permute-start(bf16[128,512]{1,0:T(8,128)(2,1)} %refs_0_.1), channel_id=1, source_target_pairs={{0,16},{1,17},{2,18},{3,19},{4,20},{5,21},{6,22},{7,23},{8,24},{9,... | collective-permute-start | bytes 393224 | tf_op jit(solution)/shard_map/ppermute | solution.py:184
  4.8 1.6 %collective-permute-start.1 = (bf16[128,512]{1,0:T(8,128)(2,1)}, bf16[128,512]{1,0:T(8,128)(2,1)S(1)}, u32[]{:S(2)}, u32[]{:S(2)}) collective-permute-start(bf16[128,512]{1,0:T(8,128)(2,1)} %refs_0_.1), channel_id=1, source_target_pairs={{0,8},{1,9},{2,10},{3,11},{4,12},{5,13},{6,14},{7,15},{8,0},{9,1},... | collective-permute-start | bytes 393224 | tf_op jit(solution)/shard_map/ppermute | solution.py:184
  6.3 0.3 collective-permute-start.2
  6.7 0.8 %compare_select_fusion = s32[128]{0:T(128)S(1)} fusion(s32[256]{0:T(256)} %param.7, s32[]{:T(128)S(6)} %select_n.12), kind=kLoop, calls=%fused_computation.3 | loop fusion | flops 384 | bytes 1028 | tf_op jit(solution)/shard_map/select_n | solution.py:197
  7.4 0.8 %gather_fusion = f32[128,512]{1,0:T(8,128)S(1)} fusion(f32[1024,512]{1,0:T(8,128)S(1)} %copy-done, s32[1024]{0:T(1024)S(1)} %pad_clamp_fusion), kind=kCustom, calls=%fused_computation | custom fusion | bytes 524800 | tf_op jit(solution)/shard_map/gather | solution.py:197
  8.2 0.1 choose.1.refs_3_
  8.3 1.6 %collective-permute-start.6 = (bf16[136,512]{1,0:T(8,128)(2,1)S(1)}, bf16[136,512]{1,0:T(8,128)(2,1)S(1)}, u32[]{:S(2)}, u32[]{:S(2)}) collective-permute-start(bf16[136,512]{1,0:T(8,128)(2,1)S(1)} %choose.1.refs_3_), channel_id=1, source_target_pairs={{0,2},{1,3},{2,0},{3,1},{4,6},{5,7},{6,4},{7,5},{8,10},{9,11},{10,... | collective-permute-start | bytes 417800 | tf_op jit(solution)/shard_map/ppermute | solution.py:184
  9.9 1.5 %collective-permute-start.5 = (bf16[136,512]{1,0:T(8,128)(2,1)S(1)}, bf16[136,512]{1,0:T(8,128)(2,1)S(1)}, u32[]{:S(2)}, u32[]{:S(2)}) collective-permute-start(bf16[136,512]{1,0:T(8,128)(2,1)S(1)} %choose.1.refs_3_), channel_id=1, source_target_pairs={{0,4},{1,5},{2,6},{3,7},{4,0},{5,1},{6,2},{7,3},{8,12},{9,13},{10,... | collective-permute-start | bytes 417800 | tf_op jit(solution)/shard_map/ppermute | solution.py:184
  11.4 0.1 collective-permute-done.2
  11.5 2.6 %collective-permute-start.4 = (bf16[136,512]{1,0:T(8,128)(2,1)S(1)}, bf16[136,512]{1,0:T(8,128)(2,1)S(1)}, u32[]{:S(2)}, u32[]{:S(2)}) collective-permute-start(bf16[136,512]{1,0:T(8,128)(2,1)S(1)} %choose.1.refs_3_), channel_id=1, source_target_pairs={{0,6},{1,7},{2,4},{3,5},{4,2},{5,3},{6,0},{7,1},{8,14},{9,15},{10,... | collective-permute-start | bytes 417800 | tf_op jit(solution)/shard_map/ppermute | solution.py:184
  14.0 0.0 collective-permute-done.feat_ref
  14.0 0.0 collective-permute-done.1.refs_1_
  14.0 0.1 pack.1.refs_1_
  14.1 0.5 %copy-done.4 = bf16[128,512]{1,0:T(8,128)(2,1)} copy-done((bf16[128,512]{1,0:T(8,128)(2,1)}, bf16[128,512]{1,0:T(8,128)(2,1)S(1)}, u32[]{:S(2)}) %copy-start.4) | copy-done | bytes 131096
  14.7 1.4 %collective-permute-start.3 = (bf16[136,512]{1,0:T(8,128)(2,1)S(1)}, bf16[136,512]{1,0:T(8,128)(2,1)}, u32[]{:S(2)}, u32[]{:S(2)}) collective-permute-start(bf16[136,512]{1,0:T(8,128)(2,1)S(1)} %pack.1.refs_1_), channel_id=1, source_target_pairs={{0,8},{1,9},{2,10},{3,11},{4,12},{5,13},{6,14},{7,15},{8,0},{9,1},... | collective-permute-start | bytes 417800 | tf_op jit(solution)/shard_map/ppermute | solution.py:184
  16.1 0.9 %copy-done.3 = bf16[128,512]{1,0:T(8,128)(2,1)S(1)} copy-done((bf16[128,512]{1,0:T(8,128)(2,1)S(1)}, bf16[128,512]{1,0:T(8,128)(2,1)}, u32[]{:S(2)}) %copy-start.3) | copy-done | bytes 131096
  17.0 0.9 %copy-done.5 = bf16[128,512]{1,0:T(8,128)(2,1)S(1)} copy-done((bf16[128,512]{1,0:T(8,128)(2,1)S(1)}, bf16[128,512]{1,0:T(8,128)(2,1)}, u32[]{:S(2)}) %copy-start.5) | copy-done | bytes 131096
  17.9 0.1 normalize.1.refs_0_
  18.1 0.0 collective-permute-done.6.refs_4_
  18.1 0.0 collective-permute-done.5.refs_5_
  18.1 0.0 collective-permute-done.4.refs_6_
  18.1 0.0 copy-start.1
  18.1 0.6 %copy-done.1 = bf16[136,512]{1,0:T(8,128)(2,1)} copy-done((bf16[136,512]{1,0:T(8,128)(2,1)}, bf16[136,512]{1,0:T(8,128)(2,1)S(1)}, u32[]{:S(2)}) %copy-start.1) | copy-done | bytes 139288
  18.8 1.1 %collective-permute-done.3.refs_2_ = bf16[136,512]{1,0:T(8,128)(2,1)} collective-permute-done((bf16[136,512]{1,0:T(8,128)(2,1)S(1)}, bf16[136,512]{1,0:T(8,128)(2,1)}, u32[]{:S(2)}, u32[]{:S(2)}) %collective-permute-start.3) | collective-permute-done | bytes 139296 | tf_op jit(solution)/shard_map/ppermute | solution.py:184
  19.8 0.5 %collective-permute-start.8 = (bf16[136,512]{1,0:T(8,128)(2,1)S(1)}, bf16[136,512]{1,0:T(8,128)(2,1)}, u32[]{:S(2)}, u32[]{:S(2)}) collective-permute-start(bf16[136,512]{1,0:T(8,128)(2,1)S(1)} %pack.1.refs_1_), channel_id=1, source_target_pairs={{0,1},{1,0},{2,3},{3,2},{4,5},{5,4},{6,7},{7,6},{8,9},{9,8},{10,11... | collective-permute-start | bytes 417800 | tf_op jit(solution)/shard_map/ppermute | solution.py:184
  20.4 0.0 collective-permute-start.9
  20.4 0.1 stack.27.place_ref
  20.4 0.9 %copy-done.2 = bf16[136,512]{1,0:T(8,128)(2,1)S(1)} copy-done((bf16[136,512]{1,0:T(8,128)(2,1)S(1)}, bf16[136,512]{1,0:T(8,128)(2,1)}, u32[]{:S(2)}) %copy-start.2) | copy-done | bytes 139288
  21.4 1.6 %logits.2 = (f32[512,512]{1,0:T(8,128)S(1)}, f32[16,128]{1,0:T(8,128)S(1)}, bf16[512,512]{1,0:T(8,128)(2,1)S(1)}, s32[4,128]{1,0:T(4,128)S(1)}, bf16[512,512]{1,0:T(8,128)(2,1)S(1)}) custom-call(s32[6]{0:T(128)S(1)} %stack.27.place_ref, bf16[256,512]{1,0:T(8,128)(2,1)S(1)} %normalize.1.refs_0_, bf16[136,512]{1,0:T(8,128)(2,1)S(1)} %pack.1.refs_1_, ...), custom_call_target="tpu_custom_call" | custom-call | tf_op jit(solution)/shard_map/logits/pallas_call | solution.py:270
  23.0 0.0 collective-permute-done.8.refs_1_
  23.0 0.0 collective-permute-done.7.refs_0_
  23.0 1.7 %logits.3 = (f32[512,512]{1,0:T(8,128)S(1)}, f32[16,128]{1,0:T(8,128)S(1)}, bf16[512,512]{1,0:T(8,128)(2,1)S(1)}, s32[4,128]{1,0:T(4,128)S(1)}) custom-call(s32[6]{0:T(128)S(1)} %stack.27.place_ref, bf16[256,512]{1,0:T(8,128)(2,1)S(1)} %collective-permute-done.7.refs_0_, bf16[136,512]{1,0:T(8,128)(2,1)} %collective-permute-done.8.refs_1_, ...), custom_call_target="tpu_custom_call" | custom-call | tf_op jit(solution)/shard_map/logits/pallas_call | solution.py:270
  24.7 1.6 %collective-permute-start.12 = (f32[16,128]{1,0:T(8,128)S(1)}, f32[16,128]{1,0:T(8,128)S(1)}, u32[]{:S(2)}, u32[]{:S(2)}) collective-permute-start(f32[16,128]{1,0:T(8,128)S(1)} %get-tuple-element.46), channel_id=1, source_target_pairs={{0,9},{1,8},{2,11},{3,10},{4,13},{5,12},{6,15},{7,14},{8,1},{9,0},... | collective-permute-start | bytes 24584 | tf_op jit(solution)/shard_map/ppermute | solution.py:184
  26.3 0.6 %collective-permute-start.11 = (f32[16,128]{1,0:T(8,128)S(1)}, f32[16,128]{1,0:T(8,128)S(1)}, u32[]{:S(2)}, u32[]{:S(2)}) collective-permute-start(f32[16,128]{1,0:T(8,128)S(1)} %get-tuple-element.46), channel_id=1, source_target_pairs={{0,8},{1,9},{2,10},{3,11},{4,12},{5,13},{6,14},{7,15},{8,0},{9,1},... | collective-permute-start | bytes 24584 | tf_op jit(solution)/shard_map/ppermute | solution.py:184
  26.9 0.9 %collective-permute-done.12 = f32[16,128]{1,0:T(8,128)S(1)} collective-permute-done((f32[16,128]{1,0:T(8,128)S(1)}, f32[16,128]{1,0:T(8,128)S(1)}, u32[]{:S(2)}, u32[]{:S(2)}) %collective-permute-start.12) | collective-permute-done | bytes 8224 | tf_op jit(solution)/shard_map/ppermute | solution.py:184
  27.8 2.1 %collective-permute-done.11 = f32[16,128]{1,0:T(8,128)S(1)} collective-permute-done((f32[16,128]{1,0:T(8,128)S(1)}, f32[16,128]{1,0:T(8,128)S(1)}, u32[]{:S(2)}, u32[]{:S(2)}) %collective-permute-start.11) | collective-permute-done | bytes 8224 | tf_op jit(solution)/shard_map/ppermute | solution.py:184
  29.9 2.8 %collective-permute-start.13 = (f32[16,128]{1,0:T(8,128)S(1)}, f32[16,128]{1,0:T(8,128)S(1)}, u32[]{:S(2)}, u32[]{:S(2)}) collective-permute-start(f32[16,128]{1,0:T(8,128)S(1)} %add_add_fusion), channel_id=1, source_target_pairs={{0,16},{1,17},{2,18},{3,19},{4,20},{5,21},{6,22},{7,23},{8,24},{9,... | collective-permute-start | bytes 24584 | tf_op jit(solution)/shard_map/ppermute | solution.py:184
  32.7 1.8 %collective-permute-done.13 = f32[16,128]{1,0:T(8,128)S(1)} collective-permute-done((f32[16,128]{1,0:T(8,128)S(1)}, f32[16,128]{1,0:T(8,128)S(1)}, u32[]{:S(2)}, u32[]{:S(2)}) %collective-permute-start.13) | collective-permute-done | bytes 8224 | tf_op jit(solution)/shard_map/ppermute | solution.py:184
  34.6 1.2 %grads.3 = (bf16[128,512]{1,0:T(8,128)(2,1)S(1)}, bf16[128,512]{1,0:T(8,128)(2,1)S(1)}, bf16[128,512]{1,0:T(8,128)(2,1)S(1)}) custom-call(s32[6]{0:T(128)S(1)} %stack.27.place_ref, f32[16,128]{1,0:T(8,128)S(1)} %add.48.stat_ref, f32[512,512]{1,0:T(8,128)S(1)} %get-tuple-element.47.refs_0_, bf16[512,512]{1,0:T(8,128)(2,1)S(1)} %get-tuple-element.48.refs_1_, ...), custom_call_target="tpu_custom_call" | custom-call | tf_op jit(solution)/shard_map/grads/pallas_call | solution.py:291
  35.7 0.6 %collective-permute-start.14 = (bf16[128,512]{1,0:T(8,128)(2,1)S(1)}, bf16[128,512]{1,0:T(8,128)(2,1)S(1)}, u32[]{:S(2)}, u32[]{:S(2)}) collective-permute-start(bf16[128,512]{1,0:T(8,128)(2,1)S(1)} %get-tuple-element.55), channel_id=1, source_target_pairs={{0,2},{1,3},{2,0},{3,1},{4,6},{5,7},{6,4},{7,5},{8,10},{9,11},{10,... | collective-permute-start | bytes 393224 | tf_op jit(solution)/shard_map/ppermute | solution.py:184
  36.3 0.9 %collective-permute-start.15 = (bf16[128,512]{1,0:T(8,128)(2,1)S(1)}, bf16[128,512]{1,0:T(8,128)(2,1)S(1)}, u32[]{:S(2)}, u32[]{:S(2)}) collective-permute-start(bf16[128,512]{1,0:T(8,128)(2,1)S(1)} %get-tuple-element.56), channel_id=1, source_target_pairs={{0,4},{1,5},{2,6},{3,7},{4,0},{5,1},{6,2},{7,3},{8,12},{9,13},{10,... | collective-permute-start | bytes 393224 | tf_op jit(solution)/shard_map/ppermute | solution.py:184
  37.3 2.0 %collective-permute-start.16 = (bf16[128,512]{1,0:T(8,128)(2,1)S(1)}, bf16[128,512]{1,0:T(8,128)(2,1)S(1)}, u32[]{:S(2)}, u32[]{:S(2)}) collective-permute-start(bf16[128,512]{1,0:T(8,128)(2,1)S(1)} %get-tuple-element.57), channel_id=1, source_target_pairs={{0,6},{1,7},{2,4},{3,5},{4,2},{5,3},{6,0},{7,1},{8,14},{9,15},{10,... | collective-permute-start | bytes 393224 | tf_op jit(solution)/shard_map/ppermute | solution.py:184
  39.3 1.3 %grads.2 = (f32[128,512]{1,0:T(8,128)S(1)}, f32[1,128]{1,0:T(1,128)}) custom-call(s32[6]{0:T(128)S(1)} %stack.27.place_ref, f32[16,128]{1,0:T(8,128)S(1)} %add.48.stat_ref, f32[512,512]{1,0:T(8,128)S(1)} %get-tuple-element.47.refs_0_, bf16[512,512]{1,0:T(8,128)(2,1)S(1)} %get-tuple-element.48.refs_1_, s32[4,128]{1,0:T(4,128)S(1)} %get-tuple-element.49.refs_2_, ...), custom_call_target="tpu_custom_call" | custom-call | tf_op jit(solution)/shard_map/grads/pallas_call | solution.py:291
  40.5 0.2 collective-permute-done.14.refs_0_
  40.8 0.6 %collective-permute-done.15.refs_1_ = bf16[128,512]{1,0:T(8,128)(2,1)S(1)} collective-permute-done((bf16[128,512]{1,0:T(8,128)(2,1)S(1)}, bf16[128,512]{1,0:T(8,128)(2,1)S(1)}, u32[]{:S(2)}, u32[]{:S(2)}) %collective-permute-start.15) | collective-permute-done | bytes 131104 | tf_op jit(solution)/shard_map/ppermute | solution.py:184
  41.3 1.8 %collective-permute-done.16.refs_2_ = bf16[128,512]{1,0:T(8,128)(2,1)S(1)} collective-permute-done((bf16[128,512]{1,0:T(8,128)(2,1)S(1)}, bf16[128,512]{1,0:T(8,128)(2,1)S(1)}, u32[]{:S(2)}, u32[]{:S(2)}) %collective-permute-start.16) | collective-permute-done | bytes 131104 | tf_op jit(solution)/shard_map/ppermute | solution.py:184
  43.1 0.9 %finish.1 = f32[128,512]{1,0:T(8,128)} custom-call(f32[128,512]{1,0:T(8,128)S(1)} %gather_fusion, f32[128,512]{1,0:T(8,128)S(1)} %get-tuple-element.54.own_ref, bf16[128,512]{1,0:T(8,128)(2,1)S(1)} %collective-permute-done.14.refs_0_, bf16[128,512]{1,0:T(8,128)(2,1)S(1)} %collective-permute-done.15.refs_1_, bf16[128,512]{1,0:T(8,128)(2,1)S(1)} %collective-permute-done.16.refs_2_), custom_call_target="tpu_custom_call" | custom-call | tf_op jit(solution)/shard_map/finish/pallas_call | solution.py:306
  (15 shorter events, 0.0 us)
Async XLA Ops:
  0.6 6.8 %copy-start = (f32[1024,512]{1,0:T(8,128)S(1)}, f32[1024,512]{1,0:T(8,128)}, u32[]{:S(2)}) copy-start(f32[1024,512]{1,0:T(8,128)} %param.6) | copy-start | bytes 6291460
  0.6 10.8 %copy-start.6 = (s32[128]{0:T(128)S(1)}, s32[128]{0:T(128)}, u32[]{:S(2)}) copy-start(s32[128]{0:T(128)} %param.5) | copy-start | bytes 1540
  0.7 13.4 %collective-permute-start = (bf16[128,512]{1,0:T(8,128)(2,1)}, bf16[128,512]{1,0:T(8,128)(2,1)S(1)}, u32[]{:S(2)}, u32[]{:S(2)}) collective-permute-start(bf16[128,512]{1,0:T(8,128)(2,1)} %refs_0_.1), channel_id=1, source_target_pairs={{0,16},{1,17},{2,18},{3,19},{4,20},{5,21},{6,22},{7,23},{8,24},{9,... | collective-permute-start | bytes 393224 | tf_op jit(solution)/shard_map/ppermute | solution.py:184
  4.8 9.3 %collective-permute-start.1 = (bf16[128,512]{1,0:T(8,128)(2,1)}, bf16[128,512]{1,0:T(8,128)(2,1)S(1)}, u32[]{:S(2)}, u32[]{:S(2)}) collective-permute-start(bf16[128,512]{1,0:T(8,128)(2,1)} %refs_0_.1), channel_id=1, source_target_pairs={{0,8},{1,9},{2,10},{3,11},{4,12},{5,13},{6,14},{7,15},{8,0},{9,1},... | collective-permute-start | bytes 393224 | tf_op jit(solution)/shard_map/ppermute | solution.py:184
  6.3 5.1 %collective-permute-start.2 = (s32[1,128]{1,0:T(1,128)}, s32[1,128]{1,0:T(1,128)S(1)}, u32[]{:S(2)}, u32[]{:S(2)}) collective-permute-start(s32[1,128]{1,0:T(1,128)} %bitcast.8), channel_id=1, source_target_pairs={{0,16},{1,17},{2,18},{3,19},{4,20},{5,21},{6,22},{7,23},{8,24},{9,... | collective-permute-start | bytes 1544 | tf_op jit(solution)/shard_map/ppermute | solution.py:184
  8.3 9.8 %collective-permute-start.6 = (bf16[136,512]{1,0:T(8,128)(2,1)S(1)}, bf16[136,512]{1,0:T(8,128)(2,1)S(1)}, u32[]{:S(2)}, u32[]{:S(2)}) collective-permute-start(bf16[136,512]{1,0:T(8,128)(2,1)S(1)} %choose.1.refs_3_), channel_id=1, source_target_pairs={{0,2},{1,3},{2,0},{3,1},{4,6},{5,7},{6,4},{7,5},{8,10},{9,11},{10,... | collective-permute-start | bytes 417800 | tf_op jit(solution)/shard_map/ppermute | solution.py:184
  9.9 8.2 %collective-permute-start.5 = (bf16[136,512]{1,0:T(8,128)(2,1)S(1)}, bf16[136,512]{1,0:T(8,128)(2,1)S(1)}, u32[]{:S(2)}, u32[]{:S(2)}) collective-permute-start(bf16[136,512]{1,0:T(8,128)(2,1)S(1)} %choose.1.refs_3_), channel_id=1, source_target_pairs={{0,4},{1,5},{2,6},{3,7},{4,0},{5,1},{6,2},{7,3},{8,12},{9,13},{10,... | collective-permute-start | bytes 417800 | tf_op jit(solution)/shard_map/ppermute | solution.py:184
  11.5 6.6 %collective-permute-start.4 = (bf16[136,512]{1,0:T(8,128)(2,1)S(1)}, bf16[136,512]{1,0:T(8,128)(2,1)S(1)}, u32[]{:S(2)}, u32[]{:S(2)}) collective-permute-start(bf16[136,512]{1,0:T(8,128)(2,1)S(1)} %choose.1.refs_3_), channel_id=1, source_target_pairs={{0,6},{1,7},{2,4},{3,5},{4,2},{5,3},{6,0},{7,1},{8,14},{9,15},{10,... | collective-permute-start | bytes 417800 | tf_op jit(solution)/shard_map/ppermute | solution.py:184
  14.0 0.7 %copy-start.4 = (bf16[128,512]{1,0:T(8,128)(2,1)}, bf16[128,512]{1,0:T(8,128)(2,1)S(1)}, u32[]{:S(2)}) copy-start(bf16[128,512]{1,0:T(8,128)(2,1)S(1)} %collective-permute-done.1.refs_1_) | copy-start | bytes 393220
  14.7 5.2 %collective-permute-start.3 = (bf16[136,512]{1,0:T(8,128)(2,1)S(1)}, bf16[136,512]{1,0:T(8,128)(2,1)}, u32[]{:S(2)}, u32[]{:S(2)}) collective-permute-start(bf16[136,512]{1,0:T(8,128)(2,1)S(1)} %pack.1.refs_1_), channel_id=1, source_target_pairs={{0,8},{1,9},{2,10},{3,11},{4,12},{5,13},{6,14},{7,15},{8,0},{9,1},... | collective-permute-start | bytes 417800 | tf_op jit(solution)/shard_map/ppermute | solution.py:184
  16.1 0.9 %copy-start.3 = (bf16[128,512]{1,0:T(8,128)(2,1)S(1)}, bf16[128,512]{1,0:T(8,128)(2,1)}, u32[]{:S(2)}) copy-start(bf16[128,512]{1,0:T(8,128)(2,1)} %refs_0_.1) | copy-start | bytes 393220
  17.0 0.9 %copy-start.5 = (bf16[128,512]{1,0:T(8,128)(2,1)S(1)}, bf16[128,512]{1,0:T(8,128)(2,1)}, u32[]{:S(2)}) copy-start(bf16[128,512]{1,0:T(8,128)(2,1)} %copy-done.4) | copy-start | bytes 393220
  18.1 0.7 %copy-start.1 = (bf16[136,512]{1,0:T(8,128)(2,1)}, bf16[136,512]{1,0:T(8,128)(2,1)S(1)}, u32[]{:S(2)}) copy-start(bf16[136,512]{1,0:T(8,128)(2,1)S(1)} %collective-permute-done.4.refs_6_) | copy-start | bytes 417796
  19.8 3.1 %collective-permute-start.7 = (bf16[256,512]{1,0:T(8,128)(2,1)S(1)}, bf16[256,512]{1,0:T(8,128)(2,1)S(1)}, u32[]{:S(2)}, u32[]{:S(2)}) collective-permute-start(bf16[256,512]{1,0:T(8,128)(2,1)S(1)} %normalize.1.refs_0_), channel_id=1, source_target_pairs={{0,1},{1,0},{2,3},{3,2},{4,5},{5,4},{6,7},{7,6},{8,9},{9,8},{10,11... | collective-permute-start | bytes 786440 | tf_op jit(solution)/shard_map/ppermute | solution.py:184
  19.8 3.1 %collective-permute-start.8 = (bf16[136,512]{1,0:T(8,128)(2,1)S(1)}, bf16[136,512]{1,0:T(8,128)(2,1)}, u32[]{:S(2)}, u32[]{:S(2)}) collective-permute-start(bf16[136,512]{1,0:T(8,128)(2,1)S(1)} %pack.1.refs_1_), channel_id=1, source_target_pairs={{0,1},{1,0},{2,3},{3,2},{4,5},{5,4},{6,7},{7,6},{8,9},{9,8},{10,11... | collective-permute-start | bytes 417800 | tf_op jit(solution)/shard_map/ppermute | solution.py:184
  20.4 2.6 %collective-permute-start.9 = (bf16[136,512]{1,0:T(8,128)(2,1)}, bf16[136,512]{1,0:T(8,128)(2,1)}, u32[]{:S(2)}, u32[]{:S(2)}) collective-permute-start(bf16[136,512]{1,0:T(8,128)(2,1)} %collective-permute-done.3.refs_2_), channel_id=1, source_target_pairs={{0,1},{1,0},{2,3},{3,2},{4,5},{5,4},{6,7},{7,6},{8,9},{9,8},{10,11... | collective-permute-start | bytes 417800 | tf_op jit(solution)/shard_map/ppermute | solution.py:184
  20.4 0.9 %copy-start.2 = (bf16[136,512]{1,0:T(8,128)(2,1)S(1)}, bf16[136,512]{1,0:T(8,128)(2,1)}, u32[]{:S(2)}) copy-start(bf16[136,512]{1,0:T(8,128)(2,1)} %copy-done.1) | copy-start | bytes 417796
  24.7 3.1 %collective-permute-start.12 = (f32[16,128]{1,0:T(8,128)S(1)}, f32[16,128]{1,0:T(8,128)S(1)}, u32[]{:S(2)}, u32[]{:S(2)}) collective-permute-start(f32[16,128]{1,0:T(8,128)S(1)} %get-tuple-element.46), channel_id=1, source_target_pairs={{0,9},{1,8},{2,11},{3,10},{4,13},{5,12},{6,15},{7,14},{8,1},{9,0},... | collective-permute-start | bytes 24584 | tf_op jit(solution)/shard_map/ppermute | solution.py:184
  26.3 3.7 %collective-permute-start.11 = (f32[16,128]{1,0:T(8,128)S(1)}, f32[16,128]{1,0:T(8,128)S(1)}, u32[]{:S(2)}, u32[]{:S(2)}) collective-permute-start(f32[16,128]{1,0:T(8,128)S(1)} %get-tuple-element.46), channel_id=1, source_target_pairs={{0,8},{1,9},{2,10},{3,11},{4,12},{5,13},{6,14},{7,15},{8,0},{9,1},... | collective-permute-start | bytes 24584 | tf_op jit(solution)/shard_map/ppermute | solution.py:184
  26.9 3.1 %collective-permute-start.10 = (f32[16,128]{1,0:T(8,128)S(1)}, f32[16,128]{1,0:T(8,128)S(1)}, u32[]{:S(2)}, u32[]{:S(2)}) collective-permute-start(f32[16,128]{1,0:T(8,128)S(1)} %get-tuple-element.46), channel_id=1, source_target_pairs={{0,1},{1,0},{2,3},{3,2},{4,5},{5,4},{6,7},{7,6},{8,9},{9,8},{10,11... | collective-permute-start | bytes 24584 | tf_op jit(solution)/shard_map/ppermute | solution.py:184
  29.9 4.6 %collective-permute-start.13 = (f32[16,128]{1,0:T(8,128)S(1)}, f32[16,128]{1,0:T(8,128)S(1)}, u32[]{:S(2)}, u32[]{:S(2)}) collective-permute-start(f32[16,128]{1,0:T(8,128)S(1)} %add_add_fusion), channel_id=1, source_target_pairs={{0,16},{1,17},{2,18},{3,19},{4,20},{5,21},{6,22},{7,23},{8,24},{9,... | collective-permute-start | bytes 24584 | tf_op jit(solution)/shard_map/ppermute | solution.py:184
  35.7 5.0 %collective-permute-start.14 = (bf16[128,512]{1,0:T(8,128)(2,1)S(1)}, bf16[128,512]{1,0:T(8,128)(2,1)S(1)}, u32[]{:S(2)}, u32[]{:S(2)}) collective-permute-start(bf16[128,512]{1,0:T(8,128)(2,1)S(1)} %get-tuple-element.55), channel_id=1, source_target_pairs={{0,2},{1,3},{2,0},{3,1},{4,6},{5,7},{6,4},{7,5},{8,10},{9,11},{10,... | collective-permute-start | bytes 393224 | tf_op jit(solution)/shard_map/ppermute | solution.py:184
  36.3 5.0 %collective-permute-start.15 = (bf16[128,512]{1,0:T(8,128)(2,1)S(1)}, bf16[128,512]{1,0:T(8,128)(2,1)S(1)}, u32[]{:S(2)}, u32[]{:S(2)}) collective-permute-start(bf16[128,512]{1,0:T(8,128)(2,1)S(1)} %get-tuple-element.56), channel_id=1, source_target_pairs={{0,4},{1,5},{2,6},{3,7},{4,0},{5,1},{6,2},{7,3},{8,12},{9,13},{10,... | collective-permute-start | bytes 393224 | tf_op jit(solution)/shard_map/ppermute | solution.py:184
  37.3 5.9 %collective-permute-start.16 = (bf16[128,512]{1,0:T(8,128)(2,1)S(1)}, bf16[128,512]{1,0:T(8,128)(2,1)S(1)}, u32[]{:S(2)}, u32[]{:S(2)}) collective-permute-start(bf16[128,512]{1,0:T(8,128)(2,1)S(1)} %get-tuple-element.57), channel_id=1, source_target_pairs={{0,6},{1,7},{2,4},{3,5},{4,2},{5,3},{6,0},{7,1},{8,14},{9,15},{10,... | collective-permute-start | bytes 393224 | tf_op jit(solution)/shard_map/ppermute | solution.py:184

commit v2 on v0

--- a/solution.py
+++ b/solution.py
@@ -253,7 +253,7 @@
     )(features, near_raw)
     passed = {mask | square: swap(block, square, 0) for mask, block in packed.items()}
     rows = tie(rows[::-1])[::-1]
-    passed, rows, pair = tie((passed, rows, pair))
+    passed, rows = tie((passed, rows))
     ups = list(packed)
     held = [pair, *packed.values(), *passed.values()]
     spread_out = [spread(array) for array in held]

time: 42.1 us -> 41.6 us (0.988)
  no operation moved by 1% of the time
where the time goes in v2:
time: 41.6 us; the launch traced here: 41.4 us
  starting transfers between devices  20 us (48%)
  waiting for transfers between devices  11.1 us (27%)
  Pallas kernels  8.69 us (21%)
  local copies, waits for them, and re-layouts  0.77 us (2%)
  between operations  0.73 us (2%)
    ppermute x17, starting transfers between devices, swap(): lax.ppermute(value, ('cls', 'dp'), [(i, i ^ mask) for i in range(groups *...  20 us
    ppermute x17, waiting for transfers between devices, swap(): lax.ppermute(value, ('cls', 'dp'), [(i, i ^ mask) for i in range(groups *...  11.1 us
    pallas_call x1, Pallas kernels, per_device(): pl.pallas_call(choose_kernel, out_shape=[jax.ShapeDtypeStruct((part + ext...  2.66 us
    pallas_call x2, Pallas kernels, per_device(): pl.pallas_call(functools.partial(logits_kernel, count, span, len(arrays[j...  2.44 us
    pallas_call x2, Pallas kernels, grads(): pl.pallas_call(functools.partial(grads_kernel, count, replicas, spans, si...  2.44 us
    pallas_call x1, Pallas kernels, per_device(): pl.pallas_call(finish_kernel, out_shape=jax.ShapeDtypeStruct((part, width...  0.91 us
  transfers between devices with their start and end apart: 17, of which 9 were waited for; matrix products, arithmetic and copies ran while one was open for 0% of the time, Pallas kernels for 13%

profile of v2, /device:TPU:0, one launch (start us, length us, event | category | flops | bytes accessed | tf_op | source)
XLA Modules:
  0.0 41.4 jit_solution(16549958287502140025)
XLA Ops:
  0.6 0.0 copy-start
  0.6 4.1 %collective-permute-start = (bf16[128,512]{1,0:T(8,128)(2,1)}, bf16[128,512]{1,0:T(8,128)(2,1)S(1)}, u32[]{:S(2)}, u32[]{:S(2)}) collective-permute-start(bf16[128,512]{1,0:T(8,128)(2,1)} %refs_0_.1), channel_id=1, source_target_pairs={{0,16},{1,17},{2,18},{3,19},{4,20},{5,21},{6,22},{7,23},{8,24},{9,... | collective-permute-start | bytes 393224 | tf_op jit(solution)/shard_map/ppermute | solution.py:199
  4.7 1.6 %collective-permute-start.1 = (bf16[128,512]{1,0:T(8,128)(2,1)}, bf16[128,512]{1,0:T(8,128)(2,1)S(1)}, u32[]{:S(2)}, u32[]{:S(2)}) collective-permute-start(bf16[128,512]{1,0:T(8,128)(2,1)} %refs_0_.1), channel_id=1, source_target_pairs={{0,8},{1,9},{2,10},{3,11},{4,12},{5,13},{6,14},{7,15},{8,0},{9,1},... | collective-permute-start | bytes 393224 | tf_op jit(solution)/shard_map/ppermute | solution.py:199
  6.3 0.3 collective-permute-start.3
  6.7 0.1 stack.27.place_ref
  6.7 0.0 copy-start.1
  6.7 0.7 %copy-done.1 = s32[256]{0:T(256)S(1)} copy-done((s32[256]{0:T(256)S(1)}, s32[256]{0:T(256)}, u32[]{:S(2)}) %copy-start.1) | copy-done | bytes 1048
  7.4 2.7 %choose.1 = (bf16[136,512]{1,0:T(8,128)(2,1)S(1)}, f32[128,512]{1,0:T(8,128)S(1)}) custom-call(s32[6]{0:T(128)S(1)} %stack.27.place_ref, s32[256]{0:T(256)S(1)} %copy-done.1, f32[1024,512]{1,0:T(8,128)} %weight_hbm.1), custom_call_target="tpu_custom_call" | custom-call | tf_op jit(solution)/shard_map/choose/pallas_call | solution.py:211
  10.1 1.6 %collective-permute-start.8 = (bf16[136,512]{1,0:T(8,128)(2,1)S(1)}, bf16[136,512]{1,0:T(8,128)(2,1)S(1)}, u32[]{:S(2)}, u32[]{:S(2)}) collective-permute-start(bf16[136,512]{1,0:T(8,128)(2,1)S(1)} %get-tuple-element.41.refs_3_), channel_id=1, source_target_pairs={{0,2},{1,3},{2,0},{3,1},{4,6},{5,7},{6,4},{7,5},{8,10},{9,11},{10,... | collective-permute-start | bytes 417800 | tf_op jit(solution)/shard_map/ppermute | solution.py:199
  11.6 1.5 %collective-permute-start.7 = (bf16[136,512]{1,0:T(8,128)(2,1)S(1)}, bf16[136,512]{1,0:T(8,128)(2,1)S(1)}, u32[]{:S(2)}, u32[]{:S(2)}) collective-permute-start(bf16[136,512]{1,0:T(8,128)(2,1)S(1)} %get-tuple-element.41.refs_3_), channel_id=1, source_target_pairs={{0,4},{1,5},{2,6},{3,7},{4,0},{5,1},{6,2},{7,3},{8,12},{9,13},{10,... | collective-permute-start | bytes 417800 | tf_op jit(solution)/shard_map/ppermute | solution.py:199
  13.2 0.0 collective-permute-done.3
  13.2 0.0 copy-done.2
  13.2 0.8 %collective-permute-start.6 = (bf16[136,512]{1,0:T(8,128)(2,1)S(1)}, bf16[136,512]{1,0:T(8,128)(2,1)S(1)}, u32[]{:S(2)}, u32[]{:S(2)}) collective-permute-start(bf16[136,512]{1,0:T(8,128)(2,1)S(1)} %get-tuple-element.41.refs_3_), channel_id=1, source_target_pairs={{0,6},{1,7},{2,4},{3,5},{4,2},{5,3},{6,0},{7,1},{8,14},{9,15},{10,... | collective-permute-start | bytes 417800 | tf_op jit(solution)/shard_map/ppermute | solution.py:199
  14.0 0.0 collective-permute-done.feat_ref
  14.0 0.0 collective-permute-done.1.refs_1_
  14.0 0.1 pack.1.refs_1_
  14.1 1.5 %collective-permute-start.5 = (bf16[136,512]{1,0:T(8,128)(2,1)S(1)}, bf16[136,512]{1,0:T(8,128)(2,1)S(1)}, u32[]{:S(2)}, u32[]{:S(2)}) collective-permute-start(bf16[136,512]{1,0:T(8,128)(2,1)S(1)} %pack.1.refs_1_), channel_id=1, source_target_pairs={{0,8},{1,9},{2,10},{3,11},{4,12},{5,13},{6,14},{7,15},{8,0},{9,1},... | collective-permute-start | bytes 417800 | tf_op jit(solution)/shard_map/ppermute | solution.py:199
  15.6 0.0 copy-done
  15.6 0.1 normalize.1.refs_0_
  15.8 0.1 collective-permute-start.2
  15.8 0.4 collective-permute-done.8.refs_4_
  16.2 0.1 collective-permute-start.4
  16.3 3.3 %collective-permute-done.7.refs_5_ = bf16[136,512]{1,0:T(8,128)(2,1)S(1)} collective-permute-done((bf16[136,512]{1,0:T(8,128)(2,1)S(1)}, bf16[136,512]{1,0:T(8,128)(2,1)S(1)}, u32[]{:S(2)}, u32[]{:S(2)}) %collective-permute-start.7) | collective-permute-done | bytes 139296 | tf_op jit(solution)/shard_map/ppermute | solution.py:199
  19.7 0.0 collective-permute-done.6.refs_6_
  19.7 0.0 collective-permute-done.5.refs_2_
  19.7 0.0 collective-permute-start.9
  19.7 1.2 %logits.2 = (f32[512,512]{1,0:T(8,128)S(1)}, f32[16,128]{1,0:T(8,128)S(1)}, bf16[512,512]{1,0:T(8,128)(2,1)S(1)}, s32[4,128]{1,0:T(4,128)S(1)}, bf16[512,512]{1,0:T(8,128)(2,1)S(1)}) custom-call(s32[6]{0:T(128)S(1)} %stack.27.place_ref, bf16[256,512]{1,0:T(8,128)(2,1)S(1)} %normalize.1.refs_0_, bf16[136,512]{1,0:T(8,128)(2,1)S(1)} %pack.1.refs_1_, ...), custom_call_target="tpu_custom_call" | custom-call | tf_op jit(solution)/shard_map/logits/pallas_call | solution.py:287
  20.9 0.0 collective-permute-done.4.refs_1_
  20.9 0.0 collective-permute-done.2.refs_0_
  21.0 0.1 collective-permute-done.9.refs_2_
  21.0 1.2 %logits.3 = (f32[512,512]{1,0:T(8,128)S(1)}, f32[16,128]{1,0:T(8,128)S(1)}, bf16[512,512]{1,0:T(8,128)(2,1)S(1)}, s32[4,128]{1,0:T(4,128)S(1)}) custom-call(s32[6]{0:T(128)S(1)} %stack.27.place_ref, bf16[256,512]{1,0:T(8,128)(2,1)S(1)} %collective-permute-done.2.refs_0_, bf16[136,512]{1,0:T(8,128)(2,1)S(1)} %collective-permute-done.4.refs_1_, ...), custom_call_target="tpu_custom_call" | custom-call | tf_op jit(solution)/shard_map/logits/pallas_call | solution.py:287
  22.3 1.1 %collective-permute-start.12 = (f32[16,128]{1,0:T(8,128)S(1)}, f32[16,128]{1,0:T(8,128)S(1)}, u32[]{:S(2)}, u32[]{:S(2)}) collective-permute-start(f32[16,128]{1,0:T(8,128)S(1)} %get-tuple-element.47), channel_id=1, source_target_pairs={{0,9},{1,8},{2,11},{3,10},{4,13},{5,12},{6,15},{7,14},{8,1},{9,0},... | collective-permute-start | bytes 24584 | tf_op jit(solution)/shard_map/ppermute | solution.py:199
  23.4 1.0 %collective-permute-start.11 = (f32[16,128]{1,0:T(8,128)S(1)}, f32[16,128]{1,0:T(8,128)S(1)}, u32[]{:S(2)}, u32[]{:S(2)}) collective-permute-start(f32[16,128]{1,0:T(8,128)S(1)} %get-tuple-element.47), channel_id=1, source_target_pairs={{0,8},{1,9},{2,10},{3,11},{4,12},{5,13},{6,14},{7,15},{8,0},{9,1},... | collective-permute-start | bytes 24584 | tf_op jit(solution)/shard_map/ppermute | solution.py:199
  24.4 0.0 collective-permute-start.10
  24.4 1.0 %collective-permute-done.12 = f32[16,128]{1,0:T(8,128)S(1)} collective-permute-done((f32[16,128]{1,0:T(8,128)S(1)}, f32[16,128]{1,0:T(8,128)S(1)}, u32[]{:S(2)}, u32[]{:S(2)}) %collective-permute-start.12) | collective-permute-done | bytes 8224 | tf_op jit(solution)/shard_map/ppermute | solution.py:199
  25.4 1.6 %collective-permute-done.11 = f32[16,128]{1,0:T(8,128)S(1)} collective-permute-done((f32[16,128]{1,0:T(8,128)S(1)}, f32[16,128]{1,0:T(8,128)S(1)}, u32[]{:S(2)}, u32[]{:S(2)}) %collective-permute-start.11) | collective-permute-done | bytes 8224 | tf_op jit(solution)/shard_map/ppermute | solution.py:199
  27.0 0.0 collective-permute-done.10
  27.0 2.8 %collective-permute-start.13 = (f32[16,128]{1,0:T(8,128)S(1)}, f32[16,128]{1,0:T(8,128)S(1)}, u32[]{:S(2)}, u32[]{:S(2)}) collective-permute-start(f32[16,128]{1,0:T(8,128)S(1)} %add_add_fusion), channel_id=1, source_target_pairs={{0,16},{1,17},{2,18},{3,19},{4,20},{5,21},{6,22},{7,23},{8,24},{9,... | collective-permute-start | bytes 24584 | tf_op jit(solution)/shard_map/ppermute | solution.py:199
  29.8 1.8 %collective-permute-done.13 = f32[16,128]{1,0:T(8,128)S(1)} collective-permute-done((f32[16,128]{1,0:T(8,128)S(1)}, f32[16,128]{1,0:T(8,128)S(1)}, u32[]{:S(2)}, u32[]{:S(2)}) %collective-permute-start.13) | collective-permute-done | bytes 8224 | tf_op jit(solution)/shard_map/ppermute | solution.py:199
  31.6 1.2 %grads.3 = (bf16[128,512]{1,0:T(8,128)(2,1)S(1)}, bf16[128,512]{1,0:T(8,128)(2,1)S(1)}, bf16[128,512]{1,0:T(8,128)(2,1)S(1)}) custom-call(s32[6]{0:T(128)S(1)} %stack.27.place_ref, f32[16,128]{1,0:T(8,128)S(1)} %add.36.stat_ref, f32[512,512]{1,0:T(8,128)S(1)} %get-tuple-element.48.refs_0_, bf16[512,512]{1,0:T(8,128)(2,1)S(1)} %get-tuple-element.49.refs_1_, ...), custom_call_target="tpu_custom_call" | custom-call | tf_op jit(solution)/shard_map/grads/pallas_call | solution.py:308
  32.8 0.6 %collective-permute-start.14 = (bf16[128,512]{1,0:T(8,128)(2,1)S(1)}, bf16[128,512]{1,0:T(8,128)(2,1)S(1)}, u32[]{:S(2)}, u32[]{:S(2)}) collective-permute-start(bf16[128,512]{1,0:T(8,128)(2,1)S(1)} %get-tuple-element.57), channel_id=1, source_target_pairs={{0,2},{1,3},{2,0},{3,1},{4,6},{5,7},{6,4},{7,5},{8,10},{9,11},{10,... | collective-permute-start | bytes 393224 | tf_op jit(solution)/shard_map/ppermute | solution.py:199
  33.4 1.2 %collective-permute-start.15 = (bf16[128,512]{1,0:T(8,128)(2,1)S(1)}, bf16[128,512]{1,0:T(8,128)(2,1)S(1)}, u32[]{:S(2)}, u32[]{:S(2)}) collective-permute-start(bf16[128,512]{1,0:T(8,128)(2,1)S(1)} %get-tuple-element.58), channel_id=1, source_target_pairs={{0,4},{1,5},{2,6},{3,7},{4,0},{5,1},{6,2},{7,3},{8,12},{9,13},{10,... | collective-permute-start | bytes 393224 | tf_op jit(solution)/shard_map/ppermute | solution.py:199
  34.6 1.8 %collective-permute-start.16 = (bf16[128,512]{1,0:T(8,128)(2,1)S(1)}, bf16[128,512]{1,0:T(8,128)(2,1)S(1)}, u32[]{:S(2)}, u32[]{:S(2)}) collective-permute-start(bf16[128,512]{1,0:T(8,128)(2,1)S(1)} %get-tuple-element.59), channel_id=1, source_target_pairs={{0,6},{1,7},{2,4},{3,5},{4,2},{5,3},{6,0},{7,1},{8,14},{9,15},{10,... | collective-permute-start | bytes 393224 | tf_op jit(solution)/shard_map/ppermute | solution.py:199
  36.4 1.3 %grads.2 = (f32[128,512]{1,0:T(8,128)S(1)}, f32[1,128]{1,0:T(1,128)}) custom-call(s32[6]{0:T(128)S(1)} %stack.27.place_ref, f32[16,128]{1,0:T(8,128)S(1)} %add.36.stat_ref, f32[512,512]{1,0:T(8,128)S(1)} %get-tuple-element.48.refs_0_, bf16[512,512]{1,0:T(8,128)(2,1)S(1)} %get-tuple-element.49.refs_1_, s32[4,128]{1,0:T(4,128)S(1)} %get-tuple-element.50.refs_2_, ...), custom_call_target="tpu_custom_call" | custom-call | tf_op jit(solution)/shard_map/grads/pallas_call | solution.py:308
  37.6 0.2 collective-permute-done.14.refs_0_
  37.9 0.8 %collective-permute-done.15.refs_1_ = bf16[128,512]{1,0:T(8,128)(2,1)S(1)} collective-permute-done((bf16[128,512]{1,0:T(8,128)(2,1)S(1)}, bf16[128,512]{1,0:T(8,128)(2,1)S(1)}, u32[]{:S(2)}, u32[]{:S(2)}) %collective-permute-start.15) | collective-permute-done | bytes 131104 | tf_op jit(solution)/shard_map/ppermute | solution.py:199
  38.6 1.9 %collective-permute-done.16.refs_2_ = bf16[128,512]{1,0:T(8,128)(2,1)S(1)} collective-permute-done((bf16[128,512]{1,0:T(8,128)(2,1)S(1)}, bf16[128,512]{1,0:T(8,128)(2,1)S(1)}, u32[]{:S(2)}, u32[]{:S(2)}) %collective-permute-start.16) | collective-permute-done | bytes 131104 | tf_op jit(solution)/shard_map/ppermute | solution.py:199
  40.5 0.9 %finish.1 = f32[128,512]{1,0:T(8,128)} custom-call(f32[128,512]{1,0:T(8,128)S(1)} %get-tuple-element.55.chosen_ref, f32[128,512]{1,0:T(8,128)S(1)} %get-tuple-element.56.own_ref, bf16[128,512]{1,0:T(8,128)(2,1)S(1)} %collective-permute-done.14.refs_0_, bf16[128,512]{1,0:T(8,128)(2,1)S(1)} %collective-permute-done.15.refs_1_, ...), custom_call_target="tpu_custom_call" | custom-call | tf_op jit(solution)/shard_map/finish/pallas_call | solution.py:323
  (4 shorter events, 0.0 us)
Async XLA Ops:
  0.6 15.0 %copy-start = (bf16[128,512]{1,0:T(8,128)(2,1)S(1)}, bf16[128,512]{1,0:T(8,128)(2,1)}, u32[]{:S(2)}) copy-start(bf16[128,512]{1,0:T(8,128)(2,1)} %refs_0_.1) | copy-start | bytes 393220
  0.6 13.4 %collective-permute-start = (bf16[128,512]{1,0:T(8,128)(2,1)}, bf16[128,512]{1,0:T(8,128)(2,1)S(1)}, u32[]{:S(2)}, u32[]{:S(2)}) collective-permute-start(bf16[128,512]{1,0:T(8,128)(2,1)} %refs_0_.1), channel_id=1, source_target_pairs={{0,16},{1,17},{2,18},{3,19},{4,20},{5,21},{6,22},{7,23},{8,24},{9,... | collective-permute-start | bytes 393224 | tf_op jit(solution)/shard_map/ppermute | solution.py:199
  4.7 9.3 %collective-permute-start.1 = (bf16[128,512]{1,0:T(8,128)(2,1)}, bf16[128,512]{1,0:T(8,128)(2,1)S(1)}, u32[]{:S(2)}, u32[]{:S(2)}) collective-permute-start(bf16[128,512]{1,0:T(8,128)(2,1)} %refs_0_.1), channel_id=1, source_target_pairs={{0,8},{1,9},{2,10},{3,11},{4,12},{5,13},{6,14},{7,15},{8,0},{9,1},... | collective-permute-start | bytes 393224 | tf_op jit(solution)/shard_map/ppermute | solution.py:199
  6.3 6.9 %collective-permute-start.3 = (s32[1,128]{1,0:T(1,128)}, s32[1,128]{1,0:T(1,128)S(1)}, u32[]{:S(2)}, u32[]{:S(2)}) collective-permute-start(s32[1,128]{1,0:T(1,128)} %bitcast.8), channel_id=1, source_target_pairs={{0,16},{1,17},{2,18},{3,19},{4,20},{5,21},{6,22},{7,23},{8,24},{9,... | collective-permute-start | bytes 1544 | tf_op jit(solution)/shard_map/ppermute | solution.py:199
  6.7 0.7 %copy-start.1 = (s32[256]{0:T(256)S(1)}, s32[256]{0:T(256)}, u32[]{:S(2)}) copy-start(s32[256]{0:T(256)} %sampled_hbm.1) | copy-start | bytes 3076
  7.4 5.8 %copy-start.2 = (s32[128]{0:T(128)S(1)}, s32[128]{0:T(128)}, u32[]{:S(2)}) copy-start(s32[128]{0:T(128)} %param.5) | copy-start | bytes 1540
  10.1 6.2 %collective-permute-start.8 = (bf16[136,512]{1,0:T(8,128)(2,1)S(1)}, bf16[136,512]{1,0:T(8,128)(2,1)S(1)}, u32[]{:S(2)}, u32[]{:S(2)}) collective-permute-start(bf16[136,512]{1,0:T(8,128)(2,1)S(1)} %get-tuple-element.41.refs_3_), channel_id=1, source_target_pairs={{0,2},{1,3},{2,0},{3,1},{4,6},{5,7},{6,4},{7,5},{8,10},{9,11},{10,... | collective-permute-start | bytes 417800 | tf_op jit(solution)/shard_map/ppermute | solution.py:199
  11.6 8.0 %collective-permute-start.7 = (bf16[136,512]{1,0:T(8,128)(2,1)S(1)}, bf16[136,512]{1,0:T(8,128)(2,1)S(1)}, u32[]{:S(2)}, u32[]{:S(2)}) collective-permute-start(bf16[136,512]{1,0:T(8,128)(2,1)S(1)} %get-tuple-element.41.refs_3_), channel_id=1, source_target_pairs={{0,4},{1,5},{2,6},{3,7},{4,0},{5,1},{6,2},{7,3},{8,12},{9,13},{10,... | collective-permute-start | bytes 417800 | tf_op jit(solution)/shard_map/ppermute | solution.py:199
  13.2 6.5 %collective-permute-start.6 = (bf16[136,512]{1,0:T(8,128)(2,1)S(1)}, bf16[136,512]{1,0:T(8,128)(2,1)S(1)}, u32[]{:S(2)}, u32[]{:S(2)}) collective-permute-start(bf16[136,512]{1,0:T(8,128)(2,1)S(1)} %get-tuple-element.41.refs_3_), channel_id=1, source_target_pairs={{0,6},{1,7},{2,4},{3,5},{4,2},{5,3},{6,0},{7,1},{8,14},{9,15},{10,... | collective-permute-start | bytes 417800 | tf_op jit(solution)/shard_map/ppermute | solution.py:199
  14.1 5.6 %collective-permute-start.5 = (bf16[136,512]{1,0:T(8,128)(2,1)S(1)}, bf16[136,512]{1,0:T(8,128)(2,1)S(1)}, u32[]{:S(2)}, u32[]{:S(2)}) collective-permute-start(bf16[136,512]{1,0:T(8,128)(2,1)S(1)} %pack.1.refs_1_), channel_id=1, source_target_pairs={{0,8},{1,9},{2,10},{3,11},{4,12},{5,13},{6,14},{7,15},{8,0},{9,1},... | collective-permute-start | bytes 417800 | tf_op jit(solution)/shard_map/ppermute | solution.py:199
  15.8 5.2 %collective-permute-start.2 = (bf16[256,512]{1,0:T(8,128)(2,1)S(1)}, bf16[256,512]{1,0:T(8,128)(2,1)S(1)}, u32[]{:S(2)}, u32[]{:S(2)}) collective-permute-start(bf16[256,512]{1,0:T(8,128)(2,1)S(1)} %normalize.1.refs_0_), channel_id=1, source_target_pairs={{0,1},{1,0},{2,3},{3,2},{4,5},{5,4},{6,7},{7,6},{8,9},{9,8},{10,11... | collective-permute-start | bytes 786440 | tf_op jit(solution)/shard_map/ppermute | solution.py:199
  16.2 4.7 %collective-permute-start.4 = (bf16[136,512]{1,0:T(8,128)(2,1)S(1)}, bf16[136,512]{1,0:T(8,128)(2,1)S(1)}, u32[]{:S(2)}, u32[]{:S(2)}) collective-permute-start(bf16[136,512]{1,0:T(8,128)(2,1)S(1)} %pack.1.refs_1_), channel_id=1, source_target_pairs={{0,1},{1,0},{2,3},{3,2},{4,5},{5,4},{6,7},{7,6},{8,9},{9,8},{10,11... | collective-permute-start | bytes 417800 | tf_op jit(solution)/shard_map/ppermute | solution.py:199
  19.7 1.4 %collective-permute-start.9 = (bf16[136,512]{1,0:T(8,128)(2,1)S(1)}, bf16[136,512]{1,0:T(8,128)(2,1)S(1)}, u32[]{:S(2)}, u32[]{:S(2)}) collective-permute-start(bf16[136,512]{1,0:T(8,128)(2,1)S(1)} %collective-permute-done.5.refs_2_), channel_id=1, source_target_pairs={{0,1},{1,0},{2,3},{3,2},{4,5},{5,4},{6,7},{7,6},{8,9},{9,8},{10,11... | collective-permute-start | bytes 417800 | tf_op jit(solution)/shard_map/ppermute | solution.py:199
  22.3 3.1 %collective-permute-start.12 = (f32[16,128]{1,0:T(8,128)S(1)}, f32[16,128]{1,0:T(8,128)S(1)}, u32[]{:S(2)}, u32[]{:S(2)}) collective-permute-start(f32[16,128]{1,0:T(8,128)S(1)} %get-tuple-element.47), channel_id=1, source_target_pairs={{0,9},{1,8},{2,11},{3,10},{4,13},{5,12},{6,15},{7,14},{8,1},{9,0},... | collective-permute-start | bytes 24584 | tf_op jit(solution)/shard_map/ppermute | solution.py:199
  23.4 3.7 %collective-permute-start.11 = (f32[16,128]{1,0:T(8,128)S(1)}, f32[16,128]{1,0:T(8,128)S(1)}, u32[]{:S(2)}, u32[]{:S(2)}) collective-permute-start(f32[16,128]{1,0:T(8,128)S(1)} %get-tuple-element.47), channel_id=1, source_target_pairs={{0,8},{1,9},{2,10},{3,11},{4,12},{5,13},{6,14},{7,15},{8,0},{9,1},... | collective-permute-start | bytes 24584 | tf_op jit(solution)/shard_map/ppermute | solution.py:199
  24.4 2.6 %collective-permute-start.10 = (f32[16,128]{1,0:T(8,128)S(1)}, f32[16,128]{1,0:T(8,128)S(1)}, u32[]{:S(2)}, u32[]{:S(2)}) collective-permute-start(f32[16,128]{1,0:T(8,128)S(1)} %get-tuple-element.47), channel_id=1, source_target_pairs={{0,1},{1,0},{2,3},{3,2},{4,5},{5,4},{6,7},{7,6},{8,9},{9,8},{10,11... | collective-permute-start | bytes 24584 | tf_op jit(solution)/shard_map/ppermute | solution.py:199
  27.0 4.6 %collective-permute-start.13 = (f32[16,128]{1,0:T(8,128)S(1)}, f32[16,128]{1,0:T(8,128)S(1)}, u32[]{:S(2)}, u32[]{:S(2)}) collective-permute-start(f32[16,128]{1,0:T(8,128)S(1)} %add_add_fusion), channel_id=1, source_target_pairs={{0,16},{1,17},{2,18},{3,19},{4,20},{5,21},{6,22},{7,23},{8,24},{9,... | collective-permute-start | bytes 24584 | tf_op jit(solution)/shard_map/ppermute | solution.py:199
  32.8 5.0 %collective-permute-start.14 = (bf16[128,512]{1,0:T(8,128)(2,1)S(1)}, bf16[128,512]{1,0:T(8,128)(2,1)S(1)}, u32[]{:S(2)}, u32[]{:S(2)}) collective-permute-start(bf16[128,512]{1,0:T(8,128)(2,1)S(1)} %get-tuple-element.57), channel_id=1, source_target_pairs={{0,2},{1,3},{2,0},{3,1},{4,6},{5,7},{6,4},{7,5},{8,10},{9,11},{10,... | collective-permute-start | bytes 393224 | tf_op jit(solution)/shard_map/ppermute | solution.py:199
  33.4 5.2 %collective-permute-start.15 = (bf16[128,512]{1,0:T(8,128)(2,1)S(1)}, bf16[128,512]{1,0:T(8,128)(2,1)S(1)}, u32[]{:S(2)}, u32[]{:S(2)}) collective-permute-start(bf16[128,512]{1,0:T(8,128)(2,1)S(1)} %get-tuple-element.58), channel_id=1, source_target_pairs={{0,4},{1,5},{2,6},{3,7},{4,0},{5,1},{6,2},{7,3},{8,12},{9,13},{10,... | collective-permute-start | bytes 393224 | tf_op jit(solution)/shard_map/ppermute | solution.py:199
  34.6 5.9 %collective-permute-start.16 = (bf16[128,512]{1,0:T(8,128)(2,1)S(1)}, bf16[128,512]{1,0:T(8,128)(2,1)S(1)}, u32[]{:S(2)}, u32[]{:S(2)}) collective-permute-start(bf16[128,512]{1,0:T(8,128)(2,1)S(1)} %get-tuple-element.59), channel_id=1, source_target_pairs={{0,6},{1,7},{2,4},{3,5},{4,2},{5,3},{6,0},{7,1},{8,14},{9,15},{10,... | collective-permute-start | bytes 393224 | tf_op jit(solution)/shard_map/ppermute | solution.py:199

commit v3 on v2

--- a/solution.py
+++ b/solution.py
@@ -75,15 +75,17 @@
     copy.start()
     copy.wait()
 
-    def start_row(row, carry):
-        pltpu.make_async_copy(
-            weight_hbm.at[pl.ds(sampled_ref[first + row], 1), :],
-            chosen_ref.at[pl.ds(row, 1), :],
-            sems.at[1],
-        ).start()
+    def start_rows(step, carry):
+        for lane in range(8):
+            row = step * 8 + lane
+            pltpu.make_async_copy(
+                weight_hbm.at[pl.ds(sampled_ref[first + row], 1), :],
+                chosen_ref.at[pl.ds(row, 1), :],
+                sems.at[1],
+            ).start(priority=lane % 2)
         return carry
 
-    lax.fori_loop(0, part, start_row, 0, unroll=32)
+    lax.fori_loop(0, part // 8, start_rows, 0, unroll=4)
     pltpu.make_async_copy(weight_hbm.at[pl.ds(0, part), :], chosen_ref, sems.at[1]).wait()
     rows = chosen_ref[...]
     inverse = lax.rsqrt(jnp.sum(rows * rows, axis=1, keepdims=True) + epsilon)

time: 41.6 us -> 41.6 us (level)
  no operation moved by 1% of the time
where the time goes in v3:
time: 41.6 us; the launch traced here: 41.4 us
  starting transfers between devices  20 us (48%)
  waiting for transfers between devices  11.2 us (27%)
  Pallas kernels  8.71 us (21%)
  local copies, waits for them, and re-layouts  0.77 us (2%)
  between operations  0.73 us (2%)
    ppermute x17, starting transfers between devices, swap(): lax.ppermute(value, ('cls', 'dp'), [(i, i ^ mask) for i in range(groups *...  20 us
    ppermute x17, waiting for transfers between devices, swap(): lax.ppermute(value, ('cls', 'dp'), [(i, i ^ mask) for i in range(groups *...  11.2 us
    pallas_call x1, Pallas kernels, per_device(): pl.pallas_call(choose_kernel, out_shape=[jax.ShapeDtypeStruct((part + ext...  2.68 us
    pallas_call x2, Pallas kernels, per_device(): pl.pallas_call(functools.partial(logits_kernel, count, span, len(arrays[j...  2.44 us
    pallas_call x2, Pallas kernels, grads(): pl.pallas_call(functools.partial(grads_kernel, count, replicas, spans, si...  2.44 us
    pallas_call x1, Pallas kernels, per_device(): pl.pallas_call(finish_kernel, out_shape=jax.ShapeDtypeStruct((part, width...  0.91 us
  transfers between devices with their start and end apart: 17, of which 9 were waited for; matrix products, arithmetic and copies ran while one was open for 0% of the time, Pallas kernels for 13%

profile of v3, /device:TPU:0, one launch (start us, length us, event | category | flops | bytes accessed | tf_op | source)
XLA Modules:
  0.0 41.4 jit_solution(2806049830788060583)
XLA Ops:
  0.6 0.0 copy-start
  0.6 4.1 %collective-permute-start = (bf16[128,512]{1,0:T(8,128)(2,1)}, bf16[128,512]{1,0:T(8,128)(2,1)S(1)}, u32[]{:S(2)}, u32[]{:S(2)}) collective-permute-start(bf16[128,512]{1,0:T(8,128)(2,1)} %refs_0_.1), channel_id=1, source_target_pairs={{0,16},{1,17},{2,18},{3,19},{4,20},{5,21},{6,22},{7,23},{8,24},{9,... | collective-permute-start | bytes 393224 | tf_op jit(solution)/shard_map/ppermute | solution.py:201
  4.7 1.6 %collective-permute-start.1 = (bf16[128,512]{1,0:T(8,128)(2,1)}, bf16[128,512]{1,0:T(8,128)(2,1)S(1)}, u32[]{:S(2)}, u32[]{:S(2)}) collective-permute-start(bf16[128,512]{1,0:T(8,128)(2,1)} %refs_0_.1), channel_id=1, source_target_pairs={{0,8},{1,9},{2,10},{3,11},{4,12},{5,13},{6,14},{7,15},{8,0},{9,1},... | collective-permute-start | bytes 393224 | tf_op jit(solution)/shard_map/ppermute | solution.py:201
  6.3 0.3 collective-permute-start.3
  6.7 0.1 stack.27.place_ref
  6.7 0.0 copy-start.1
  6.7 0.7 %copy-done.1 = s32[256]{0:T(256)S(1)} copy-done((s32[256]{0:T(256)S(1)}, s32[256]{0:T(256)}, u32[]{:S(2)}) %copy-start.1) | copy-done | bytes 1048
  7.4 2.7 %choose.1 = (bf16[136,512]{1,0:T(8,128)(2,1)S(1)}, f32[128,512]{1,0:T(8,128)S(1)}) custom-call(s32[6]{0:T(128)S(1)} %stack.27.place_ref, s32[256]{0:T(256)S(1)} %copy-done.1, f32[1024,512]{1,0:T(8,128)} %weight_hbm.1), custom_call_target="tpu_custom_call" | custom-call | tf_op jit(solution)/shard_map/choose/pallas_call | solution.py:213
  10.1 1.6 %collective-permute-start.8 = (bf16[136,512]{1,0:T(8,128)(2,1)S(1)}, bf16[136,512]{1,0:T(8,128)(2,1)S(1)}, u32[]{:S(2)}, u32[]{:S(2)}) collective-permute-start(bf16[136,512]{1,0:T(8,128)(2,1)S(1)} %get-tuple-element.41.refs_3_), channel_id=1, source_target_pairs={{0,2},{1,3},{2,0},{3,1},{4,6},{5,7},{6,4},{7,5},{8,10},{9,11},{10,... | collective-permute-start | bytes 417800 | tf_op jit(solution)/shard_map/ppermute | solution.py:201
  11.7 1.5 %collective-permute-start.7 = (bf16[136,512]{1,0:T(8,128)(2,1)S(1)}, bf16[136,512]{1,0:T(8,128)(2,1)S(1)}, u32[]{:S(2)}, u32[]{:S(2)}) collective-permute-start(bf16[136,512]{1,0:T(8,128)(2,1)S(1)} %get-tuple-element.41.refs_3_), channel_id=1, source_target_pairs={{0,4},{1,5},{2,6},{3,7},{4,0},{5,1},{6,2},{7,3},{8,12},{9,13},{10,... | collective-permute-start | bytes 417800 | tf_op jit(solution)/shard_map/ppermute | solution.py:201
  13.2 0.0 collective-permute-done.3
  13.2 0.0 copy-done.2
  13.2 0.8 %collective-permute-start.6 = (bf16[136,512]{1,0:T(8,128)(2,1)S(1)}, bf16[136,512]{1,0:T(8,128)(2,1)S(1)}, u32[]{:S(2)}, u32[]{:S(2)}) collective-permute-start(bf16[136,512]{1,0:T(8,128)(2,1)S(1)} %get-tuple-element.41.refs_3_), channel_id=1, source_target_pairs={{0,6},{1,7},{2,4},{3,5},{4,2},{5,3},{6,0},{7,1},{8,14},{9,15},{10,... | collective-permute-start | bytes 417800 | tf_op jit(solution)/shard_map/ppermute | solution.py:201
  14.0 0.0 collective-permute-done.feat_ref
  14.0 0.0 collective-permute-done.1.refs_1_
  14.0 0.1 pack.1.refs_1_
  14.1 1.5 %collective-permute-start.5 = (bf16[136,512]{1,0:T(8,128)(2,1)S(1)}, bf16[136,512]{1,0:T(8,128)(2,1)S(1)}, u32[]{:S(2)}, u32[]{:S(2)}) collective-permute-start(bf16[136,512]{1,0:T(8,128)(2,1)S(1)} %pack.1.refs_1_), channel_id=1, source_target_pairs={{0,8},{1,9},{2,10},{3,11},{4,12},{5,13},{6,14},{7,15},{8,0},{9,1},... | collective-permute-start | bytes 417800 | tf_op jit(solution)/shard_map/ppermute | solution.py:201
  15.6 0.0 copy-done
  15.6 0.1 normalize.1.refs_0_
  15.8 0.1 collective-permute-start.2
  15.8 0.4 %collective-permute-done.8.refs_4_ = bf16[136,512]{1,0:T(8,128)(2,1)S(1)} collective-permute-done((bf16[136,512]{1,0:T(8,128)(2,1)S(1)}, bf16[136,512]{1,0:T(8,128)(2,1)S(1)}, u32[]{:S(2)}, u32[]{:S(2)}) %collective-permute-start.8) | collective-permute-done | bytes 139296 | tf_op jit(solution)/shard_map/ppermute | solution.py:201
  16.3 0.1 collective-permute-start.4
  16.3 3.4 %collective-permute-done.7.refs_5_ = bf16[136,512]{1,0:T(8,128)(2,1)S(1)} collective-permute-done((bf16[136,512]{1,0:T(8,128)(2,1)S(1)}, bf16[136,512]{1,0:T(8,128)(2,1)S(1)}, u32[]{:S(2)}, u32[]{:S(2)}) %collective-permute-start.7) | collective-permute-done | bytes 139296 | tf_op jit(solution)/shard_map/ppermute | solution.py:201
  19.7 0.0 collective-permute-done.6.refs_6_
  19.7 0.0 collective-permute-done.5.refs_2_
  19.7 0.0 collective-permute-start.9
  19.7 1.2 %logits.2 = (f32[512,512]{1,0:T(8,128)S(1)}, f32[16,128]{1,0:T(8,128)S(1)}, bf16[512,512]{1,0:T(8,128)(2,1)S(1)}, s32[4,128]{1,0:T(4,128)S(1)}, bf16[512,512]{1,0:T(8,128)(2,1)S(1)}) custom-call(s32[6]{0:T(128)S(1)} %stack.27.place_ref, bf16[256,512]{1,0:T(8,128)(2,1)S(1)} %normalize.1.refs_0_, bf16[136,512]{1,0:T(8,128)(2,1)S(1)} %pack.1.refs_1_, ...), custom_call_target="tpu_custom_call" | custom-call | tf_op jit(solution)/shard_map/logits/pallas_call | solution.py:289
  21.0 0.0 collective-permute-done.4.refs_1_
  21.0 0.0 collective-permute-done.2.refs_0_
  21.0 0.1 collective-permute-done.9.refs_2_
  21.1 1.2 %logits.3 = (f32[512,512]{1,0:T(8,128)S(1)}, f32[16,128]{1,0:T(8,128)S(1)}, bf16[512,512]{1,0:T(8,128)(2,1)S(1)}, s32[4,128]{1,0:T(4,128)S(1)}) custom-call(s32[6]{0:T(128)S(1)} %stack.27.place_ref, bf16[256,512]{1,0:T(8,128)(2,1)S(1)} %collective-permute-done.2.refs_0_, bf16[136,512]{1,0:T(8,128)(2,1)S(1)} %collective-permute-done.4.refs_1_, ...), custom_call_target="tpu_custom_call" | custom-call | tf_op jit(solution)/shard_map/logits/pallas_call | solution.py:289
  22.3 1.1 %collective-permute-start.12 = (f32[16,128]{1,0:T(8,128)S(1)}, f32[16,128]{1,0:T(8,128)S(1)}, u32[]{:S(2)}, u32[]{:S(2)}) collective-permute-start(f32[16,128]{1,0:T(8,128)S(1)} %get-tuple-element.47), channel_id=1, source_target_pairs={{0,9},{1,8},{2,11},{3,10},{4,13},{5,12},{6,15},{7,14},{8,1},{9,0},... | collective-permute-start | bytes 24584 | tf_op jit(solution)/shard_map/ppermute | solution.py:201
  23.4 1.1 %collective-permute-start.11 = (f32[16,128]{1,0:T(8,128)S(1)}, f32[16,128]{1,0:T(8,128)S(1)}, u32[]{:S(2)}, u32[]{:S(2)}) collective-permute-start(f32[16,128]{1,0:T(8,128)S(1)} %get-tuple-element.47), channel_id=1, source_target_pairs={{0,8},{1,9},{2,10},{3,11},{4,12},{5,13},{6,14},{7,15},{8,0},{9,1},... | collective-permute-start | bytes 24584 | tf_op jit(solution)/shard_map/ppermute | solution.py:201
  24.4 0.0 collective-permute-start.10
  24.4 1.0 %collective-permute-done.12 = f32[16,128]{1,0:T(8,128)S(1)} collective-permute-done((f32[16,128]{1,0:T(8,128)S(1)}, f32[16,128]{1,0:T(8,128)S(1)}, u32[]{:S(2)}, u32[]{:S(2)}) %collective-permute-start.12) | collective-permute-done | bytes 8224 | tf_op jit(solution)/shard_map/ppermute | solution.py:201
  25.4 1.6 %collective-permute-done.11 = f32[16,128]{1,0:T(8,128)S(1)} collective-permute-done((f32[16,128]{1,0:T(8,128)S(1)}, f32[16,128]{1,0:T(8,128)S(1)}, u32[]{:S(2)}, u32[]{:S(2)}) %collective-permute-start.11) | collective-permute-done | bytes 8224 | tf_op jit(solution)/shard_map/ppermute | solution.py:201
  27.0 0.0 collective-permute-done.10
  27.0 2.8 %collective-permute-start.13 = (f32[16,128]{1,0:T(8,128)S(1)}, f32[16,128]{1,0:T(8,128)S(1)}, u32[]{:S(2)}, u32[]{:S(2)}) collective-permute-start(f32[16,128]{1,0:T(8,128)S(1)} %add_add_fusion), channel_id=1, source_target_pairs={{0,16},{1,17},{2,18},{3,19},{4,20},{5,21},{6,22},{7,23},{8,24},{9,... | collective-permute-start | bytes 24584 | tf_op jit(solution)/shard_map/ppermute | solution.py:201
  29.8 1.8 %collective-permute-done.13 = f32[16,128]{1,0:T(8,128)S(1)} collective-permute-done((f32[16,128]{1,0:T(8,128)S(1)}, f32[16,128]{1,0:T(8,128)S(1)}, u32[]{:S(2)}, u32[]{:S(2)}) %collective-permute-start.13) | collective-permute-done | bytes 8224 | tf_op jit(solution)/shard_map/ppermute | solution.py:201
  31.6 1.2 %grads.3 = (bf16[128,512]{1,0:T(8,128)(2,1)S(1)}, bf16[128,512]{1,0:T(8,128)(2,1)S(1)}, bf16[128,512]{1,0:T(8,128)(2,1)S(1)}) custom-call(s32[6]{0:T(128)S(1)} %stack.27.place_ref, f32[16,128]{1,0:T(8,128)S(1)} %add.36.stat_ref, f32[512,512]{1,0:T(8,128)S(1)} %get-tuple-element.48.refs_0_, bf16[512,512]{1,0:T(8,128)(2,1)S(1)} %get-tuple-element.49.refs_1_, ...), custom_call_target="tpu_custom_call" | custom-call | tf_op jit(solution)/shard_map/grads/pallas_call | solution.py:310
  32.8 0.6 %collective-permute-start.14 = (bf16[128,512]{1,0:T(8,128)(2,1)S(1)}, bf16[128,512]{1,0:T(8,128)(2,1)S(1)}, u32[]{:S(2)}, u32[]{:S(2)}) collective-permute-start(bf16[128,512]{1,0:T(8,128)(2,1)S(1)} %get-tuple-element.57), channel_id=1, source_target_pairs={{0,2},{1,3},{2,0},{3,1},{4,6},{5,7},{6,4},{7,5},{8,10},{9,11},{10,... | collective-permute-start | bytes 393224 | tf_op jit(solution)/shard_map/ppermute | solution.py:201
  33.4 1.3 %collective-permute-start.15 = (bf16[128,512]{1,0:T(8,128)(2,1)S(1)}, bf16[128,512]{1,0:T(8,128)(2,1)S(1)}, u32[]{:S(2)}, u32[]{:S(2)}) collective-permute-start(bf16[128,512]{1,0:T(8,128)(2,1)S(1)} %get-tuple-element.58), channel_id=1, source_target_pairs={{0,4},{1,5},{2,6},{3,7},{4,0},{5,1},{6,2},{7,3},{8,12},{9,13},{10,... | collective-permute-start | bytes 393224 | tf_op jit(solution)/shard_map/ppermute | solution.py:201
  34.7 1.7 %collective-permute-start.16 = (bf16[128,512]{1,0:T(8,128)(2,1)S(1)}, bf16[128,512]{1,0:T(8,128)(2,1)S(1)}, u32[]{:S(2)}, u32[]{:S(2)}) collective-permute-start(bf16[128,512]{1,0:T(8,128)(2,1)S(1)} %get-tuple-element.59), channel_id=1, source_target_pairs={{0,6},{1,7},{2,4},{3,5},{4,2},{5,3},{6,0},{7,1},{8,14},{9,15},{10,... | collective-permute-start | bytes 393224 | tf_op jit(solution)/shard_map/ppermute | solution.py:201
  36.4 1.3 %grads.2 = (f32[128,512]{1,0:T(8,128)S(1)}, f32[1,128]{1,0:T(1,128)}) custom-call(s32[6]{0:T(128)S(1)} %stack.27.place_ref, f32[16,128]{1,0:T(8,128)S(1)} %add.36.stat_ref, f32[512,512]{1,0:T(8,128)S(1)} %get-tuple-element.48.refs_0_, bf16[512,512]{1,0:T(8,128)(2,1)S(1)} %get-tuple-element.49.refs_1_, s32[4,128]{1,0:T(4,128)S(1)} %get-tuple-element.50.refs_2_, ...), custom_call_target="tpu_custom_call" | custom-call | tf_op jit(solution)/shard_map/grads/pallas_call | solution.py:310
  37.6 0.2 collective-permute-done.14.refs_0_
  37.9 0.8 %collective-permute-done.15.refs_1_ = bf16[128,512]{1,0:T(8,128)(2,1)S(1)} collective-permute-done((bf16[128,512]{1,0:T(8,128)(2,1)S(1)}, bf16[128,512]{1,0:T(8,128)(2,1)S(1)}, u32[]{:S(2)}, u32[]{:S(2)}) %collective-permute-start.15) | collective-permute-done | bytes 131104 | tf_op jit(solution)/shard_map/ppermute | solution.py:201
  38.7 1.9 %collective-permute-done.16.refs_2_ = bf16[128,512]{1,0:T(8,128)(2,1)S(1)} collective-permute-done((bf16[128,512]{1,0:T(8,128)(2,1)S(1)}, bf16[128,512]{1,0:T(8,128)(2,1)S(1)}, u32[]{:S(2)}, u32[]{:S(2)}) %collective-permute-start.16) | collective-permute-done | bytes 131104 | tf_op jit(solution)/shard_map/ppermute | solution.py:201
  40.5 0.9 %finish.1 = f32[128,512]{1,0:T(8,128)} custom-call(f32[128,512]{1,0:T(8,128)S(1)} %get-tuple-element.55.chosen_ref, f32[128,512]{1,0:T(8,128)S(1)} %get-tuple-element.56.own_ref, bf16[128,512]{1,0:T(8,128)(2,1)S(1)} %collective-permute-done.14.refs_0_, bf16[128,512]{1,0:T(8,128)(2,1)S(1)} %collective-permute-done.15.refs_1_, ...), custom_call_target="tpu_custom_call" | custom-call | tf_op jit(solution)/shard_map/finish/pallas_call | solution.py:325
  (4 shorter events, 0.0 us)
Async XLA Ops:
  0.6 15.0 %copy-start = (bf16[128,512]{1,0:T(8,128)(2,1)S(1)}, bf16[128,512]{1,0:T(8,128)(2,1)}, u32[]{:S(2)}) copy-start(bf16[128,512]{1,0:T(8,128)(2,1)} %refs_0_.1) | copy-start | bytes 393220
  0.6 13.4 %collective-permute-start = (bf16[128,512]{1,0:T(8,128)(2,1)}, bf16[128,512]{1,0:T(8,128)(2,1)S(1)}, u32[]{:S(2)}, u32[]{:S(2)}) collective-permute-start(bf16[128,512]{1,0:T(8,128)(2,1)} %refs_0_.1), channel_id=1, source_target_pairs={{0,16},{1,17},{2,18},{3,19},{4,20},{5,21},{6,22},{7,23},{8,24},{9,... | collective-permute-start | bytes 393224 | tf_op jit(solution)/shard_map/ppermute | solution.py:201
  4.7 9.3 %collective-permute-start.1 = (bf16[128,512]{1,0:T(8,128)(2,1)}, bf16[128,512]{1,0:T(8,128)(2,1)S(1)}, u32[]{:S(2)}, u32[]{:S(2)}) collective-permute-start(bf16[128,512]{1,0:T(8,128)(2,1)} %refs_0_.1), channel_id=1, source_target_pairs={{0,8},{1,9},{2,10},{3,11},{4,12},{5,13},{6,14},{7,15},{8,0},{9,1},... | collective-permute-start | bytes 393224 | tf_op jit(solution)/shard_map/ppermute | solution.py:201
  6.3 6.9 %collective-permute-start.3 = (s32[1,128]{1,0:T(1,128)}, s32[1,128]{1,0:T(1,128)S(1)}, u32[]{:S(2)}, u32[]{:S(2)}) collective-permute-start(s32[1,128]{1,0:T(1,128)} %bitcast.8), channel_id=1, source_target_pairs={{0,16},{1,17},{2,18},{3,19},{4,20},{5,21},{6,22},{7,23},{8,24},{9,... | collective-permute-start | bytes 1544 | tf_op jit(solution)/shard_map/ppermute | solution.py:201
  6.7 0.7 %copy-start.1 = (s32[256]{0:T(256)S(1)}, s32[256]{0:T(256)}, u32[]{:S(2)}) copy-start(s32[256]{0:T(256)} %sampled_hbm.1) | copy-start | bytes 3076
  7.4 5.8 %copy-start.2 = (s32[128]{0:T(128)S(1)}, s32[128]{0:T(128)}, u32[]{:S(2)}) copy-start(s32[128]{0:T(128)} %param.5) | copy-start | bytes 1540
  10.1 6.2 %collective-permute-start.8 = (bf16[136,512]{1,0:T(8,128)(2,1)S(1)}, bf16[136,512]{1,0:T(8,128)(2,1)S(1)}, u32[]{:S(2)}, u32[]{:S(2)}) collective-permute-start(bf16[136,512]{1,0:T(8,128)(2,1)S(1)} %get-tuple-element.41.refs_3_), channel_id=1, source_target_pairs={{0,2},{1,3},{2,0},{3,1},{4,6},{5,7},{6,4},{7,5},{8,10},{9,11},{10,... | collective-permute-start | bytes 417800 | tf_op jit(solution)/shard_map/ppermute | solution.py:201
  11.7 8.0 %collective-permute-start.7 = (bf16[136,512]{1,0:T(8,128)(2,1)S(1)}, bf16[136,512]{1,0:T(8,128)(2,1)S(1)}, u32[]{:S(2)}, u32[]{:S(2)}) collective-permute-start(bf16[136,512]{1,0:T(8,128)(2,1)S(1)} %get-tuple-element.41.refs_3_), channel_id=1, source_target_pairs={{0,4},{1,5},{2,6},{3,7},{4,0},{5,1},{6,2},{7,3},{8,12},{9,13},{10,... | collective-permute-start | bytes 417800 | tf_op jit(solution)/shard_map/ppermute | solution.py:201
  13.2 6.5 %collective-permute-start.6 = (bf16[136,512]{1,0:T(8,128)(2,1)S(1)}, bf16[136,512]{1,0:T(8,128)(2,1)S(1)}, u32[]{:S(2)}, u32[]{:S(2)}) collective-permute-start(bf16[136,512]{1,0:T(8,128)(2,1)S(1)} %get-tuple-element.41.refs_3_), channel_id=1, source_target_pairs={{0,6},{1,7},{2,4},{3,5},{4,2},{5,3},{6,0},{7,1},{8,14},{9,15},{10,... | collective-permute-start | bytes 417800 | tf_op jit(solution)/shard_map/ppermute | solution.py:201
  14.1 5.6 %collective-permute-start.5 = (bf16[136,512]{1,0:T(8,128)(2,1)S(1)}, bf16[136,512]{1,0:T(8,128)(2,1)S(1)}, u32[]{:S(2)}, u32[]{:S(2)}) collective-permute-start(bf16[136,512]{1,0:T(8,128)(2,1)S(1)} %pack.1.refs_1_), channel_id=1, source_target_pairs={{0,8},{1,9},{2,10},{3,11},{4,12},{5,13},{6,14},{7,15},{8,0},{9,1},... | collective-permute-start | bytes 417800 | tf_op jit(solution)/shard_map/ppermute | solution.py:201
  15.8 5.2 %collective-permute-start.2 = (bf16[256,512]{1,0:T(8,128)(2,1)S(1)}, bf16[256,512]{1,0:T(8,128)(2,1)S(1)}, u32[]{:S(2)}, u32[]{:S(2)}) collective-permute-start(bf16[256,512]{1,0:T(8,128)(2,1)S(1)} %normalize.1.refs_0_), channel_id=1, source_target_pairs={{0,1},{1,0},{2,3},{3,2},{4,5},{5,4},{6,7},{7,6},{8,9},{9,8},{10,11... | collective-permute-start | bytes 786440 | tf_op jit(solution)/shard_map/ppermute | solution.py:201
  16.3 4.7 %collective-permute-start.4 = (bf16[136,512]{1,0:T(8,128)(2,1)S(1)}, bf16[136,512]{1,0:T(8,128)(2,1)S(1)}, u32[]{:S(2)}, u32[]{:S(2)}) collective-permute-start(bf16[136,512]{1,0:T(8,128)(2,1)S(1)} %pack.1.refs_1_), channel_id=1, source_target_pairs={{0,1},{1,0},{2,3},{3,2},{4,5},{5,4},{6,7},{7,6},{8,9},{9,8},{10,11... | collective-permute-start | bytes 417800 | tf_op jit(solution)/shard_map/ppermute | solution.py:201
  19.7 1.4 %collective-permute-start.9 = (bf16[136,512]{1,0:T(8,128)(2,1)S(1)}, bf16[136,512]{1,0:T(8,128)(2,1)S(1)}, u32[]{:S(2)}, u32[]{:S(2)}) collective-permute-start(bf16[136,512]{1,0:T(8,128)(2,1)S(1)} %collective-permute-done.5.refs_2_), channel_id=1, source_target_pairs={{0,1},{1,0},{2,3},{3,2},{4,5},{5,4},{6,7},{7,6},{8,9},{9,8},{10,11... | collective-permute-start | bytes 417800 | tf_op jit(solution)/shard_map/ppermute | solution.py:201
  22.3 3.1 %collective-permute-start.12 = (f32[16,128]{1,0:T(8,128)S(1)}, f32[16,128]{1,0:T(8,128)S(1)}, u32[]{:S(2)}, u32[]{:S(2)}) collective-permute-start(f32[16,128]{1,0:T(8,128)S(1)} %get-tuple-element.47), channel_id=1, source_target_pairs={{0,9},{1,8},{2,11},{3,10},{4,13},{5,12},{6,15},{7,14},{8,1},{9,0},... | collective-permute-start | bytes 24584 | tf_op jit(solution)/shard_map/ppermute | solution.py:201
  23.4 3.7 %collective-permute-start.11 = (f32[16,128]{1,0:T(8,128)S(1)}, f32[16,128]{1,0:T(8,128)S(1)}, u32[]{:S(2)}, u32[]{:S(2)}) collective-permute-start(f32[16,128]{1,0:T(8,128)S(1)} %get-tuple-element.47), channel_id=1, source_target_pairs={{0,8},{1,9},{2,10},{3,11},{4,12},{5,13},{6,14},{7,15},{8,0},{9,1},... | collective-permute-start | bytes 24584 | tf_op jit(solution)/shard_map/ppermute | solution.py:201
  24.4 2.6 %collective-permute-start.10 = (f32[16,128]{1,0:T(8,128)S(1)}, f32[16,128]{1,0:T(8,128)S(1)}, u32[]{:S(2)}, u32[]{:S(2)}) collective-permute-start(f32[16,128]{1,0:T(8,128)S(1)} %get-tuple-element.47), channel_id=1, source_target_pairs={{0,1},{1,0},{2,3},{3,2},{4,5},{5,4},{6,7},{7,6},{8,9},{9,8},{10,11... | collective-permute-start | bytes 24584 | tf_op jit(solution)/shard_map/ppermute | solution.py:201
  27.0 4.6 %collective-permute-start.13 = (f32[16,128]{1,0:T(8,128)S(1)}, f32[16,128]{1,0:T(8,128)S(1)}, u32[]{:S(2)}, u32[]{:S(2)}) collective-permute-start(f32[16,128]{1,0:T(8,128)S(1)} %add_add_fusion), channel_id=1, source_target_pairs={{0,16},{1,17},{2,18},{3,19},{4,20},{5,21},{6,22},{7,23},{8,24},{9,... | collective-permute-start | bytes 24584 | tf_op jit(solution)/shard_map/ppermute | solution.py:201
  32.8 5.0 %collective-permute-start.14 = (bf16[128,512]{1,0:T(8,128)(2,1)S(1)}, bf16[128,512]{1,0:T(8,128)(2,1)S(1)}, u32[]{:S(2)}, u32[]{:S(2)}) collective-permute-start(bf16[128,512]{1,0:T(8,128)(2,1)S(1)} %get-tuple-element.57), channel_id=1, source_target_pairs={{0,2},{1,3},{2,0},{3,1},{4,6},{5,7},{6,4},{7,5},{8,10},{9,11},{10,... | collective-permute-start | bytes 393224 | tf_op jit(solution)/shard_map/ppermute | solution.py:201
  33.4 5.3 %collective-permute-start.15 = (bf16[128,512]{1,0:T(8,128)(2,1)S(1)}, bf16[128,512]{1,0:T(8,128)(2,1)S(1)}, u32[]{:S(2)}, u32[]{:S(2)}) collective-permute-start(bf16[128,512]{1,0:T(8,128)(2,1)S(1)} %get-tuple-element.58), channel_id=1, source_target_pairs={{0,4},{1,5},{2,6},{3,7},{4,0},{5,1},{6,2},{7,3},{8,12},{9,13},{10,... | collective-permute-start | bytes 393224 | tf_op jit(solution)/shard_map/ppermute | solution.py:201
  34.7 5.9 %collective-permute-start.16 = (bf16[128,512]{1,0:T(8,128)(2,1)S(1)}, bf16[128,512]{1,0:T(8,128)(2,1)S(1)}, u32[]{:S(2)}, u32[]{:S(2)}) collective-permute-start(bf16[128,512]{1,0:T(8,128)(2,1)S(1)} %get-tuple-element.59), channel_id=1, source_target_pairs={{0,6},{1,7},{2,4},{3,5},{4,2},{5,3},{6,0},{7,1},{8,14},{9,15},{10,... | collective-permute-start | bytes 393224 | tf_op jit(solution)/shard_map/ppermute | solution.py:201

commit v4 on v2

--- a/solution.py
+++ b/solution.py
@@ -68,23 +68,19 @@
     return digits[:, start : start + rows] * digit + digits[:, start + rows : start + 2 * rows]
 
 
-def choose_kernel(place_ref, sampled_hbm, weight_hbm, low_ref, chosen_ref, sampled_ref, sems):
+def choose_kernel(sampled_ref, weight_hbm, low_ref, chosen_ref, sem):
     part = chosen_ref.shape[0]
-    first = place_ref[square] * part
-    copy = pltpu.make_async_copy(sampled_hbm, sampled_ref, sems.at[0])
-    copy.start()
-    copy.wait()
 
     def start_row(row, carry):
         pltpu.make_async_copy(
-            weight_hbm.at[pl.ds(sampled_ref[first + row], 1), :],
+            weight_hbm.at[pl.ds(sampled_ref[row], 1), :],
             chosen_ref.at[pl.ds(row, 1), :],
-            sems.at[1],
+            sem,
         ).start()
         return carry
 
     lax.fori_loop(0, part, start_row, 0, unroll=32)
-    pltpu.make_async_copy(weight_hbm.at[pl.ds(0, part), :], chosen_ref, sems.at[1]).wait()
+    pltpu.make_async_copy(weight_hbm.at[pl.ds(0, part), :], chosen_ref, sem).wait()
     rows = chosen_ref[...]
     inverse = lax.rsqrt(jnp.sum(rows * rows, axis=1, keepdims=True) + epsilon)
     low_ref[:part, :] = (rows * inverse).astype(jnp.bfloat16) * logit_scale
@@ -214,12 +210,12 @@
             jax.ShapeDtypeStruct((part + extra, width), jnp.bfloat16),
             jax.ShapeDtypeStruct((part, width), jnp.float32),
         ],
-        in_specs=[smem_spec, hbm_spec, hbm_spec],
+        in_specs=[smem_spec, hbm_spec],
         out_specs=[vmem_spec] * 2,
-        scratch_shapes=[pltpu.SMEM((classes,), jnp.int32), pltpu.SemaphoreType.DMA((2,))],
-        compiler_params=params(11264),
+        scratch_shapes=[pltpu.SemaphoreType.DMA],
+        compiler_params=params(11 * 1024),
         name="choose",
-    )(place, sampled, weights)
+    )(lax.dynamic_slice_in_dim(sampled, replica * part, part), weights)
     def spread(block):
         near = [block]
         for _, bit in bits:

time: 41.6 us -> 41.3 us (level)
  starting transfers between devices: 20 us -> 21.1 us
  waiting for transfers between devices: 11.1 us -> 10.3 us
  Pallas kernels: 8.69 us -> 8.12 us
    ppermute x17, starting transfers between devices: 20 us -> 21.1 us  [swap(): lax.ppermute(value, ('cls', 'dp'), [(i, i ^ mask) for i in range(groups *...]
    ppermute x17, waiting for transfers between devices: 11.1 us -> 10.3 us  [swap(): lax.ppermute(value, ('cls', 'dp'), [(i, i ^ mask) for i in range(groups *...]
    dynamic_slice x0 -> x1, local copies, waits for them, and re-layouts: none -> 0.75 us  [per_device(): lax.dynamic_slice_in_dim(sampled, replica * part, part)]
    unnamed x6 -> x4, local copies, waits for them, and re-layouts: 0.69 us -> 0.01 us
    pallas_call x1, Pallas kernels: 2.66 us -> 2.1 us  [per_device(): pl.pallas_call(choose_kernel, out_shape=[jax.ShapeDtypeStruct((part + ext...]
  transfers between devices with their start and end apart: 17 -> 17, of which waited for: 9 -> 8; matrix products, arithmetic and copies ran while one was open for 0% -> 2% of each run, Pallas kernels for 13% -> 12%
where the time goes in v4:
time: 41.3 us; the launch traced here: 41.1 us
  starting transfers between devices  21.1 us (51%)
  waiting for transfers between devices  10.3 us (25%)
  Pallas kernels  8.12 us (20%)
  local copies, waits for them, and re-layouts  0.84 us (2%)
  between operations  0.74 us (2%)
    ppermute x17, starting transfers between devices, swap(): lax.ppermute(value, ('cls', 'dp'), [(i, i ^ mask) for i in range(groups *...  21.1 us
    ppermute x17, waiting for transfers between devices, swap(): lax.ppermute(value, ('cls', 'dp'), [(i, i ^ mask) for i in range(groups *...  10.3 us
    pallas_call x2, Pallas kernels, per_device(): pl.pallas_call(functools.partial(logits_kernel, count, span, len(arrays[j...  2.44 us
    pallas_call x2, Pallas kernels, grads(): pl.pallas_call(functools.partial(grads_kernel, count, replicas, spans, si...  2.41 us
    pallas_call x1, Pallas kernels, per_device(): pl.pallas_call(choose_kernel, out_shape=[jax.ShapeDtypeStruct((part + ext...  2.1 us
    pallas_call x1, Pallas kernels, per_device(): pl.pallas_call(finish_kernel, out_shape=jax.ShapeDtypeStruct((part, width...  0.91 us
  transfers between devices with their start and end apart: 17, of which 8 were waited for; matrix products, arithmetic and copies ran while one was open for 2% of the time, Pallas kernels for 12%

profile of v4, /device:TPU:0, one launch (start us, length us, event | category | flops | bytes accessed | tf_op | source)
XLA Modules:
  0.0 41.1 jit_solution(16317703034532989748)
XLA Ops:
  0.6 0.0 copy-start
  0.6 0.0 copy-start.1
  0.6 4.1 %collective-permute-start = (bf16[128,512]{1,0:T(8,128)(2,1)}, bf16[128,512]{1,0:T(8,128)(2,1)S(1)}, u32[]{:S(2)}, u32[]{:S(2)}) collective-permute-start(bf16[128,512]{1,0:T(8,128)(2,1)} %refs_0_.1), channel_id=1, source_target_pairs={{0,16},{1,17},{2,18},{3,19},{4,20},{5,21},{6,22},{7,23},{8,24},{9,... | collective-permute-start | bytes 393224 | tf_op jit(solution)/shard_map/ppermute | solution.py:195
  4.8 1.6 %collective-permute-start.1 = (bf16[128,512]{1,0:T(8,128)(2,1)}, bf16[128,512]{1,0:T(8,128)(2,1)S(1)}, u32[]{:S(2)}, u32[]{:S(2)}) collective-permute-start(bf16[128,512]{1,0:T(8,128)(2,1)} %refs_0_.1), channel_id=1, source_target_pairs={{0,8},{1,9},{2,10},{3,11},{4,12},{5,13},{6,14},{7,15},{8,0},{9,1},... | collective-permute-start | bytes 393224 | tf_op jit(solution)/shard_map/ppermute | solution.py:195
  6.3 0.3 collective-permute-start.3
  6.7 0.8 %dynamic_slice.3.sampled_ref = s32[128]{0:T(128)S(1)} dynamic-slice(s32[256]{0:T(256)} %param.7, s32[]{:T(128)S(6)} %select_n.9), dynamic_slice_sizes={128} | dynamic-slice | bytes 1028 | tf_op jit(solution)/shard_map/dynamic_slice | solution.py:218
  7.4 2.1 %choose.1 = (bf16[136,512]{1,0:T(8,128)(2,1)S(1)}, f32[128,512]{1,0:T(8,128)S(1)}) custom-call(s32[128]{0:T(128)S(1)} %dynamic_slice.3.sampled_ref, f32[1024,512]{1,0:T(8,128)} %weight_hbm.1), custom_call_target="tpu_custom_call" | custom-call | tf_op jit(solution)/shard_map/choose/pallas_call | solution.py:207
  9.5 1.6 %collective-permute-start.8 = (bf16[136,512]{1,0:T(8,128)(2,1)S(1)}, bf16[136,512]{1,0:T(8,128)(2,1)S(1)}, u32[]{:S(2)}, u32[]{:S(2)}) collective-permute-start(bf16[136,512]{1,0:T(8,128)(2,1)S(1)} %get-tuple-element.41.refs_3_), channel_id=1, source_target_pairs={{0,2},{1,3},{2,0},{3,1},{4,6},{5,7},{6,4},{7,5},{8,10},{9,11},{10,... | collective-permute-start | bytes 417800 | tf_op jit(solution)/shard_map/ppermute | solution.py:195
  11.1 1.5 %collective-permute-start.7 = (bf16[136,512]{1,0:T(8,128)(2,1)S(1)}, bf16[136,512]{1,0:T(8,128)(2,1)S(1)}, u32[]{:S(2)}, u32[]{:S(2)}) collective-permute-start(bf16[136,512]{1,0:T(8,128)(2,1)S(1)} %get-tuple-element.41.refs_3_), channel_id=1, source_target_pairs={{0,4},{1,5},{2,6},{3,7},{4,0},{5,1},{6,2},{7,3},{8,12},{9,13},{10,... | collective-permute-start | bytes 417800 | tf_op jit(solution)/shard_map/ppermute | solution.py:195
  12.6 0.0 collective-permute-done.3
  12.6 0.0 copy-done.1
  12.6 1.4 %collective-permute-start.6 = (bf16[136,512]{1,0:T(8,128)(2,1)S(1)}, bf16[136,512]{1,0:T(8,128)(2,1)S(1)}, u32[]{:S(2)}, u32[]{:S(2)}) collective-permute-start(bf16[136,512]{1,0:T(8,128)(2,1)S(1)} %get-tuple-element.41.refs_3_), channel_id=1, source_target_pairs={{0,6},{1,7},{2,4},{3,5},{4,2},{5,3},{6,0},{7,1},{8,14},{9,15},{10,... | collective-permute-start | bytes 417800 | tf_op jit(solution)/shard_map/ppermute | solution.py:195
  14.0 0.0 collective-permute-done.feat_ref
  14.0 0.0 collective-permute-done.1.refs_1_
  14.0 0.1 pack.1.refs_1_
  14.1 1.5 %collective-permute-start.5 = (bf16[136,512]{1,0:T(8,128)(2,1)S(1)}, bf16[136,512]{1,0:T(8,128)(2,1)S(1)}, u32[]{:S(2)}, u32[]{:S(2)}) collective-permute-start(bf16[136,512]{1,0:T(8,128)(2,1)S(1)} %pack.1.refs_1_), channel_id=1, source_target_pairs={{0,8},{1,9},{2,10},{3,11},{4,12},{5,13},{6,14},{7,15},{8,0},{9,1},... | collective-permute-start | bytes 417800 | tf_op jit(solution)/shard_map/ppermute | solution.py:195
  15.6 0.0 copy-done
  15.6 0.1 normalize.1.refs_0_
  15.8 0.1 collective-permute-start.2
  15.9 0.0 collective-permute-done.8.refs_4_
  15.9 0.5 %collective-permute-start.4 = (bf16[136,512]{1,0:T(8,128)(2,1)S(1)}, bf16[136,512]{1,0:T(8,128)(2,1)S(1)}, u32[]{:S(2)}, u32[]{:S(2)}) collective-permute-start(bf16[136,512]{1,0:T(8,128)(2,1)S(1)} %pack.1.refs_1_), channel_id=1, source_target_pairs={{0,1},{1,0},{2,3},{3,2},{4,5},{5,4},{6,7},{7,6},{8,9},{9,8},{10,11... | collective-permute-start | bytes 417800 | tf_op jit(solution)/shard_map/ppermute | solution.py:195
  16.4 2.8 %collective-permute-done.7.refs_5_ = bf16[136,512]{1,0:T(8,128)(2,1)S(1)} collective-permute-done((bf16[136,512]{1,0:T(8,128)(2,1)S(1)}, bf16[136,512]{1,0:T(8,128)(2,1)S(1)}, u32[]{:S(2)}, u32[]{:S(2)}) %collective-permute-start.7) | collective-permute-done | bytes 139296 | tf_op jit(solution)/shard_map/ppermute | solution.py:195
  19.1 0.0 collective-permute-done.6.refs_6_
  19.1 0.1 collective-permute-done.5.refs_2_
  19.3 0.0 collective-permute-start.9
  19.3 0.1 stack.27.place_ref
  19.3 1.2 %logits.2 = (f32[512,512]{1,0:T(8,128)S(1)}, f32[16,128]{1,0:T(8,128)S(1)}, bf16[512,512]{1,0:T(8,128)(2,1)S(1)}, s32[4,128]{1,0:T(4,128)S(1)}, bf16[512,512]{1,0:T(8,128)(2,1)S(1)}) custom-call(s32[6]{0:T(128)S(1)} %stack.27.place_ref, bf16[256,512]{1,0:T(8,128)(2,1)S(1)} %normalize.1.refs_0_, bf16[136,512]{1,0:T(8,128)(2,1)S(1)} %pack.1.refs_1_, ...), custom_call_target="tpu_custom_call" | custom-call | tf_op jit(solution)/shard_map/logits/pallas_call | solution.py:283
  20.6 0.0 collective-permute-done.4.refs_1_
  20.6 0.0 collective-permute-done.2.refs_0_
  20.6 0.0 collective-permute-done.9.refs_2_
  20.6 1.2 %logits.3 = (f32[512,512]{1,0:T(8,128)S(1)}, f32[16,128]{1,0:T(8,128)S(1)}, bf16[512,512]{1,0:T(8,128)(2,1)S(1)}, s32[4,128]{1,0:T(4,128)S(1)}) custom-call(s32[6]{0:T(128)S(1)} %stack.27.place_ref, bf16[256,512]{1,0:T(8,128)(2,1)S(1)} %collective-permute-done.2.refs_0_, bf16[136,512]{1,0:T(8,128)(2,1)S(1)} %collective-permute-done.4.refs_1_, ...), custom_call_target="tpu_custom_call" | custom-call | tf_op jit(solution)/shard_map/logits/pallas_call | solution.py:283
  21.8 1.6 %collective-permute-start.12 = (f32[16,128]{1,0:T(8,128)S(1)}, f32[16,128]{1,0:T(8,128)S(1)}, u32[]{:S(2)}, u32[]{:S(2)}) collective-permute-start(f32[16,128]{1,0:T(8,128)S(1)} %get-tuple-element.47), channel_id=1, source_target_pairs={{0,9},{1,8},{2,11},{3,10},{4,13},{5,12},{6,15},{7,14},{8,1},{9,0},... | collective-permute-start | bytes 24584 | tf_op jit(solution)/shard_map/ppermute | solution.py:195
  23.5 0.6 %collective-permute-start.11 = (f32[16,128]{1,0:T(8,128)S(1)}, f32[16,128]{1,0:T(8,128)S(1)}, u32[]{:S(2)}, u32[]{:S(2)}) collective-permute-start(f32[16,128]{1,0:T(8,128)S(1)} %get-tuple-element.47), channel_id=1, source_target_pairs={{0,8},{1,9},{2,10},{3,11},{4,12},{5,13},{6,14},{7,15},{8,0},{9,1},... | collective-permute-start | bytes 24584 | tf_op jit(solution)/shard_map/ppermute | solution.py:195
  24.0 0.0 collective-permute-start.10
  24.0 0.9 %collective-permute-done.12 = f32[16,128]{1,0:T(8,128)S(1)} collective-permute-done((f32[16,128]{1,0:T(8,128)S(1)}, f32[16,128]{1,0:T(8,128)S(1)}, u32[]{:S(2)}, u32[]{:S(2)}) %collective-permute-start.12) | collective-permute-done | bytes 8224 | tf_op jit(solution)/shard_map/ppermute | solution.py:195
  25.0 2.1 %collective-permute-done.11 = f32[16,128]{1,0:T(8,128)S(1)} collective-permute-done((f32[16,128]{1,0:T(8,128)S(1)}, f32[16,128]{1,0:T(8,128)S(1)}, u32[]{:S(2)}, u32[]{:S(2)}) %collective-permute-start.11) | collective-permute-done | bytes 8224 | tf_op jit(solution)/shard_map/ppermute | solution.py:195
  27.1 0.0 collective-permute-done.10
  27.1 2.8 %collective-permute-start.13 = (f32[16,128]{1,0:T(8,128)S(1)}, f32[16,128]{1,0:T(8,128)S(1)}, u32[]{:S(2)}, u32[]{:S(2)}) collective-permute-start(f32[16,128]{1,0:T(8,128)S(1)} %add_add_fusion), channel_id=1, source_target_pairs={{0,16},{1,17},{2,18},{3,19},{4,20},{5,21},{6,22},{7,23},{8,24},{9,... | collective-permute-start | bytes 24584 | tf_op jit(solution)/shard_map/ppermute | solution.py:195
  29.9 1.9 %collective-permute-done.13 = f32[16,128]{1,0:T(8,128)S(1)} collective-permute-done((f32[16,128]{1,0:T(8,128)S(1)}, f32[16,128]{1,0:T(8,128)S(1)}, u32[]{:S(2)}, u32[]{:S(2)}) %collective-permute-start.13) | collective-permute-done | bytes 8224 | tf_op jit(solution)/shard_map/ppermute | solution.py:195
  31.7 1.2 %grads.3 = (bf16[128,512]{1,0:T(8,128)(2,1)S(1)}, bf16[128,512]{1,0:T(8,128)(2,1)S(1)}, bf16[128,512]{1,0:T(8,128)(2,1)S(1)}) custom-call(s32[6]{0:T(128)S(1)} %stack.27.place_ref, f32[16,128]{1,0:T(8,128)S(1)} %add.40.stat_ref, f32[512,512]{1,0:T(8,128)S(1)} %get-tuple-element.48.refs_0_, bf16[512,512]{1,0:T(8,128)(2,1)S(1)} %get-tuple-element.49.refs_1_, ...), custom_call_target="tpu_custom_call" | custom-call | tf_op jit(solution)/shard_map/grads/pallas_call | solution.py:304
  32.9 0.6 %collective-permute-start.14 = (bf16[128,512]{1,0:T(8,128)(2,1)S(1)}, bf16[128,512]{1,0:T(8,128)(2,1)S(1)}, u32[]{:S(2)}, u32[]{:S(2)}) collective-permute-start(bf16[128,512]{1,0:T(8,128)(2,1)S(1)} %get-tuple-element.57), channel_id=1, source_target_pairs={{0,2},{1,3},{2,0},{3,1},{4,6},{5,7},{6,4},{7,5},{8,10},{9,11},{10,... | collective-permute-start | bytes 393224 | tf_op jit(solution)/shard_map/ppermute | solution.py:195
  33.5 0.8 %collective-permute-start.15 = (bf16[128,512]{1,0:T(8,128)(2,1)S(1)}, bf16[128,512]{1,0:T(8,128)(2,1)S(1)}, u32[]{:S(2)}, u32[]{:S(2)}) collective-permute-start(bf16[128,512]{1,0:T(8,128)(2,1)S(1)} %get-tuple-element.58), channel_id=1, source_target_pairs={{0,4},{1,5},{2,6},{3,7},{4,0},{5,1},{6,2},{7,3},{8,12},{9,13},{10,... | collective-permute-start | bytes 393224 | tf_op jit(solution)/shard_map/ppermute | solution.py:195
  34.3 2.1 %collective-permute-start.16 = (bf16[128,512]{1,0:T(8,128)(2,1)S(1)}, bf16[128,512]{1,0:T(8,128)(2,1)S(1)}, u32[]{:S(2)}, u32[]{:S(2)}) collective-permute-start(bf16[128,512]{1,0:T(8,128)(2,1)S(1)} %get-tuple-element.59), channel_id=1, source_target_pairs={{0,6},{1,7},{2,4},{3,5},{4,2},{5,3},{6,0},{7,1},{8,14},{9,15},{10,... | collective-permute-start | bytes 393224 | tf_op jit(solution)/shard_map/ppermute | solution.py:195
  36.5 1.3 %grads.2 = (f32[128,512]{1,0:T(8,128)S(1)}, f32[1,128]{1,0:T(1,128)}) custom-call(s32[6]{0:T(128)S(1)} %stack.27.place_ref, f32[16,128]{1,0:T(8,128)S(1)} %add.40.stat_ref, f32[512,512]{1,0:T(8,128)S(1)} %get-tuple-element.48.refs_0_, bf16[512,512]{1,0:T(8,128)(2,1)S(1)} %get-tuple-element.49.refs_1_, s32[4,128]{1,0:T(4,128)S(1)} %get-tuple-element.50.refs_2_, ...), custom_call_target="tpu_custom_call" | custom-call | tf_op jit(solution)/shard_map/grads/pallas_call | solution.py:304
  37.7 0.2 collective-permute-done.14.refs_0_
  37.9 0.5 %collective-permute-done.15.refs_1_ = bf16[128,512]{1,0:T(8,128)(2,1)S(1)} collective-permute-done((bf16[128,512]{1,0:T(8,128)(2,1)S(1)}, bf16[128,512]{1,0:T(8,128)(2,1)S(1)}, u32[]{:S(2)}, u32[]{:S(2)}) %collective-permute-start.15) | collective-permute-done | bytes 131104 | tf_op jit(solution)/shard_map/ppermute | solution.py:195
  38.5 1.7 %collective-permute-done.16.refs_2_ = bf16[128,512]{1,0:T(8,128)(2,1)S(1)} collective-permute-done((bf16[128,512]{1,0:T(8,128)(2,1)S(1)}, bf16[128,512]{1,0:T(8,128)(2,1)S(1)}, u32[]{:S(2)}, u32[]{:S(2)}) %collective-permute-start.16) | collective-permute-done | bytes 131104 | tf_op jit(solution)/shard_map/ppermute | solution.py:195
  40.2 0.9 %finish.1 = f32[128,512]{1,0:T(8,128)} custom-call(f32[128,512]{1,0:T(8,128)S(1)} %get-tuple-element.55.chosen_ref, f32[128,512]{1,0:T(8,128)S(1)} %get-tuple-element.56.own_ref, bf16[128,512]{1,0:T(8,128)(2,1)S(1)} %collective-permute-done.14.refs_0_, bf16[128,512]{1,0:T(8,128)(2,1)S(1)} %collective-permute-done.15.refs_1_, ...), custom_call_target="tpu_custom_call" | custom-call | tf_op jit(solution)/shard_map/finish/pallas_call | solution.py:319
  (3 shorter events, 0.0 us)
Async XLA Ops:
  0.6 15.0 %copy-start = (bf16[128,512]{1,0:T(8,128)(2,1)S(1)}, bf16[128,512]{1,0:T(8,128)(2,1)}, u32[]{:S(2)}) copy-start(bf16[128,512]{1,0:T(8,128)(2,1)} %refs_0_.1) | copy-start | bytes 393220
  0.6 12.0 %copy-start.1 = (s32[128]{0:T(128)S(1)}, s32[128]{0:T(128)}, u32[]{:S(2)}) copy-start(s32[128]{0:T(128)} %param.5) | copy-start | bytes 1540
  0.6 13.4 %collective-permute-start = (bf16[128,512]{1,0:T(8,128)(2,1)}, bf16[128,512]{1,0:T(8,128)(2,1)S(1)}, u32[]{:S(2)}, u32[]{:S(2)}) collective-permute-start(bf16[128,512]{1,0:T(8,128)(2,1)} %refs_0_.1), channel_id=1, source_target_pairs={{0,16},{1,17},{2,18},{3,19},{4,20},{5,21},{6,22},{7,23},{8,24},{9,... | collective-permute-start | bytes 393224 | tf_op jit(solution)/shard_map/ppermute | solution.py:195
  4.8 9.3 %collective-permute-start.1 = (bf16[128,512]{1,0:T(8,128)(2,1)}, bf16[128,512]{1,0:T(8,128)(2,1)S(1)}, u32[]{:S(2)}, u32[]{:S(2)}) collective-permute-start(bf16[128,512]{1,0:T(8,128)(2,1)} %refs_0_.1), channel_id=1, source_target_pairs={{0,8},{1,9},{2,10},{3,11},{4,12},{5,13},{6,14},{7,15},{8,0},{9,1},... | collective-permute-start | bytes 393224 | tf_op jit(solution)/shard_map/ppermute | solution.py:195
  6.3 6.3 %collective-permute-start.3 = (s32[1,128]{1,0:T(1,128)}, s32[1,128]{1,0:T(1,128)S(1)}, u32[]{:S(2)}, u32[]{:S(2)}) collective-permute-start(s32[1,128]{1,0:T(1,128)} %bitcast.8), channel_id=1, source_target_pairs={{0,16},{1,17},{2,18},{3,19},{4,20},{5,21},{6,22},{7,23},{8,24},{9,... | collective-permute-start | bytes 1544 | tf_op jit(solution)/shard_map/ppermute | solution.py:195
  9.5 6.3 %collective-permute-start.8 = (bf16[136,512]{1,0:T(8,128)(2,1)S(1)}, bf16[136,512]{1,0:T(8,128)(2,1)S(1)}, u32[]{:S(2)}, u32[]{:S(2)}) collective-permute-start(bf16[136,512]{1,0:T(8,128)(2,1)S(1)} %get-tuple-element.41.refs_3_), channel_id=1, source_target_pairs={{0,2},{1,3},{2,0},{3,1},{4,6},{5,7},{6,4},{7,5},{8,10},{9,11},{10,... | collective-permute-start | bytes 417800 | tf_op jit(solution)/shard_map/ppermute | solution.py:195
  11.1 8.0 %collective-permute-start.7 = (bf16[136,512]{1,0:T(8,128)(2,1)S(1)}, bf16[136,512]{1,0:T(8,128)(2,1)S(1)}, u32[]{:S(2)}, u32[]{:S(2)}) collective-permute-start(bf16[136,512]{1,0:T(8,128)(2,1)S(1)} %get-tuple-element.41.refs_3_), channel_id=1, source_target_pairs={{0,4},{1,5},{2,6},{3,7},{4,0},{5,1},{6,2},{7,3},{8,12},{9,13},{10,... | collective-permute-start | bytes 417800 | tf_op jit(solution)/shard_map/ppermute | solution.py:195
  12.6 6.5 %collective-permute-start.6 = (bf16[136,512]{1,0:T(8,128)(2,1)S(1)}, bf16[136,512]{1,0:T(8,128)(2,1)S(1)}, u32[]{:S(2)}, u32[]{:S(2)}) collective-permute-start(bf16[136,512]{1,0:T(8,128)(2,1)S(1)} %get-tuple-element.41.refs_3_), channel_id=1, source_target_pairs={{0,6},{1,7},{2,4},{3,5},{4,2},{5,3},{6,0},{7,1},{8,14},{9,15},{10,... | collective-permute-start | bytes 417800 | tf_op jit(solution)/shard_map/ppermute | solution.py:195
  14.1 5.1 %collective-permute-start.5 = (bf16[136,512]{1,0:T(8,128)(2,1)S(1)}, bf16[136,512]{1,0:T(8,128)(2,1)S(1)}, u32[]{:S(2)}, u32[]{:S(2)}) collective-permute-start(bf16[136,512]{1,0:T(8,128)(2,1)S(1)} %pack.1.refs_1_), channel_id=1, source_target_pairs={{0,8},{1,9},{2,10},{3,11},{4,12},{5,13},{6,14},{7,15},{8,0},{9,1},... | collective-permute-start | bytes 417800 | tf_op jit(solution)/shard_map/ppermute | solution.py:195
  15.8 4.8 %collective-permute-start.2 = (bf16[256,512]{1,0:T(8,128)(2,1)S(1)}, bf16[256,512]{1,0:T(8,128)(2,1)S(1)}, u32[]{:S(2)}, u32[]{:S(2)}) collective-permute-start(bf16[256,512]{1,0:T(8,128)(2,1)S(1)} %normalize.1.refs_0_), channel_id=1, source_target_pairs={{0,1},{1,0},{2,3},{3,2},{4,5},{5,4},{6,7},{7,6},{8,9},{9,8},{10,11... | collective-permute-start | bytes 786440 | tf_op jit(solution)/shard_map/ppermute | solution.py:195
  15.9 4.7 %collective-permute-start.4 = (bf16[136,512]{1,0:T(8,128)(2,1)S(1)}, bf16[136,512]{1,0:T(8,128)(2,1)S(1)}, u32[]{:S(2)}, u32[]{:S(2)}) collective-permute-start(bf16[136,512]{1,0:T(8,128)(2,1)S(1)} %pack.1.refs_1_), channel_id=1, source_target_pairs={{0,1},{1,0},{2,3},{3,2},{4,5},{5,4},{6,7},{7,6},{8,9},{9,8},{10,11... | collective-permute-start | bytes 417800 | tf_op jit(solution)/shard_map/ppermute | solution.py:195
  19.3 1.4 %collective-permute-start.9 = (bf16[136,512]{1,0:T(8,128)(2,1)S(1)}, bf16[136,512]{1,0:T(8,128)(2,1)S(1)}, u32[]{:S(2)}, u32[]{:S(2)}) collective-permute-start(bf16[136,512]{1,0:T(8,128)(2,1)S(1)} %collective-permute-done.5.refs_2_), channel_id=1, source_target_pairs={{0,1},{1,0},{2,3},{3,2},{4,5},{5,4},{6,7},{7,6},{8,9},{9,8},{10,11... | collective-permute-start | bytes 417800 | tf_op jit(solution)/shard_map/ppermute | solution.py:195
  21.8 3.1 %collective-permute-start.12 = (f32[16,128]{1,0:T(8,128)S(1)}, f32[16,128]{1,0:T(8,128)S(1)}, u32[]{:S(2)}, u32[]{:S(2)}) collective-permute-start(f32[16,128]{1,0:T(8,128)S(1)} %get-tuple-element.47), channel_id=1, source_target_pairs={{0,9},{1,8},{2,11},{3,10},{4,13},{5,12},{6,15},{7,14},{8,1},{9,0},... | collective-permute-start | bytes 24584 | tf_op jit(solution)/shard_map/ppermute | solution.py:195
  23.5 3.7 %collective-permute-start.11 = (f32[16,128]{1,0:T(8,128)S(1)}, f32[16,128]{1,0:T(8,128)S(1)}, u32[]{:S(2)}, u32[]{:S(2)}) collective-permute-start(f32[16,128]{1,0:T(8,128)S(1)} %get-tuple-element.47), channel_id=1, source_target_pairs={{0,8},{1,9},{2,10},{3,11},{4,12},{5,13},{6,14},{7,15},{8,0},{9,1},... | collective-permute-start | bytes 24584 | tf_op jit(solution)/shard_map/ppermute | solution.py:195
  24.0 3.1 %collective-permute-start.10 = (f32[16,128]{1,0:T(8,128)S(1)}, f32[16,128]{1,0:T(8,128)S(1)}, u32[]{:S(2)}, u32[]{:S(2)}) collective-permute-start(f32[16,128]{1,0:T(8,128)S(1)} %get-tuple-element.47), channel_id=1, source_target_pairs={{0,1},{1,0},{2,3},{3,2},{4,5},{5,4},{6,7},{7,6},{8,9},{9,8},{10,11... | collective-permute-start | bytes 24584 | tf_op jit(solution)/shard_map/ppermute | solution.py:195
  27.1 4.6 %collective-permute-start.13 = (f32[16,128]{1,0:T(8,128)S(1)}, f32[16,128]{1,0:T(8,128)S(1)}, u32[]{:S(2)}, u32[]{:S(2)}) collective-permute-start(f32[16,128]{1,0:T(8,128)S(1)} %add_add_fusion), channel_id=1, source_target_pairs={{0,16},{1,17},{2,18},{3,19},{4,20},{5,21},{6,22},{7,23},{8,24},{9,... | collective-permute-start | bytes 24584 | tf_op jit(solution)/shard_map/ppermute | solution.py:195
  32.9 5.0 %collective-permute-start.14 = (bf16[128,512]{1,0:T(8,128)(2,1)S(1)}, bf16[128,512]{1,0:T(8,128)(2,1)S(1)}, u32[]{:S(2)}, u32[]{:S(2)}) collective-permute-start(bf16[128,512]{1,0:T(8,128)(2,1)S(1)} %get-tuple-element.57), channel_id=1, source_target_pairs={{0,2},{1,3},{2,0},{3,1},{4,6},{5,7},{6,4},{7,5},{8,10},{9,11},{10,... | collective-permute-start | bytes 393224 | tf_op jit(solution)/shard_map/ppermute | solution.py:195
  33.5 5.0 %collective-permute-start.15 = (bf16[128,512]{1,0:T(8,128)(2,1)S(1)}, bf16[128,512]{1,0:T(8,128)(2,1)S(1)}, u32[]{:S(2)}, u32[]{:S(2)}) collective-permute-start(bf16[128,512]{1,0:T(8,128)(2,1)S(1)} %get-tuple-element.58), channel_id=1, source_target_pairs={{0,4},{1,5},{2,6},{3,7},{4,0},{5,1},{6,2},{7,3},{8,12},{9,13},{10,... | collective-permute-start | bytes 393224 | tf_op jit(solution)/shard_map/ppermute | solution.py:195
  34.3 5.9 %collective-permute-start.16 = (bf16[128,512]{1,0:T(8,128)(2,1)S(1)}, bf16[128,512]{1,0:T(8,128)(2,1)S(1)}, u32[]{:S(2)}, u32[]{:S(2)}) collective-permute-start(bf16[128,512]{1,0:T(8,128)(2,1)S(1)} %get-tuple-element.59), channel_id=1, source_target_pairs={{0,6},{1,7},{2,4},{3,5},{4,2},{5,3},{6,0},{7,1},{8,14},{9,15},{10,... | collective-permute-start | bytes 393224 | tf_op jit(solution)/shard_map/ppermute | solution.py:195

commit v5 on v4

--- a/solution.py
+++ b/solution.py
@@ -115,8 +115,8 @@
         for index in (pair, pair + 1):
             start = (index - pair) * lanes
             labels = label_ref[index : index + 1, :]
-            total = jnp.zeros((1, lanes), jnp.float32)
-            target = jnp.zeros((1, lanes), jnp.float32)
+            total = jnp.zeros((8, lanes), jnp.float32)
+            target = jnp.zeros((8, lanes), jnp.float32)
             for side in range(square):
                 lines = slice(side * part, (side + 1) * part)
                 hit = labels - place_ref[side] == line
@@ -125,11 +125,11 @@
                     tile - jnp.where(hit, logit_scale + logit_scale * margin, logit_scale)
                 )
                 exp_ref[lines, index * lanes : (index + 1) * lanes] = exps
-                total = total + jnp.sum(exps, axis=0, keepdims=True)
-                target = target + jnp.sum(jnp.where(hit, tile, 0.0), axis=0, keepdims=True)
+                total = total + jnp.sum(exps.reshape(-1, 8, lanes), axis=0)
+                target = target + jnp.sum(jnp.where(hit, tile, 0.0).reshape(-1, 8, lanes), axis=0)
             group = place_ref[square + 1] ^ span[index][0]
-            stat_ref[pl.ds(group, 1), :] = total
-            stat_ref[pl.ds(count + group, 1), :] = target
+            stat_ref[pl.ds(group, 1), :] = jnp.sum(total, axis=0, keepdims=True)
+            stat_ref[pl.ds(count + group, 1), :] = jnp.sum(target, axis=0, keepdims=True)
 
 
 def grads_kernel(count, replicas, spans, sides, place_ref, stat_ref, *refs):

time: 41.3 us -> 41.2 us (level)
  no operation moved by 1% of the time
where the time goes in v5:
time: 41.2 us; the launch traced here: 41.1 us
  starting transfers between devices  21.1 us (51%)
  waiting for transfers between devices  10.3 us (25%)
  Pallas kernels  8.1 us (20%)
  local copies, waits for them, and re-layouts  0.84 us (2%)
  between operations  0.74 us (2%)
    ppermute x17, starting transfers between devices, swap(): lax.ppermute(value, ('cls', 'dp'), [(i, i ^ mask) for i in range(groups *...  21.1 us
    ppermute x17, waiting for transfers between devices, swap(): lax.ppermute(value, ('cls', 'dp'), [(i, i ^ mask) for i in range(groups *...  10.3 us
    pallas_call x2, Pallas kernels, grads(): pl.pallas_call(functools.partial(grads_kernel, count, replicas, spans, si...  2.42 us
    pallas_call x2, Pallas kernels, per_device(): pl.pallas_call(functools.partial(logits_kernel, count, span, len(arrays[j...  2.41 us
    pallas_call x1, Pallas kernels, per_device(): pl.pallas_call(choose_kernel, out_shape=[jax.ShapeDtypeStruct((part + ext...  2.1 us
    pallas_call x1, Pallas kernels, per_device(): pl.pallas_call(finish_kernel, out_shape=jax.ShapeDtypeStruct((part, width...  0.91 us
  transfers between devices with their start and end apart: 17, of which 8 were waited for; matrix products, arithmetic and copies ran while one was open for 2% of the time, Pallas kernels for 12%

profile of v5, /device:TPU:0, one launch (start us, length us, event | category | flops | bytes accessed | tf_op | source)
XLA Modules:
  0.0 41.1 jit_solution(17994489892613724625)
XLA Ops:
  0.6 0.0 copy-start
  0.6 0.0 copy-start.1
  0.6 4.1 %collective-permute-start = (bf16[128,512]{1,0:T(8,128)(2,1)}, bf16[128,512]{1,0:T(8,128)(2,1)S(1)}, u32[]{:S(2)}, u32[]{:S(2)}) collective-permute-start(bf16[128,512]{1,0:T(8,128)(2,1)} %refs_0_.1), channel_id=1, source_target_pairs={{0,16},{1,17},{2,18},{3,19},{4,20},{5,21},{6,22},{7,23},{8,24},{9,... | collective-permute-start | bytes 393224 | tf_op jit(solution)/shard_map/ppermute | solution.py:195
  4.8 1.6 %collective-permute-start.1 = (bf16[128,512]{1,0:T(8,128)(2,1)}, bf16[128,512]{1,0:T(8,128)(2,1)S(1)}, u32[]{:S(2)}, u32[]{:S(2)}) collective-permute-start(bf16[128,512]{1,0:T(8,128)(2,1)} %refs_0_.1), channel_id=1, source_target_pairs={{0,8},{1,9},{2,10},{3,11},{4,12},{5,13},{6,14},{7,15},{8,0},{9,1},... | collective-permute-start | bytes 393224 | tf_op jit(solution)/shard_map/ppermute | solution.py:195
  6.3 0.3 collective-permute-start.3
  6.7 0.8 %dynamic_slice.3.sampled_ref = s32[128]{0:T(128)S(1)} dynamic-slice(s32[256]{0:T(256)} %param.7, s32[]{:T(128)S(6)} %select_n.9), dynamic_slice_sizes={128} | dynamic-slice | bytes 1028 | tf_op jit(solution)/shard_map/dynamic_slice | solution.py:218
  7.4 2.1 %choose.1 = (bf16[136,512]{1,0:T(8,128)(2,1)S(1)}, f32[128,512]{1,0:T(8,128)S(1)}) custom-call(s32[128]{0:T(128)S(1)} %dynamic_slice.3.sampled_ref, f32[1024,512]{1,0:T(8,128)} %weight_hbm.1), custom_call_target="tpu_custom_call" | custom-call | tf_op jit(solution)/shard_map/choose/pallas_call | solution.py:207
  9.5 1.6 %collective-permute-start.8 = (bf16[136,512]{1,0:T(8,128)(2,1)S(1)}, bf16[136,512]{1,0:T(8,128)(2,1)S(1)}, u32[]{:S(2)}, u32[]{:S(2)}) collective-permute-start(bf16[136,512]{1,0:T(8,128)(2,1)S(1)} %get-tuple-element.41.refs_3_), channel_id=1, source_target_pairs={{0,2},{1,3},{2,0},{3,1},{4,6},{5,7},{6,4},{7,5},{8,10},{9,11},{10,... | collective-permute-start | bytes 417800 | tf_op jit(solution)/shard_map/ppermute | solution.py:195
  11.1 1.5 %collective-permute-start.7 = (bf16[136,512]{1,0:T(8,128)(2,1)S(1)}, bf16[136,512]{1,0:T(8,128)(2,1)S(1)}, u32[]{:S(2)}, u32[]{:S(2)}) collective-permute-start(bf16[136,512]{1,0:T(8,128)(2,1)S(1)} %get-tuple-element.41.refs_3_), channel_id=1, source_target_pairs={{0,4},{1,5},{2,6},{3,7},{4,0},{5,1},{6,2},{7,3},{8,12},{9,13},{10,... | collective-permute-start | bytes 417800 | tf_op jit(solution)/shard_map/ppermute | solution.py:195
  12.6 0.0 collective-permute-done.3
  12.6 0.0 copy-done.1
  12.6 1.4 %collective-permute-start.6 = (bf16[136,512]{1,0:T(8,128)(2,1)S(1)}, bf16[136,512]{1,0:T(8,128)(2,1)S(1)}, u32[]{:S(2)}, u32[]{:S(2)}) collective-permute-start(bf16[136,512]{1,0:T(8,128)(2,1)S(1)} %get-tuple-element.41.refs_3_), channel_id=1, source_target_pairs={{0,6},{1,7},{2,4},{3,5},{4,2},{5,3},{6,0},{7,1},{8,14},{9,15},{10,... | collective-permute-start | bytes 417800 | tf_op jit(solution)/shard_map/ppermute | solution.py:195
  14.0 0.0 collective-permute-done.feat_ref
  14.0 0.0 collective-permute-done.1.refs_1_
  14.0 0.1 pack.1.refs_1_
  14.1 1.5 %collective-permute-start.5 = (bf16[136,512]{1,0:T(8,128)(2,1)S(1)}, bf16[136,512]{1,0:T(8,128)(2,1)S(1)}, u32[]{:S(2)}, u32[]{:S(2)}) collective-permute-start(bf16[136,512]{1,0:T(8,128)(2,1)S(1)} %pack.1.refs_1_), channel_id=1, source_target_pairs={{0,8},{1,9},{2,10},{3,11},{4,12},{5,13},{6,14},{7,15},{8,0},{9,1},... | collective-permute-start | bytes 417800 | tf_op jit(solution)/shard_map/ppermute | solution.py:195
  15.6 0.0 copy-done
  15.6 0.1 normalize.1.refs_0_
  15.8 0.1 collective-permute-start.2
  15.9 0.0 collective-permute-done.8.refs_4_
  15.9 0.5 %collective-permute-start.4 = (bf16[136,512]{1,0:T(8,128)(2,1)S(1)}, bf16[136,512]{1,0:T(8,128)(2,1)S(1)}, u32[]{:S(2)}, u32[]{:S(2)}) collective-permute-start(bf16[136,512]{1,0:T(8,128)(2,1)S(1)} %pack.1.refs_1_), channel_id=1, source_target_pairs={{0,1},{1,0},{2,3},{3,2},{4,5},{5,4},{6,7},{7,6},{8,9},{9,8},{10,11... | collective-permute-start | bytes 417800 | tf_op jit(solution)/shard_map/ppermute | solution.py:195
  16.4 2.8 %collective-permute-done.7.refs_5_ = bf16[136,512]{1,0:T(8,128)(2,1)S(1)} collective-permute-done((bf16[136,512]{1,0:T(8,128)(2,1)S(1)}, bf16[136,512]{1,0:T(8,128)(2,1)S(1)}, u32[]{:S(2)}, u32[]{:S(2)}) %collective-permute-start.7) | collective-permute-done | bytes 139296 | tf_op jit(solution)/shard_map/ppermute | solution.py:195
  19.1 0.0 collective-permute-done.6.refs_6_
  19.1 0.1 collective-permute-done.5.refs_2_
  19.3 0.0 collective-permute-start.9
  19.3 0.1 stack.27.place_ref
  19.3 1.2 %logits.2 = (f32[512,512]{1,0:T(8,128)S(1)}, f32[16,128]{1,0:T(8,128)S(1)}, bf16[512,512]{1,0:T(8,128)(2,1)S(1)}, s32[4,128]{1,0:T(4,128)S(1)}, bf16[512,512]{1,0:T(8,128)(2,1)S(1)}) custom-call(s32[6]{0:T(128)S(1)} %stack.27.place_ref, bf16[256,512]{1,0:T(8,128)(2,1)S(1)} %normalize.1.refs_0_, bf16[136,512]{1,0:T(8,128)(2,1)S(1)} %pack.1.refs_1_, ...), custom_call_target="tpu_custom_call" | custom-call | tf_op jit(solution)/shard_map/logits/pallas_call | solution.py:283
  20.6 0.0 collective-permute-done.4.refs_1_
  20.6 0.0 collective-permute-done.2.refs_0_
  20.6 0.0 collective-permute-done.9.refs_2_
  20.6 1.2 %logits.3 = (f32[512,512]{1,0:T(8,128)S(1)}, f32[16,128]{1,0:T(8,128)S(1)}, bf16[512,512]{1,0:T(8,128)(2,1)S(1)}, s32[4,128]{1,0:T(4,128)S(1)}) custom-call(s32[6]{0:T(128)S(1)} %stack.27.place_ref, bf16[256,512]{1,0:T(8,128)(2,1)S(1)} %collective-permute-done.2.refs_0_, bf16[136,512]{1,0:T(8,128)(2,1)S(1)} %collective-permute-done.4.refs_1_, ...), custom_call_target="tpu_custom_call" | custom-call | tf_op jit(solution)/shard_map/logits/pallas_call | solution.py:283
  21.8 1.6 %collective-permute-start.12 = (f32[16,128]{1,0:T(8,128)S(1)}, f32[16,128]{1,0:T(8,128)S(1)}, u32[]{:S(2)}, u32[]{:S(2)}) collective-permute-start(f32[16,128]{1,0:T(8,128)S(1)} %get-tuple-element.47), channel_id=1, source_target_pairs={{0,9},{1,8},{2,11},{3,10},{4,13},{5,12},{6,15},{7,14},{8,1},{9,0},... | collective-permute-start | bytes 24584 | tf_op jit(solution)/shard_map/ppermute | solution.py:195
  23.4 0.6 %collective-permute-start.11 = (f32[16,128]{1,0:T(8,128)S(1)}, f32[16,128]{1,0:T(8,128)S(1)}, u32[]{:S(2)}, u32[]{:S(2)}) collective-permute-start(f32[16,128]{1,0:T(8,128)S(1)} %get-tuple-element.47), channel_id=1, source_target_pairs={{0,8},{1,9},{2,10},{3,11},{4,12},{5,13},{6,14},{7,15},{8,0},{9,1},... | collective-permute-start | bytes 24584 | tf_op jit(solution)/shard_map/ppermute | solution.py:195
  24.0 0.0 collective-permute-start.10
  24.0 0.9 %collective-permute-done.12 = f32[16,128]{1,0:T(8,128)S(1)} collective-permute-done((f32[16,128]{1,0:T(8,128)S(1)}, f32[16,128]{1,0:T(8,128)S(1)}, u32[]{:S(2)}, u32[]{:S(2)}) %collective-permute-start.12) | collective-permute-done | bytes 8224 | tf_op jit(solution)/shard_map/ppermute | solution.py:195
  25.0 2.1 %collective-permute-done.11 = f32[16,128]{1,0:T(8,128)S(1)} collective-permute-done((f32[16,128]{1,0:T(8,128)S(1)}, f32[16,128]{1,0:T(8,128)S(1)}, u32[]{:S(2)}, u32[]{:S(2)}) %collective-permute-start.11) | collective-permute-done | bytes 8224 | tf_op jit(solution)/shard_map/ppermute | solution.py:195
  27.1 0.0 collective-permute-done.10
  27.1 2.8 %collective-permute-start.13 = (f32[16,128]{1,0:T(8,128)S(1)}, f32[16,128]{1,0:T(8,128)S(1)}, u32[]{:S(2)}, u32[]{:S(2)}) collective-permute-start(f32[16,128]{1,0:T(8,128)S(1)} %add_add_fusion), channel_id=1, source_target_pairs={{0,16},{1,17},{2,18},{3,19},{4,20},{5,21},{6,22},{7,23},{8,24},{9,... | collective-permute-start | bytes 24584 | tf_op jit(solution)/shard_map/ppermute | solution.py:195
  29.9 1.9 %collective-permute-done.13 = f32[16,128]{1,0:T(8,128)S(1)} collective-permute-done((f32[16,128]{1,0:T(8,128)S(1)}, f32[16,128]{1,0:T(8,128)S(1)}, u32[]{:S(2)}, u32[]{:S(2)}) %collective-permute-start.13) | collective-permute-done | bytes 8224 | tf_op jit(solution)/shard_map/ppermute | solution.py:195
  31.7 1.2 %grads.3 = (bf16[128,512]{1,0:T(8,128)(2,1)S(1)}, bf16[128,512]{1,0:T(8,128)(2,1)S(1)}, bf16[128,512]{1,0:T(8,128)(2,1)S(1)}) custom-call(s32[6]{0:T(128)S(1)} %stack.27.place_ref, f32[16,128]{1,0:T(8,128)S(1)} %add.40.stat_ref, f32[512,512]{1,0:T(8,128)S(1)} %get-tuple-element.48.refs_0_, bf16[512,512]{1,0:T(8,128)(2,1)S(1)} %get-tuple-element.49.refs_1_, ...), custom_call_target="tpu_custom_call" | custom-call | tf_op jit(solution)/shard_map/grads/pallas_call | solution.py:304
  32.9 0.6 %collective-permute-start.14 = (bf16[128,512]{1,0:T(8,128)(2,1)S(1)}, bf16[128,512]{1,0:T(8,128)(2,1)S(1)}, u32[]{:S(2)}, u32[]{:S(2)}) collective-permute-start(bf16[128,512]{1,0:T(8,128)(2,1)S(1)} %get-tuple-element.57), channel_id=1, source_target_pairs={{0,2},{1,3},{2,0},{3,1},{4,6},{5,7},{6,4},{7,5},{8,10},{9,11},{10,... | collective-permute-start | bytes 393224 | tf_op jit(solution)/shard_map/ppermute | solution.py:195
  33.5 0.8 %collective-permute-start.15 = (bf16[128,512]{1,0:T(8,128)(2,1)S(1)}, bf16[128,512]{1,0:T(8,128)(2,1)S(1)}, u32[]{:S(2)}, u32[]{:S(2)}) collective-permute-start(bf16[128,512]{1,0:T(8,128)(2,1)S(1)} %get-tuple-element.58), channel_id=1, source_target_pairs={{0,4},{1,5},{2,6},{3,7},{4,0},{5,1},{6,2},{7,3},{8,12},{9,13},{10,... | collective-permute-start | bytes 393224 | tf_op jit(solution)/shard_map/ppermute | solution.py:195
  34.3 2.2 %collective-permute-start.16 = (bf16[128,512]{1,0:T(8,128)(2,1)S(1)}, bf16[128,512]{1,0:T(8,128)(2,1)S(1)}, u32[]{:S(2)}, u32[]{:S(2)}) collective-permute-start(bf16[128,512]{1,0:T(8,128)(2,1)S(1)} %get-tuple-element.59), channel_id=1, source_target_pairs={{0,6},{1,7},{2,4},{3,5},{4,2},{5,3},{6,0},{7,1},{8,14},{9,15},{10,... | collective-permute-start | bytes 393224 | tf_op jit(solution)/shard_map/ppermute | solution.py:195
  36.4 1.3 %grads.2 = (f32[128,512]{1,0:T(8,128)S(1)}, f32[1,128]{1,0:T(1,128)}) custom-call(s32[6]{0:T(128)S(1)} %stack.27.place_ref, f32[16,128]{1,0:T(8,128)S(1)} %add.40.stat_ref, f32[512,512]{1,0:T(8,128)S(1)} %get-tuple-element.48.refs_0_, bf16[512,512]{1,0:T(8,128)(2,1)S(1)} %get-tuple-element.49.refs_1_, s32[4,128]{1,0:T(4,128)S(1)} %get-tuple-element.50.refs_2_, ...), custom_call_target="tpu_custom_call" | custom-call | tf_op jit(solution)/shard_map/grads/pallas_call | solution.py:304
  37.7 0.2 collective-permute-done.14.refs_0_
  37.9 0.5 %collective-permute-done.15.refs_1_ = bf16[128,512]{1,0:T(8,128)(2,1)S(1)} collective-permute-done((bf16[128,512]{1,0:T(8,128)(2,1)S(1)}, bf16[128,512]{1,0:T(8,128)(2,1)S(1)}, u32[]{:S(2)}, u32[]{:S(2)}) %collective-permute-start.15) | collective-permute-done | bytes 131104 | tf_op jit(solution)/shard_map/ppermute | solution.py:195
  38.5 1.7 %collective-permute-done.16.refs_2_ = bf16[128,512]{1,0:T(8,128)(2,1)S(1)} collective-permute-done((bf16[128,512]{1,0:T(8,128)(2,1)S(1)}, bf16[128,512]{1,0:T(8,128)(2,1)S(1)}, u32[]{:S(2)}, u32[]{:S(2)}) %collective-permute-start.16) | collective-permute-done | bytes 131104 | tf_op jit(solution)/shard_map/ppermute | solution.py:195
  40.2 0.9 %finish.1 = f32[128,512]{1,0:T(8,128)} custom-call(f32[128,512]{1,0:T(8,128)S(1)} %get-tuple-element.55.chosen_ref, f32[128,512]{1,0:T(8,128)S(1)} %get-tuple-element.56.own_ref, bf16[128,512]{1,0:T(8,128)(2,1)S(1)} %collective-permute-done.14.refs_0_, bf16[128,512]{1,0:T(8,128)(2,1)S(1)} %collective-permute-done.15.refs_1_, ...), custom_call_target="tpu_custom_call" | custom-call | tf_op jit(solution)/shard_map/finish/pallas_call | solution.py:319
  (3 shorter events, 0.0 us)
Async XLA Ops:
  0.6 15.0 %copy-start = (bf16[128,512]{1,0:T(8,128)(2,1)S(1)}, bf16[128,512]{1,0:T(8,128)(2,1)}, u32[]{:S(2)}) copy-start(bf16[128,512]{1,0:T(8,128)(2,1)} %refs_0_.1) | copy-start | bytes 393220
  0.6 12.0 %copy-start.1 = (s32[128]{0:T(128)S(1)}, s32[128]{0:T(128)}, u32[]{:S(2)}) copy-start(s32[128]{0:T(128)} %param.5) | copy-start | bytes 1540
  0.6 13.4 %collective-permute-start = (bf16[128,512]{1,0:T(8,128)(2,1)}, bf16[128,512]{1,0:T(8,128)(2,1)S(1)}, u32[]{:S(2)}, u32[]{:S(2)}) collective-permute-start(bf16[128,512]{1,0:T(8,128)(2,1)} %refs_0_.1), channel_id=1, source_target_pairs={{0,16},{1,17},{2,18},{3,19},{4,20},{5,21},{6,22},{7,23},{8,24},{9,... | collective-permute-start | bytes 393224 | tf_op jit(solution)/shard_map/ppermute | solution.py:195
  4.8 9.3 %collective-permute-start.1 = (bf16[128,512]{1,0:T(8,128)(2,1)}, bf16[128,512]{1,0:T(8,128)(2,1)S(1)}, u32[]{:S(2)}, u32[]{:S(2)}) collective-permute-start(bf16[128,512]{1,0:T(8,128)(2,1)} %refs_0_.1), channel_id=1, source_target_pairs={{0,8},{1,9},{2,10},{3,11},{4,12},{5,13},{6,14},{7,15},{8,0},{9,1},... | collective-permute-start | bytes 393224 | tf_op jit(solution)/shard_map/ppermute | solution.py:195
  6.3 6.3 %collective-permute-start.3 = (s32[1,128]{1,0:T(1,128)}, s32[1,128]{1,0:T(1,128)S(1)}, u32[]{:S(2)}, u32[]{:S(2)}) collective-permute-start(s32[1,128]{1,0:T(1,128)} %bitcast.8), channel_id=1, source_target_pairs={{0,16},{1,17},{2,18},{3,19},{4,20},{5,21},{6,22},{7,23},{8,24},{9,... | collective-permute-start | bytes 1544 | tf_op jit(solution)/shard_map/ppermute | solution.py:195
  9.5 6.3 %collective-permute-start.8 = (bf16[136,512]{1,0:T(8,128)(2,1)S(1)}, bf16[136,512]{1,0:T(8,128)(2,1)S(1)}, u32[]{:S(2)}, u32[]{:S(2)}) collective-permute-start(bf16[136,512]{1,0:T(8,128)(2,1)S(1)} %get-tuple-element.41.refs_3_), channel_id=1, source_target_pairs={{0,2},{1,3},{2,0},{3,1},{4,6},{5,7},{6,4},{7,5},{8,10},{9,11},{10,... | collective-permute-start | bytes 417800 | tf_op jit(solution)/shard_map/ppermute | solution.py:195
  11.1 8.0 %collective-permute-start.7 = (bf16[136,512]{1,0:T(8,128)(2,1)S(1)}, bf16[136,512]{1,0:T(8,128)(2,1)S(1)}, u32[]{:S(2)}, u32[]{:S(2)}) collective-permute-start(bf16[136,512]{1,0:T(8,128)(2,1)S(1)} %get-tuple-element.41.refs_3_), channel_id=1, source_target_pairs={{0,4},{1,5},{2,6},{3,7},{4,0},{5,1},{6,2},{7,3},{8,12},{9,13},{10,... | collective-permute-start | bytes 417800 | tf_op jit(solution)/shard_map/ppermute | solution.py:195
  12.6 6.5 %collective-permute-start.6 = (bf16[136,512]{1,0:T(8,128)(2,1)S(1)}, bf16[136,512]{1,0:T(8,128)(2,1)S(1)}, u32[]{:S(2)}, u32[]{:S(2)}) collective-permute-start(bf16[136,512]{1,0:T(8,128)(2,1)S(1)} %get-tuple-element.41.refs_3_), channel_id=1, source_target_pairs={{0,6},{1,7},{2,4},{3,5},{4,2},{5,3},{6,0},{7,1},{8,14},{9,15},{10,... | collective-permute-start | bytes 417800 | tf_op jit(solution)/shard_map/ppermute | solution.py:195
  14.1 5.1 %collective-permute-start.5 = (bf16[136,512]{1,0:T(8,128)(2,1)S(1)}, bf16[136,512]{1,0:T(8,128)(2,1)S(1)}, u32[]{:S(2)}, u32[]{:S(2)}) collective-permute-start(bf16[136,512]{1,0:T(8,128)(2,1)S(1)} %pack.1.refs_1_), channel_id=1, source_target_pairs={{0,8},{1,9},{2,10},{3,11},{4,12},{5,13},{6,14},{7,15},{8,0},{9,1},... | collective-permute-start | bytes 417800 | tf_op jit(solution)/shard_map/ppermute | solution.py:195
  15.8 4.8 %collective-permute-start.2 = (bf16[256,512]{1,0:T(8,128)(2,1)S(1)}, bf16[256,512]{1,0:T(8,128)(2,1)S(1)}, u32[]{:S(2)}, u32[]{:S(2)}) collective-permute-start(bf16[256,512]{1,0:T(8,128)(2,1)S(1)} %normalize.1.refs_0_), channel_id=1, source_target_pairs={{0,1},{1,0},{2,3},{3,2},{4,5},{5,4},{6,7},{7,6},{8,9},{9,8},{10,11... | collective-permute-start | bytes 786440 | tf_op jit(solution)/shard_map/ppermute | solution.py:195
  15.9 4.7 %collective-permute-start.4 = (bf16[136,512]{1,0:T(8,128)(2,1)S(1)}, bf16[136,512]{1,0:T(8,128)(2,1)S(1)}, u32[]{:S(2)}, u32[]{:S(2)}) collective-permute-start(bf16[136,512]{1,0:T(8,128)(2,1)S(1)} %pack.1.refs_1_), channel_id=1, source_target_pairs={{0,1},{1,0},{2,3},{3,2},{4,5},{5,4},{6,7},{7,6},{8,9},{9,8},{10,11... | collective-permute-start | bytes 417800 | tf_op jit(solution)/shard_map/ppermute | solution.py:195
  19.3 1.4 %collective-permute-start.9 = (bf16[136,512]{1,0:T(8,128)(2,1)S(1)}, bf16[136,512]{1,0:T(8,128)(2,1)S(1)}, u32[]{:S(2)}, u32[]{:S(2)}) collective-permute-start(bf16[136,512]{1,0:T(8,128)(2,1)S(1)} %collective-permute-done.5.refs_2_), channel_id=1, source_target_pairs={{0,1},{1,0},{2,3},{3,2},{4,5},{5,4},{6,7},{7,6},{8,9},{9,8},{10,11... | collective-permute-start | bytes 417800 | tf_op jit(solution)/shard_map/ppermute | solution.py:195
  21.8 3.1 %collective-permute-start.12 = (f32[16,128]{1,0:T(8,128)S(1)}, f32[16,128]{1,0:T(8,128)S(1)}, u32[]{:S(2)}, u32[]{:S(2)}) collective-permute-start(f32[16,128]{1,0:T(8,128)S(1)} %get-tuple-element.47), channel_id=1, source_target_pairs={{0,9},{1,8},{2,11},{3,10},{4,13},{5,12},{6,15},{7,14},{8,1},{9,0},... | collective-permute-start | bytes 24584 | tf_op jit(solution)/shard_map/ppermute | solution.py:195
  23.4 3.7 %collective-permute-start.11 = (f32[16,128]{1,0:T(8,128)S(1)}, f32[16,128]{1,0:T(8,128)S(1)}, u32[]{:S(2)}, u32[]{:S(2)}) collective-permute-start(f32[16,128]{1,0:T(8,128)S(1)} %get-tuple-element.47), channel_id=1, source_target_pairs={{0,8},{1,9},{2,10},{3,11},{4,12},{5,13},{6,14},{7,15},{8,0},{9,1},... | collective-permute-start | bytes 24584 | tf_op jit(solution)/shard_map/ppermute | solution.py:195
  24.0 3.1 %collective-permute-start.10 = (f32[16,128]{1,0:T(8,128)S(1)}, f32[16,128]{1,0:T(8,128)S(1)}, u32[]{:S(2)}, u32[]{:S(2)}) collective-permute-start(f32[16,128]{1,0:T(8,128)S(1)} %get-tuple-element.47), channel_id=1, source_target_pairs={{0,1},{1,0},{2,3},{3,2},{4,5},{5,4},{6,7},{7,6},{8,9},{9,8},{10,11... | collective-permute-start | bytes 24584 | tf_op jit(solution)/shard_map/ppermute | solution.py:195
  27.1 4.6 %collective-permute-start.13 = (f32[16,128]{1,0:T(8,128)S(1)}, f32[16,128]{1,0:T(8,128)S(1)}, u32[]{:S(2)}, u32[]{:S(2)}) collective-permute-start(f32[16,128]{1,0:T(8,128)S(1)} %add_add_fusion), channel_id=1, source_target_pairs={{0,16},{1,17},{2,18},{3,19},{4,20},{5,21},{6,22},{7,23},{8,24},{9,... | collective-permute-start | bytes 24584 | tf_op jit(solution)/shard_map/ppermute | solution.py:195
  32.9 5.0 %collective-permute-start.14 = (bf16[128,512]{1,0:T(8,128)(2,1)S(1)}, bf16[128,512]{1,0:T(8,128)(2,1)S(1)}, u32[]{:S(2)}, u32[]{:S(2)}) collective-permute-start(bf16[128,512]{1,0:T(8,128)(2,1)S(1)} %get-tuple-element.57), channel_id=1, source_target_pairs={{0,2},{1,3},{2,0},{3,1},{4,6},{5,7},{6,4},{7,5},{8,10},{9,11},{10,... | collective-permute-start | bytes 393224 | tf_op jit(solution)/shard_map/ppermute | solution.py:195
  33.5 5.0 %collective-permute-start.15 = (bf16[128,512]{1,0:T(8,128)(2,1)S(1)}, bf16[128,512]{1,0:T(8,128)(2,1)S(1)}, u32[]{:S(2)}, u32[]{:S(2)}) collective-permute-start(bf16[128,512]{1,0:T(8,128)(2,1)S(1)} %get-tuple-element.58), channel_id=1, source_target_pairs={{0,4},{1,5},{2,6},{3,7},{4,0},{5,1},{6,2},{7,3},{8,12},{9,13},{10,... | collective-permute-start | bytes 393224 | tf_op jit(solution)/shard_map/ppermute | solution.py:195
  34.3 5.9 %collective-permute-start.16 = (bf16[128,512]{1,0:T(8,128)(2,1)S(1)}, bf16[128,512]{1,0:T(8,128)(2,1)S(1)}, u32[]{:S(2)}, u32[]{:S(2)}) collective-permute-start(bf16[128,512]{1,0:T(8,128)(2,1)S(1)} %get-tuple-element.59), channel_id=1, source_target_pairs={{0,6},{1,7},{2,4},{3,5},{4,2},{5,3},{6,0},{7,1},{8,14},{9,15},{10,... | collective-permute-start | bytes 393224 | tf_op jit(solution)/shard_map/ppermute | solution.py:195

commit v6 on v5

--- a/solution.py
+++ b/solution.py
@@ -251,6 +251,7 @@
     rows = tie(rows[::-1])[::-1]
     passed, rows = tie((passed, rows))
     ups = list(packed)
+    pair, place = tie((pair, place))
     held = [pair, *packed.values(), *passed.values()]
     spread_out = [spread(array) for array in held]
     count = groups // square * replicas

time: 41.2 us -> 41.2 us (level)
  transfers between devices with their start and end apart: 17 -> 17, of which waited for: 8 -> 9; matrix products, arithmetic and copies ran while one was open for 2% -> 2% of each run, Pallas kernels for 12% -> 12%
where the time goes in v6:
time: 41.2 us; the launch traced here: 41 us
  starting transfers between devices  21 us (51%)
  waiting for transfers between devices  10.3 us (25%)
  Pallas kernels  8.12 us (20%)
  local copies, waits for them, and re-layouts  0.84 us (2%)
  between operations  0.74 us (2%)
    ppermute x17, starting transfers between devices, swap(): lax.ppermute(value, ('cls', 'dp'), [(i, i ^ mask) for i in range(groups *...  21 us
    ppermute x17, waiting for transfers between devices, swap(): lax.ppermute(value, ('cls', 'dp'), [(i, i ^ mask) for i in range(groups *...  10.3 us
    pallas_call x2, Pallas kernels, grads(): pl.pallas_call(functools.partial(grads_kernel, count, replicas, spans, si...  2.44 us
    pallas_call x2, Pallas kernels, per_device(): pl.pallas_call(functools.partial(logits_kernel, count, span, len(arrays[j...  2.42 us
    pallas_call x1, Pallas kernels, per_device(): pl.pallas_call(choose_kernel, out_shape=[jax.ShapeDtypeStruct((part + ext...  2.1 us
    pallas_call x1, Pallas kernels, per_device(): pl.pallas_call(finish_kernel, out_shape=jax.ShapeDtypeStruct((part, width...  0.91 us
  transfers between devices with their start and end apart: 17, of which 9 were waited for; matrix products, arithmetic and copies ran while one was open for 2% of the time, Pallas kernels for 12%

profile of v6, /device:TPU:0, one launch (start us, length us, event | category | flops | bytes accessed | tf_op | source)
XLA Modules:
  0.0 41.0 jit_solution(839992466336759826)
XLA Ops:
  0.6 0.0 copy-start
  0.6 0.0 copy-start.1
  0.6 4.1 %collective-permute-start = (bf16[128,512]{1,0:T(8,128)(2,1)}, bf16[128,512]{1,0:T(8,128)(2,1)S(1)}, u32[]{:S(2)}, u32[]{:S(2)}) collective-permute-start(bf16[128,512]{1,0:T(8,128)(2,1)} %refs_0_.1), channel_id=1, source_target_pairs={{0,16},{1,17},{2,18},{3,19},{4,20},{5,21},{6,22},{7,23},{8,24},{9,... | collective-permute-start | bytes 393224 | tf_op jit(solution)/shard_map/ppermute | solution.py:195
  4.8 1.6 %collective-permute-start.1 = (bf16[128,512]{1,0:T(8,128)(2,1)}, bf16[128,512]{1,0:T(8,128)(2,1)S(1)}, u32[]{:S(2)}, u32[]{:S(2)}) collective-permute-start(bf16[128,512]{1,0:T(8,128)(2,1)} %refs_0_.1), channel_id=1, source_target_pairs={{0,8},{1,9},{2,10},{3,11},{4,12},{5,13},{6,14},{7,15},{8,0},{9,1},... | collective-permute-start | bytes 393224 | tf_op jit(solution)/shard_map/ppermute | solution.py:195
  6.3 0.3 collective-permute-start.3
  6.7 0.8 %dynamic_slice.3.sampled_ref = s32[128]{0:T(128)S(1)} dynamic-slice(s32[256]{0:T(256)} %param.7, s32[]{:T(128)S(6)} %select_n.9), dynamic_slice_sizes={128} | dynamic-slice | bytes 1028 | tf_op jit(solution)/shard_map/dynamic_slice | solution.py:218
  7.4 2.1 %choose.1 = (bf16[136,512]{1,0:T(8,128)(2,1)S(1)}, f32[128,512]{1,0:T(8,128)S(1)}) custom-call(s32[128]{0:T(128)S(1)} %dynamic_slice.3.sampled_ref, f32[1024,512]{1,0:T(8,128)} %weight_hbm.1), custom_call_target="tpu_custom_call" | custom-call | tf_op jit(solution)/shard_map/choose/pallas_call | solution.py:207
  9.5 1.6 %collective-permute-start.8 = (bf16[136,512]{1,0:T(8,128)(2,1)S(1)}, bf16[136,512]{1,0:T(8,128)(2,1)S(1)}, u32[]{:S(2)}, u32[]{:S(2)}) collective-permute-start(bf16[136,512]{1,0:T(8,128)(2,1)S(1)} %get-tuple-element.45.refs_3_), channel_id=1, source_target_pairs={{0,2},{1,3},{2,0},{3,1},{4,6},{5,7},{6,4},{7,5},{8,10},{9,11},{10,... | collective-permute-start | bytes 417800 | tf_op jit(solution)/shard_map/ppermute | solution.py:195
  11.1 1.5 %collective-permute-start.7 = (bf16[136,512]{1,0:T(8,128)(2,1)S(1)}, bf16[136,512]{1,0:T(8,128)(2,1)S(1)}, u32[]{:S(2)}, u32[]{:S(2)}) collective-permute-start(bf16[136,512]{1,0:T(8,128)(2,1)S(1)} %get-tuple-element.45.refs_3_), channel_id=1, source_target_pairs={{0,4},{1,5},{2,6},{3,7},{4,0},{5,1},{6,2},{7,3},{8,12},{9,13},{10,... | collective-permute-start | bytes 417800 | tf_op jit(solution)/shard_map/ppermute | solution.py:195
  12.6 0.0 collective-permute-done.3
  12.6 0.0 copy-done.1
  12.6 1.4 %collective-permute-start.6 = (bf16[136,512]{1,0:T(8,128)(2,1)S(1)}, bf16[136,512]{1,0:T(8,128)(2,1)S(1)}, u32[]{:S(2)}, u32[]{:S(2)}) collective-permute-start(bf16[136,512]{1,0:T(8,128)(2,1)S(1)} %get-tuple-element.45.refs_3_), channel_id=1, source_target_pairs={{0,6},{1,7},{2,4},{3,5},{4,2},{5,3},{6,0},{7,1},{8,14},{9,15},{10,... | collective-permute-start | bytes 417800 | tf_op jit(solution)/shard_map/ppermute | solution.py:195
  14.0 0.0 collective-permute-done.feat_ref
  14.0 0.0 collective-permute-done.1.refs_1_
  14.0 0.1 pack.1.refs_1_
  14.1 1.5 %collective-permute-start.5 = (bf16[136,512]{1,0:T(8,128)(2,1)S(1)}, bf16[136,512]{1,0:T(8,128)(2,1)S(1)}, u32[]{:S(2)}, u32[]{:S(2)}) collective-permute-start(bf16[136,512]{1,0:T(8,128)(2,1)S(1)} %pack.1.refs_1_), channel_id=1, source_target_pairs={{0,8},{1,9},{2,10},{3,11},{4,12},{5,13},{6,14},{7,15},{8,0},{9,1},... | collective-permute-start | bytes 417800 | tf_op jit(solution)/shard_map/ppermute | solution.py:195
  15.6 0.1 stack.27.place_ref
  15.7 0.0 copy-done
  15.7 0.1 normalize.1.refs_0_
  15.9 0.1 collective-permute-start.2
  15.9 0.0 collective-permute-done.8.refs_4_
  16.0 0.5 %collective-permute-start.4 = (bf16[136,512]{1,0:T(8,128)(2,1)S(1)}, bf16[136,512]{1,0:T(8,128)(2,1)S(1)}, u32[]{:S(2)}, u32[]{:S(2)}) collective-permute-start(bf16[136,512]{1,0:T(8,128)(2,1)S(1)} %pack.1.refs_1_), channel_id=1, source_target_pairs={{0,1},{1,0},{2,3},{3,2},{4,5},{5,4},{6,7},{7,6},{8,9},{9,8},{10,11... | collective-permute-start | bytes 417800 | tf_op jit(solution)/shard_map/ppermute | solution.py:195
  16.4 2.7 %collective-permute-done.7.refs_5_ = bf16[136,512]{1,0:T(8,128)(2,1)S(1)} collective-permute-done((bf16[136,512]{1,0:T(8,128)(2,1)S(1)}, bf16[136,512]{1,0:T(8,128)(2,1)S(1)}, u32[]{:S(2)}, u32[]{:S(2)}) %collective-permute-start.7) | collective-permute-done | bytes 139296 | tf_op jit(solution)/shard_map/ppermute | solution.py:195
  19.1 0.0 collective-permute-done.6.refs_6_
  19.1 0.1 collective-permute-done.5.refs_2_
  19.3 0.0 collective-permute-start.9
  19.3 1.2 %logits.2 = (f32[512,512]{1,0:T(8,128)S(1)}, f32[16,128]{1,0:T(8,128)S(1)}, bf16[512,512]{1,0:T(8,128)(2,1)S(1)}, s32[4,128]{1,0:T(4,128)S(1)}, bf16[512,512]{1,0:T(8,128)(2,1)S(1)}) custom-call(s32[6]{0:T(128)S(1)} %stack.27.place_ref, bf16[256,512]{1,0:T(8,128)(2,1)S(1)} %normalize.1.refs_0_, bf16[136,512]{1,0:T(8,128)(2,1)S(1)} %pack.1.refs_1_, ...), custom_call_target="tpu_custom_call" | custom-call | tf_op jit(solution)/shard_map/logits/pallas_call | solution.py:284
  20.5 0.0 collective-permute-done.4.refs_1_
  20.5 0.0 collective-permute-done.2.refs_0_
  20.5 0.1 collective-permute-done.9.refs_2_
  20.6 1.2 %logits.3 = (f32[512,512]{1,0:T(8,128)S(1)}, f32[16,128]{1,0:T(8,128)S(1)}, bf16[512,512]{1,0:T(8,128)(2,1)S(1)}, s32[4,128]{1,0:T(4,128)S(1)}) custom-call(s32[6]{0:T(128)S(1)} %stack.27.place_ref, bf16[256,512]{1,0:T(8,128)(2,1)S(1)} %collective-permute-done.2.refs_0_, bf16[136,512]{1,0:T(8,128)(2,1)S(1)} %collective-permute-done.4.refs_1_, ...), custom_call_target="tpu_custom_call" | custom-call | tf_op jit(solution)/shard_map/logits/pallas_call | solution.py:284
  21.8 1.5 %collective-permute-start.12 = (f32[16,128]{1,0:T(8,128)S(1)}, f32[16,128]{1,0:T(8,128)S(1)}, u32[]{:S(2)}, u32[]{:S(2)}) collective-permute-start(f32[16,128]{1,0:T(8,128)S(1)} %get-tuple-element.51), channel_id=1, source_target_pairs={{0,9},{1,8},{2,11},{3,10},{4,13},{5,12},{6,15},{7,14},{8,1},{9,0},... | collective-permute-start | bytes 24584 | tf_op jit(solution)/shard_map/ppermute | solution.py:195
  23.4 0.6 %collective-permute-start.11 = (f32[16,128]{1,0:T(8,128)S(1)}, f32[16,128]{1,0:T(8,128)S(1)}, u32[]{:S(2)}, u32[]{:S(2)}) collective-permute-start(f32[16,128]{1,0:T(8,128)S(1)} %get-tuple-element.51), channel_id=1, source_target_pairs={{0,8},{1,9},{2,10},{3,11},{4,12},{5,13},{6,14},{7,15},{8,0},{9,1},... | collective-permute-start | bytes 24584 | tf_op jit(solution)/shard_map/ppermute | solution.py:195
  24.0 0.0 collective-permute-start.10
  24.0 1.0 %collective-permute-done.12 = f32[16,128]{1,0:T(8,128)S(1)} collective-permute-done((f32[16,128]{1,0:T(8,128)S(1)}, f32[16,128]{1,0:T(8,128)S(1)}, u32[]{:S(2)}, u32[]{:S(2)}) %collective-permute-start.12) | collective-permute-done | bytes 8224 | tf_op jit(solution)/shard_map/ppermute | solution.py:195
  25.0 2.0 %collective-permute-done.11 = f32[16,128]{1,0:T(8,128)S(1)} collective-permute-done((f32[16,128]{1,0:T(8,128)S(1)}, f32[16,128]{1,0:T(8,128)S(1)}, u32[]{:S(2)}, u32[]{:S(2)}) %collective-permute-start.11) | collective-permute-done | bytes 8224 | tf_op jit(solution)/shard_map/ppermute | solution.py:195
  27.0 0.0 collective-permute-done.10
  27.0 2.8 %collective-permute-start.13 = (f32[16,128]{1,0:T(8,128)S(1)}, f32[16,128]{1,0:T(8,128)S(1)}, u32[]{:S(2)}, u32[]{:S(2)}) collective-permute-start(f32[16,128]{1,0:T(8,128)S(1)} %add_add_fusion), channel_id=1, source_target_pairs={{0,16},{1,17},{2,18},{3,19},{4,20},{5,21},{6,22},{7,23},{8,24},{9,... | collective-permute-start | bytes 24584 | tf_op jit(solution)/shard_map/ppermute | solution.py:195
  29.8 1.9 %collective-permute-done.13 = f32[16,128]{1,0:T(8,128)S(1)} collective-permute-done((f32[16,128]{1,0:T(8,128)S(1)}, f32[16,128]{1,0:T(8,128)S(1)}, u32[]{:S(2)}, u32[]{:S(2)}) %collective-permute-start.13) | collective-permute-done | bytes 8224 | tf_op jit(solution)/shard_map/ppermute | solution.py:195
  31.6 1.2 %grads.3 = (bf16[128,512]{1,0:T(8,128)(2,1)S(1)}, bf16[128,512]{1,0:T(8,128)(2,1)S(1)}, bf16[128,512]{1,0:T(8,128)(2,1)S(1)}) custom-call(s32[6]{0:T(128)S(1)} %stack.27.place_ref, f32[16,128]{1,0:T(8,128)S(1)} %add.40.stat_ref, f32[512,512]{1,0:T(8,128)S(1)} %get-tuple-element.52.refs_0_, bf16[512,512]{1,0:T(8,128)(2,1)S(1)} %get-tuple-element.53.refs_1_, ...), custom_call_target="tpu_custom_call" | custom-call | tf_op jit(solution)/shard_map/grads/pallas_call | solution.py:305
  32.8 0.6 %collective-permute-start.14 = (bf16[128,512]{1,0:T(8,128)(2,1)S(1)}, bf16[128,512]{1,0:T(8,128)(2,1)S(1)}, u32[]{:S(2)}, u32[]{:S(2)}) collective-permute-start(bf16[128,512]{1,0:T(8,128)(2,1)S(1)} %get-tuple-element.61), channel_id=1, source_target_pairs={{0,2},{1,3},{2,0},{3,1},{4,6},{5,7},{6,4},{7,5},{8,10},{9,11},{10,... | collective-permute-start | bytes 393224 | tf_op jit(solution)/shard_map/ppermute | solution.py:195
  33.4 0.8 %collective-permute-start.15 = (bf16[128,512]{1,0:T(8,128)(2,1)S(1)}, bf16[128,512]{1,0:T(8,128)(2,1)S(1)}, u32[]{:S(2)}, u32[]{:S(2)}) collective-permute-start(bf16[128,512]{1,0:T(8,128)(2,1)S(1)} %get-tuple-element.62), channel_id=1, source_target_pairs={{0,4},{1,5},{2,6},{3,7},{4,0},{5,1},{6,2},{7,3},{8,12},{9,13},{10,... | collective-permute-start | bytes 393224 | tf_op jit(solution)/shard_map/ppermute | solution.py:195
  34.2 2.2 %collective-permute-start.16 = (bf16[128,512]{1,0:T(8,128)(2,1)S(1)}, bf16[128,512]{1,0:T(8,128)(2,1)S(1)}, u32[]{:S(2)}, u32[]{:S(2)}) collective-permute-start(bf16[128,512]{1,0:T(8,128)(2,1)S(1)} %get-tuple-element.63), channel_id=1, source_target_pairs={{0,6},{1,7},{2,4},{3,5},{4,2},{5,3},{6,0},{7,1},{8,14},{9,15},{10,... | collective-permute-start | bytes 393224 | tf_op jit(solution)/shard_map/ppermute | solution.py:195
  36.4 1.3 %grads.2 = (f32[128,512]{1,0:T(8,128)S(1)}, f32[1,128]{1,0:T(1,128)}) custom-call(s32[6]{0:T(128)S(1)} %stack.27.place_ref, f32[16,128]{1,0:T(8,128)S(1)} %add.40.stat_ref, f32[512,512]{1,0:T(8,128)S(1)} %get-tuple-element.52.refs_0_, bf16[512,512]{1,0:T(8,128)(2,1)S(1)} %get-tuple-element.53.refs_1_, s32[4,128]{1,0:T(4,128)S(1)} %get-tuple-element.54.refs_2_, ...), custom_call_target="tpu_custom_call" | custom-call | tf_op jit(solution)/shard_map/grads/pallas_call | solution.py:305
  37.6 0.2 collective-permute-done.14.refs_0_
  37.9 0.5 %collective-permute-done.15.refs_1_ = bf16[128,512]{1,0:T(8,128)(2,1)S(1)} collective-permute-done((bf16[128,512]{1,0:T(8,128)(2,1)S(1)}, bf16[128,512]{1,0:T(8,128)(2,1)S(1)}, u32[]{:S(2)}, u32[]{:S(2)}) %collective-permute-start.15) | collective-permute-done | bytes 131104 | tf_op jit(solution)/shard_map/ppermute | solution.py:195
  38.4 1.7 %collective-permute-done.16.refs_2_ = bf16[128,512]{1,0:T(8,128)(2,1)S(1)} collective-permute-done((bf16[128,512]{1,0:T(8,128)(2,1)S(1)}, bf16[128,512]{1,0:T(8,128)(2,1)S(1)}, u32[]{:S(2)}, u32[]{:S(2)}) %collective-permute-start.16) | collective-permute-done | bytes 131104 | tf_op jit(solution)/shard_map/ppermute | solution.py:195
  40.1 0.9 %finish.1 = f32[128,512]{1,0:T(8,128)} custom-call(f32[128,512]{1,0:T(8,128)S(1)} %get-tuple-element.59.chosen_ref, f32[128,512]{1,0:T(8,128)S(1)} %get-tuple-element.60.own_ref, bf16[128,512]{1,0:T(8,128)(2,1)S(1)} %collective-permute-done.14.refs_0_, bf16[128,512]{1,0:T(8,128)(2,1)S(1)} %collective-permute-done.15.refs_1_, ...), custom_call_target="tpu_custom_call" | custom-call | tf_op jit(solution)/shard_map/finish/pallas_call | solution.py:320
  (3 shorter events, 0.0 us)
Async XLA Ops:
  0.6 15.1 %copy-start = (bf16[128,512]{1,0:T(8,128)(2,1)S(1)}, bf16[128,512]{1,0:T(8,128)(2,1)}, u32[]{:S(2)}) copy-start(bf16[128,512]{1,0:T(8,128)(2,1)} %refs_0_.1) | copy-start | bytes 393220
  0.6 12.0 %copy-start.1 = (s32[128]{0:T(128)S(1)}, s32[128]{0:T(128)}, u32[]{:S(2)}) copy-start(s32[128]{0:T(128)} %param.5) | copy-start | bytes 1540
  0.6 13.4 %collective-permute-start = (bf16[128,512]{1,0:T(8,128)(2,1)}, bf16[128,512]{1,0:T(8,128)(2,1)S(1)}, u32[]{:S(2)}, u32[]{:S(2)}) collective-permute-start(bf16[128,512]{1,0:T(8,128)(2,1)} %refs_0_.1), channel_id=1, source_target_pairs={{0,16},{1,17},{2,18},{3,19},{4,20},{5,21},{6,22},{7,23},{8,24},{9,... | collective-permute-start | bytes 393224 | tf_op jit(solution)/shard_map/ppermute | solution.py:195
  4.8 9.3 %collective-permute-start.1 = (bf16[128,512]{1,0:T(8,128)(2,1)}, bf16[128,512]{1,0:T(8,128)(2,1)S(1)}, u32[]{:S(2)}, u32[]{:S(2)}) collective-permute-start(bf16[128,512]{1,0:T(8,128)(2,1)} %refs_0_.1), channel_id=1, source_target_pairs={{0,8},{1,9},{2,10},{3,11},{4,12},{5,13},{6,14},{7,15},{8,0},{9,1},... | collective-permute-start | bytes 393224 | tf_op jit(solution)/shard_map/ppermute | solution.py:195
  6.3 6.3 %collective-permute-start.3 = (s32[1,128]{1,0:T(1,128)}, s32[1,128]{1,0:T(1,128)S(1)}, u32[]{:S(2)}, u32[]{:S(2)}) collective-permute-start(s32[1,128]{1,0:T(1,128)} %bitcast.8), channel_id=1, source_target_pairs={{0,16},{1,17},{2,18},{3,19},{4,20},{5,21},{6,22},{7,23},{8,24},{9,... | collective-permute-start | bytes 1544 | tf_op jit(solution)/shard_map/ppermute | solution.py:195
  9.5 6.4 %collective-permute-start.8 = (bf16[136,512]{1,0:T(8,128)(2,1)S(1)}, bf16[136,512]{1,0:T(8,128)(2,1)S(1)}, u32[]{:S(2)}, u32[]{:S(2)}) collective-permute-start(bf16[136,512]{1,0:T(8,128)(2,1)S(1)} %get-tuple-element.45.refs_3_), channel_id=1, source_target_pairs={{0,2},{1,3},{2,0},{3,1},{4,6},{5,7},{6,4},{7,5},{8,10},{9,11},{10,... | collective-permute-start | bytes 417800 | tf_op jit(solution)/shard_map/ppermute | solution.py:195
  11.1 8.0 %collective-permute-start.7 = (bf16[136,512]{1,0:T(8,128)(2,1)S(1)}, bf16[136,512]{1,0:T(8,128)(2,1)S(1)}, u32[]{:S(2)}, u32[]{:S(2)}) collective-permute-start(bf16[136,512]{1,0:T(8,128)(2,1)S(1)} %get-tuple-element.45.refs_3_), channel_id=1, source_target_pairs={{0,4},{1,5},{2,6},{3,7},{4,0},{5,1},{6,2},{7,3},{8,12},{9,13},{10,... | collective-permute-start | bytes 417800 | tf_op jit(solution)/shard_map/ppermute | solution.py:195
  12.6 6.5 %collective-permute-start.6 = (bf16[136,512]{1,0:T(8,128)(2,1)S(1)}, bf16[136,512]{1,0:T(8,128)(2,1)S(1)}, u32[]{:S(2)}, u32[]{:S(2)}) collective-permute-start(bf16[136,512]{1,0:T(8,128)(2,1)S(1)} %get-tuple-element.45.refs_3_), channel_id=1, source_target_pairs={{0,6},{1,7},{2,4},{3,5},{4,2},{5,3},{6,0},{7,1},{8,14},{9,15},{10,... | collective-permute-start | bytes 417800 | tf_op jit(solution)/shard_map/ppermute | solution.py:195
  14.1 5.1 %collective-permute-start.5 = (bf16[136,512]{1,0:T(8,128)(2,1)S(1)}, bf16[136,512]{1,0:T(8,128)(2,1)S(1)}, u32[]{:S(2)}, u32[]{:S(2)}) collective-permute-start(bf16[136,512]{1,0:T(8,128)(2,1)S(1)} %pack.1.refs_1_), channel_id=1, source_target_pairs={{0,8},{1,9},{2,10},{3,11},{4,12},{5,13},{6,14},{7,15},{8,0},{9,1},... | collective-permute-start | bytes 417800 | tf_op jit(solution)/shard_map/ppermute | solution.py:195
  15.9 4.6 %collective-permute-start.2 = (bf16[256,512]{1,0:T(8,128)(2,1)S(1)}, bf16[256,512]{1,0:T(8,128)(2,1)S(1)}, u32[]{:S(2)}, u32[]{:S(2)}) collective-permute-start(bf16[256,512]{1,0:T(8,128)(2,1)S(1)} %normalize.1.refs_0_), channel_id=1, source_target_pairs={{0,1},{1,0},{2,3},{3,2},{4,5},{5,4},{6,7},{7,6},{8,9},{9,8},{10,11... | collective-permute-start | bytes 786440 | tf_op jit(solution)/shard_map/ppermute | solution.py:195
  16.0 4.5 %collective-permute-start.4 = (bf16[136,512]{1,0:T(8,128)(2,1)S(1)}, bf16[136,512]{1,0:T(8,128)(2,1)S(1)}, u32[]{:S(2)}, u32[]{:S(2)}) collective-permute-start(bf16[136,512]{1,0:T(8,128)(2,1)S(1)} %pack.1.refs_1_), channel_id=1, source_target_pairs={{0,1},{1,0},{2,3},{3,2},{4,5},{5,4},{6,7},{7,6},{8,9},{9,8},{10,11... | collective-permute-start | bytes 417800 | tf_op jit(solution)/shard_map/ppermute | solution.py:195
  19.3 1.4 %collective-permute-start.9 = (bf16[136,512]{1,0:T(8,128)(2,1)S(1)}, bf16[136,512]{1,0:T(8,128)(2,1)S(1)}, u32[]{:S(2)}, u32[]{:S(2)}) collective-permute-start(bf16[136,512]{1,0:T(8,128)(2,1)S(1)} %collective-permute-done.5.refs_2_), channel_id=1, source_target_pairs={{0,1},{1,0},{2,3},{3,2},{4,5},{5,4},{6,7},{7,6},{8,9},{9,8},{10,11... | collective-permute-start | bytes 417800 | tf_op jit(solution)/shard_map/ppermute | solution.py:195
  21.8 3.1 %collective-permute-start.12 = (f32[16,128]{1,0:T(8,128)S(1)}, f32[16,128]{1,0:T(8,128)S(1)}, u32[]{:S(2)}, u32[]{:S(2)}) collective-permute-start(f32[16,128]{1,0:T(8,128)S(1)} %get-tuple-element.51), channel_id=1, source_target_pairs={{0,9},{1,8},{2,11},{3,10},{4,13},{5,12},{6,15},{7,14},{8,1},{9,0},... | collective-permute-start | bytes 24584 | tf_op jit(solution)/shard_map/ppermute | solution.py:195
  23.4 3.7 %collective-permute-start.11 = (f32[16,128]{1,0:T(8,128)S(1)}, f32[16,128]{1,0:T(8,128)S(1)}, u32[]{:S(2)}, u32[]{:S(2)}) collective-permute-start(f32[16,128]{1,0:T(8,128)S(1)} %get-tuple-element.51), channel_id=1, source_target_pairs={{0,8},{1,9},{2,10},{3,11},{4,12},{5,13},{6,14},{7,15},{8,0},{9,1},... | collective-permute-start | bytes 24584 | tf_op jit(solution)/shard_map/ppermute | solution.py:195
  24.0 3.1 %collective-permute-start.10 = (f32[16,128]{1,0:T(8,128)S(1)}, f32[16,128]{1,0:T(8,128)S(1)}, u32[]{:S(2)}, u32[]{:S(2)}) collective-permute-start(f32[16,128]{1,0:T(8,128)S(1)} %get-tuple-element.51), channel_id=1, source_target_pairs={{0,1},{1,0},{2,3},{3,2},{4,5},{5,4},{6,7},{7,6},{8,9},{9,8},{10,11... | collective-permute-start | bytes 24584 | tf_op jit(solution)/shard_map/ppermute | solution.py:195
  27.0 4.6 %collective-permute-start.13 = (f32[16,128]{1,0:T(8,128)S(1)}, f32[16,128]{1,0:T(8,128)S(1)}, u32[]{:S(2)}, u32[]{:S(2)}) collective-permute-start(f32[16,128]{1,0:T(8,128)S(1)} %add_add_fusion), channel_id=1, source_target_pairs={{0,16},{1,17},{2,18},{3,19},{4,20},{5,21},{6,22},{7,23},{8,24},{9,... | collective-permute-start | bytes 24584 | tf_op jit(solution)/shard_map/ppermute | solution.py:195
  32.8 5.0 %collective-permute-start.14 = (bf16[128,512]{1,0:T(8,128)(2,1)S(1)}, bf16[128,512]{1,0:T(8,128)(2,1)S(1)}, u32[]{:S(2)}, u32[]{:S(2)}) collective-permute-start(bf16[128,512]{1,0:T(8,128)(2,1)S(1)} %get-tuple-element.61), channel_id=1, source_target_pairs={{0,2},{1,3},{2,0},{3,1},{4,6},{5,7},{6,4},{7,5},{8,10},{9,11},{10,... | collective-permute-start | bytes 393224 | tf_op jit(solution)/shard_map/ppermute | solution.py:195
  33.4 5.0 %collective-permute-start.15 = (bf16[128,512]{1,0:T(8,128)(2,1)S(1)}, bf16[128,512]{1,0:T(8,128)(2,1)S(1)}, u32[]{:S(2)}, u32[]{:S(2)}) collective-permute-start(bf16[128,512]{1,0:T(8,128)(2,1)S(1)} %get-tuple-element.62), channel_id=1, source_target_pairs={{0,4},{1,5},{2,6},{3,7},{4,0},{5,1},{6,2},{7,3},{8,12},{9,13},{10,... | collective-permute-start | bytes 393224 | tf_op jit(solution)/shard_map/ppermute | solution.py:195
  34.2 5.9 %collective-permute-start.16 = (bf16[128,512]{1,0:T(8,128)(2,1)S(1)}, bf16[128,512]{1,0:T(8,128)(2,1)S(1)}, u32[]{:S(2)}, u32[]{:S(2)}) collective-permute-start(bf16[128,512]{1,0:T(8,128)(2,1)S(1)} %get-tuple-element.63), channel_id=1, source_target_pairs={{0,6},{1,7},{2,4},{3,5},{4,2},{5,3},{6,0},{7,1},{8,14},{9,15},{10,... | collective-permute-start | bytes 393224 | tf_op jit(solution)/shard_map/ppermute | solution.py:195

commit v7 on v6

--- a/solution.py
+++ b/solution.py
@@ -290,12 +290,9 @@
             name="logits",
         )(place, *arrays[joined], *carried)
         chunks, carried = chunks + [exps, every, marks], together + [stats]
-    near = [(0, 0)]
-    for chip_bit, core_bit in bits[:1] + far_bits[:1]:
-        near = near + [(chip_mask | chip_bit, core_mask | core_bit) for chip_mask, core_mask in near]
-    stats = sum((swap(stats, *masks) for masks in near[1:]), stats)
-    for chip_mask, core_mask in bits[1:] + far_bits[1:]:
+    for chip_mask, core_mask in bits:
         stats = stats + swap(stats, chip_mask, core_mask)
+    stats = sum((swap(stats, mask, 0) for mask in range(square, groups, square)), stats)
 
     def grads(sides):
         kinds = [jnp.bfloat16 if side else jnp.float32 for side in sides]

time: 41.2 us -> 41.5 us (level)
    ppermute x17, waiting for transfers between devices: 10.3 us -> 10.7 us  [swap(): lax.ppermute(value, ('cls', 'dp'), [(i, i ^ mask) for i in range(groups *...]
  transfers between devices with their start and end apart: 17 -> 17, of which waited for: 9 -> 8; matrix products, arithmetic and copies ran while one was open for 2% -> 2% of each run, Pallas kernels for 12% -> 12%
where the time goes in v7:
time: 41.5 us; the launch traced here: 41.4 us
  starting transfers between devices  21 us (51%)
  waiting for transfers between devices  10.7 us (26%)
  Pallas kernels  8.1 us (20%)
  local copies, waits for them, and re-layouts  0.84 us (2%)
  between operations  0.74 us (2%)
    ppermute x17, starting transfers between devices, swap(): lax.ppermute(value, ('cls', 'dp'), [(i, i ^ mask) for i in range(groups *...  21 us
    ppermute x17, waiting for transfers between devices, swap(): lax.ppermute(value, ('cls', 'dp'), [(i, i ^ mask) for i in range(groups *...  10.7 us
    pallas_call x2, Pallas kernels, per_device(): pl.pallas_call(functools.partial(logits_kernel, count, span, len(arrays[j...  2.42 us
    pallas_call x2, Pallas kernels, grads(): pl.pallas_call(functools.partial(grads_kernel, count, replicas, spans, si...  2.42 us
    pallas_call x1, Pallas kernels, per_device(): pl.pallas_call(choose_kernel, out_shape=[jax.ShapeDtypeStruct((part + ext...  2.1 us
    pallas_call x1, Pallas kernels, per_device(): pl.pallas_call(finish_kernel, out_shape=jax.ShapeDtypeStruct((part, width...  0.91 us
  transfers between devices with their start and end apart: 17, of which 8 were waited for; matrix products, arithmetic and copies ran while one was open for 2% of the time, Pallas kernels for 12%

profile of v7, /device:TPU:0, one launch (start us, length us, event | category | flops | bytes accessed | tf_op | source)
XLA Modules:
  0.0 41.4 jit_solution(13332157952508662586)
XLA Ops:
  0.6 0.0 copy-start
  0.6 0.0 copy-start.1
  0.6 4.1 %collective-permute-start = (bf16[128,512]{1,0:T(8,128)(2,1)}, bf16[128,512]{1,0:T(8,128)(2,1)S(1)}, u32[]{:S(2)}, u32[]{:S(2)}) collective-permute-start(bf16[128,512]{1,0:T(8,128)(2,1)} %refs_0_.1), channel_id=1, source_target_pairs={{0,16},{1,17},{2,18},{3,19},{4,20},{5,21},{6,22},{7,23},{8,24},{9,... | collective-permute-start | bytes 393224 | tf_op jit(solution)/shard_map/ppermute | solution.py:195
  4.8 1.6 %collective-permute-start.1 = (bf16[128,512]{1,0:T(8,128)(2,1)}, bf16[128,512]{1,0:T(8,128)(2,1)S(1)}, u32[]{:S(2)}, u32[]{:S(2)}) collective-permute-start(bf16[128,512]{1,0:T(8,128)(2,1)} %refs_0_.1), channel_id=1, source_target_pairs={{0,8},{1,9},{2,10},{3,11},{4,12},{5,13},{6,14},{7,15},{8,0},{9,1},... | collective-permute-start | bytes 393224 | tf_op jit(solution)/shard_map/ppermute | solution.py:195
  6.3 0.3 collective-permute-start.3
  6.7 0.8 %dynamic_slice.3.sampled_ref = s32[128]{0:T(128)S(1)} dynamic-slice(s32[256]{0:T(256)} %param.7, s32[]{:T(128)S(6)} %select_n.9), dynamic_slice_sizes={128} | dynamic-slice | bytes 1028 | tf_op jit(solution)/shard_map/dynamic_slice | solution.py:218
  7.4 2.1 %choose.1 = (bf16[136,512]{1,0:T(8,128)(2,1)S(1)}, f32[128,512]{1,0:T(8,128)S(1)}) custom-call(s32[128]{0:T(128)S(1)} %dynamic_slice.3.sampled_ref, f32[1024,512]{1,0:T(8,128)} %weight_hbm.1), custom_call_target="tpu_custom_call" | custom-call | tf_op jit(solution)/shard_map/choose/pallas_call | solution.py:207
  9.5 1.6 %collective-permute-start.8 = (bf16[136,512]{1,0:T(8,128)(2,1)S(1)}, bf16[136,512]{1,0:T(8,128)(2,1)S(1)}, u32[]{:S(2)}, u32[]{:S(2)}) collective-permute-start(bf16[136,512]{1,0:T(8,128)(2,1)S(1)} %get-tuple-element.45.refs_3_), channel_id=1, source_target_pairs={{0,2},{1,3},{2,0},{3,1},{4,6},{5,7},{6,4},{7,5},{8,10},{9,11},{10,... | collective-permute-start | bytes 417800 | tf_op jit(solution)/shard_map/ppermute | solution.py:195
  11.1 1.5 %collective-permute-start.7 = (bf16[136,512]{1,0:T(8,128)(2,1)S(1)}, bf16[136,512]{1,0:T(8,128)(2,1)S(1)}, u32[]{:S(2)}, u32[]{:S(2)}) collective-permute-start(bf16[136,512]{1,0:T(8,128)(2,1)S(1)} %get-tuple-element.45.refs_3_), channel_id=1, source_target_pairs={{0,4},{1,5},{2,6},{3,7},{4,0},{5,1},{6,2},{7,3},{8,12},{9,13},{10,... | collective-permute-start | bytes 417800 | tf_op jit(solution)/shard_map/ppermute | solution.py:195
  12.6 0.0 collective-permute-done.3
  12.6 0.0 copy-done.1
  12.6 1.4 %collective-permute-start.6 = (bf16[136,512]{1,0:T(8,128)(2,1)S(1)}, bf16[136,512]{1,0:T(8,128)(2,1)S(1)}, u32[]{:S(2)}, u32[]{:S(2)}) collective-permute-start(bf16[136,512]{1,0:T(8,128)(2,1)S(1)} %get-tuple-element.45.refs_3_), channel_id=1, source_target_pairs={{0,6},{1,7},{2,4},{3,5},{4,2},{5,3},{6,0},{7,1},{8,14},{9,15},{10,... | collective-permute-start | bytes 417800 | tf_op jit(solution)/shard_map/ppermute | solution.py:195
  14.0 0.0 collective-permute-done.feat_ref
  14.0 0.0 collective-permute-done.1.refs_1_
  14.0 0.1 pack.1.refs_1_
  14.1 1.5 %collective-permute-start.5 = (bf16[136,512]{1,0:T(8,128)(2,1)S(1)}, bf16[136,512]{1,0:T(8,128)(2,1)S(1)}, u32[]{:S(2)}, u32[]{:S(2)}) collective-permute-start(bf16[136,512]{1,0:T(8,128)(2,1)S(1)} %pack.1.refs_1_), channel_id=1, source_target_pairs={{0,8},{1,9},{2,10},{3,11},{4,12},{5,13},{6,14},{7,15},{8,0},{9,1},... | collective-permute-start | bytes 417800 | tf_op jit(solution)/shard_map/ppermute | solution.py:195
  15.6 0.1 stack.27.place_ref
  15.7 0.0 copy-done
  15.7 0.1 normalize.1.refs_0_
  15.9 0.1 collective-permute-start.2
  15.9 0.0 collective-permute-done.8.refs_4_
  16.0 0.5 %collective-permute-start.4 = (bf16[136,512]{1,0:T(8,128)(2,1)S(1)}, bf16[136,512]{1,0:T(8,128)(2,1)S(1)}, u32[]{:S(2)}, u32[]{:S(2)}) collective-permute-start(bf16[136,512]{1,0:T(8,128)(2,1)S(1)} %pack.1.refs_1_), channel_id=1, source_target_pairs={{0,1},{1,0},{2,3},{3,2},{4,5},{5,4},{6,7},{7,6},{8,9},{9,8},{10,11... | collective-permute-start | bytes 417800 | tf_op jit(solution)/shard_map/ppermute | solution.py:195
  16.4 2.7 %collective-permute-done.7.refs_5_ = bf16[136,512]{1,0:T(8,128)(2,1)S(1)} collective-permute-done((bf16[136,512]{1,0:T(8,128)(2,1)S(1)}, bf16[136,512]{1,0:T(8,128)(2,1)S(1)}, u32[]{:S(2)}, u32[]{:S(2)}) %collective-permute-start.7) | collective-permute-done | bytes 139296 | tf_op jit(solution)/shard_map/ppermute | solution.py:195
  19.1 0.0 collective-permute-done.6.refs_6_
  19.1 0.1 collective-permute-done.5.refs_2_
  19.3 0.0 collective-permute-start.9
  19.3 1.2 %logits.2 = (f32[512,512]{1,0:T(8,128)S(1)}, f32[16,128]{1,0:T(8,128)S(1)}, bf16[512,512]{1,0:T(8,128)(2,1)S(1)}, s32[4,128]{1,0:T(4,128)S(1)}, bf16[512,512]{1,0:T(8,128)(2,1)S(1)}) custom-call(s32[6]{0:T(128)S(1)} %stack.27.place_ref, bf16[256,512]{1,0:T(8,128)(2,1)S(1)} %normalize.1.refs_0_, bf16[136,512]{1,0:T(8,128)(2,1)S(1)} %pack.1.refs_1_, ...), custom_call_target="tpu_custom_call" | custom-call | tf_op jit(solution)/shard_map/logits/pallas_call | solution.py:284
  20.5 0.0 collective-permute-done.4.refs_1_
  20.5 0.0 collective-permute-done.2.refs_0_
  20.5 0.1 collective-permute-done.9.refs_2_
  20.6 1.2 %logits.3 = (f32[512,512]{1,0:T(8,128)S(1)}, f32[16,128]{1,0:T(8,128)S(1)}, bf16[512,512]{1,0:T(8,128)(2,1)S(1)}, s32[4,128]{1,0:T(4,128)S(1)}) custom-call(s32[6]{0:T(128)S(1)} %stack.27.place_ref, bf16[256,512]{1,0:T(8,128)(2,1)S(1)} %collective-permute-done.2.refs_0_, bf16[136,512]{1,0:T(8,128)(2,1)S(1)} %collective-permute-done.4.refs_1_, ...), custom_call_target="tpu_custom_call" | custom-call | tf_op jit(solution)/shard_map/logits/pallas_call | solution.py:284
  21.8 0.5 %collective-permute-start.10 = (f32[16,128]{1,0:T(8,128)S(1)}, f32[16,128]{1,0:T(8,128)S(1)}, u32[]{:S(2)}, u32[]{:S(2)}) collective-permute-start(f32[16,128]{1,0:T(8,128)S(1)} %get-tuple-element.51), channel_id=1, source_target_pairs={{0,1},{1,0},{2,3},{3,2},{4,5},{5,4},{6,7},{7,6},{8,9},{9,8},{10,11... | collective-permute-start | bytes 24584 | tf_op jit(solution)/shard_map/ppermute | solution.py:195
  22.3 0.8 %collective-permute-done.10 = f32[16,128]{1,0:T(8,128)S(1)} collective-permute-done((f32[16,128]{1,0:T(8,128)S(1)}, f32[16,128]{1,0:T(8,128)S(1)}, u32[]{:S(2)}, u32[]{:S(2)}) %collective-permute-start.10) | collective-permute-done | bytes 8224 | tf_op jit(solution)/shard_map/ppermute | solution.py:195
  23.1 3.6 %collective-permute-start.13 = (f32[16,128]{1,0:T(8,128)S(1)}, f32[16,128]{1,0:T(8,128)S(1)}, u32[]{:S(2)}, u32[]{:S(2)}) collective-permute-start(f32[16,128]{1,0:T(8,128)S(1)} %add.37), channel_id=1, source_target_pairs={{0,24},{1,25},{2,26},{3,27},{4,28},{5,29},{6,30},{7,31},{8,16},{9,... | collective-permute-start | bytes 24584 | tf_op jit(solution)/shard_map/ppermute | solution.py:195
  26.7 0.0 collective-permute-start.12
  26.7 0.8 %collective-permute-start.11 = (f32[16,128]{1,0:T(8,128)S(1)}, f32[16,128]{1,0:T(8,128)S(1)}, u32[]{:S(2)}, u32[]{:S(2)}) collective-permute-start(f32[16,128]{1,0:T(8,128)S(1)} %add.37), channel_id=1, source_target_pairs={{0,8},{1,9},{2,10},{3,11},{4,12},{5,13},{6,14},{7,15},{8,0},{9,1},... | collective-permute-start | bytes 24584 | tf_op jit(solution)/shard_map/ppermute | solution.py:195
  27.5 1.1 %collective-permute-done.13 = f32[16,128]{1,0:T(8,128)S(1)} collective-permute-done((f32[16,128]{1,0:T(8,128)S(1)}, f32[16,128]{1,0:T(8,128)S(1)}, u32[]{:S(2)}, u32[]{:S(2)}) %collective-permute-start.13) | collective-permute-done | bytes 8224 | tf_op jit(solution)/shard_map/ppermute | solution.py:195
  28.6 2.7 %collective-permute-done.12 = f32[16,128]{1,0:T(8,128)S(1)} collective-permute-done((f32[16,128]{1,0:T(8,128)S(1)}, f32[16,128]{1,0:T(8,128)S(1)}, u32[]{:S(2)}, u32[]{:S(2)}) %collective-permute-start.12) | collective-permute-done | bytes 8224 | tf_op jit(solution)/shard_map/ppermute | solution.py:195
  31.3 0.0 collective-permute-done.11
  31.3 1.2 %grads.3 = (bf16[128,512]{1,0:T(8,128)(2,1)S(1)}, bf16[128,512]{1,0:T(8,128)(2,1)S(1)}, bf16[128,512]{1,0:T(8,128)(2,1)S(1)}) custom-call(s32[6]{0:T(128)S(1)} %stack.27.place_ref, f32[16,128]{1,0:T(8,128)S(1)} %add_add_fusion.stat_ref, f32[512,512]{1,0:T(8,128)S(1)} %get-tuple-element.52.refs_0_, bf16[512,512]{1,0:T(8,128)(2,1)S(1)} %get-tuple-element.53.refs_1_, ...), custom_call_target="tpu_custom_call" | custom-call | tf_op jit(solution)/shard_map/grads/pallas_call | solution.py:302
  32.4 0.6 %collective-permute-start.14 = (bf16[128,512]{1,0:T(8,128)(2,1)S(1)}, bf16[128,512]{1,0:T(8,128)(2,1)S(1)}, u32[]{:S(2)}, u32[]{:S(2)}) collective-permute-start(bf16[128,512]{1,0:T(8,128)(2,1)S(1)} %get-tuple-element.61), channel_id=1, source_target_pairs={{0,2},{1,3},{2,0},{3,1},{4,6},{5,7},{6,4},{7,5},{8,10},{9,11},{10,... | collective-permute-start | bytes 393224 | tf_op jit(solution)/shard_map/ppermute | solution.py:195
  33.0 1.0 %collective-permute-start.15 = (bf16[128,512]{1,0:T(8,128)(2,1)S(1)}, bf16[128,512]{1,0:T(8,128)(2,1)S(1)}, u32[]{:S(2)}, u32[]{:S(2)}) collective-permute-start(bf16[128,512]{1,0:T(8,128)(2,1)S(1)} %get-tuple-element.62), channel_id=1, source_target_pairs={{0,4},{1,5},{2,6},{3,7},{4,0},{5,1},{6,2},{7,3},{8,12},{9,13},{10,... | collective-permute-start | bytes 393224 | tf_op jit(solution)/shard_map/ppermute | solution.py:195
  34.1 1.9 %collective-permute-start.16 = (bf16[128,512]{1,0:T(8,128)(2,1)S(1)}, bf16[128,512]{1,0:T(8,128)(2,1)S(1)}, u32[]{:S(2)}, u32[]{:S(2)}) collective-permute-start(bf16[128,512]{1,0:T(8,128)(2,1)S(1)} %get-tuple-element.63), channel_id=1, source_target_pairs={{0,6},{1,7},{2,4},{3,5},{4,2},{5,3},{6,0},{7,1},{8,14},{9,15},{10,... | collective-permute-start | bytes 393224 | tf_op jit(solution)/shard_map/ppermute | solution.py:195
  36.0 1.3 %grads.2 = (f32[128,512]{1,0:T(8,128)S(1)}, f32[1,128]{1,0:T(1,128)}) custom-call(s32[6]{0:T(128)S(1)} %stack.27.place_ref, f32[16,128]{1,0:T(8,128)S(1)} %add_add_fusion.stat_ref, f32[512,512]{1,0:T(8,128)S(1)} %get-tuple-element.52.refs_0_, bf16[512,512]{1,0:T(8,128)(2,1)S(1)} %get-tuple-element.53.refs_1_, s32[4,128]{1,0:T(4,128)S(1)} %get-tuple-element.54.refs_2_, ...), custom_call_target="tpu_custom_call" | custom-call | tf_op jit(solution)/shard_map/grads/pallas_call | solution.py:302
  37.3 1.0 %collective-permute-done.14.refs_0_ = bf16[128,512]{1,0:T(8,128)(2,1)S(1)} collective-permute-done((bf16[128,512]{1,0:T(8,128)(2,1)S(1)}, bf16[128,512]{1,0:T(8,128)(2,1)S(1)}, u32[]{:S(2)}, u32[]{:S(2)}) %collective-permute-start.14) | collective-permute-done | bytes 131104 | tf_op jit(solution)/shard_map/ppermute | solution.py:195
  38.3 2.1 %collective-permute-done.15.refs_1_ = bf16[128,512]{1,0:T(8,128)(2,1)S(1)} collective-permute-done((bf16[128,512]{1,0:T(8,128)(2,1)S(1)}, bf16[128,512]{1,0:T(8,128)(2,1)S(1)}, u32[]{:S(2)}, u32[]{:S(2)}) %collective-permute-start.15) | collective-permute-done | bytes 131104 | tf_op jit(solution)/shard_map/ppermute | solution.py:195
  40.4 0.0 collective-permute-done.16.refs_2_
  40.4 0.9 %finish.1 = f32[128,512]{1,0:T(8,128)} custom-call(f32[128,512]{1,0:T(8,128)S(1)} %get-tuple-element.59.chosen_ref, f32[128,512]{1,0:T(8,128)S(1)} %get-tuple-element.60.own_ref, bf16[128,512]{1,0:T(8,128)(2,1)S(1)} %collective-permute-done.14.refs_0_, bf16[128,512]{1,0:T(8,128)(2,1)S(1)} %collective-permute-done.15.refs_1_, ...), custom_call_target="tpu_custom_call" | custom-call | tf_op jit(solution)/shard_map/finish/pallas_call | solution.py:317
  (3 shorter events, 0.0 us)
Async XLA Ops:
  0.6 15.1 %copy-start = (bf16[128,512]{1,0:T(8,128)(2,1)S(1)}, bf16[128,512]{1,0:T(8,128)(2,1)}, u32[]{:S(2)}) copy-start(bf16[128,512]{1,0:T(8,128)(2,1)} %refs_0_.1) | copy-start | bytes 393220
  0.6 12.0 %copy-start.1 = (s32[128]{0:T(128)S(1)}, s32[128]{0:T(128)}, u32[]{:S(2)}) copy-start(s32[128]{0:T(128)} %param.5) | copy-start | bytes 1540
  0.6 13.4 %collective-permute-start = (bf16[128,512]{1,0:T(8,128)(2,1)}, bf16[128,512]{1,0:T(8,128)(2,1)S(1)}, u32[]{:S(2)}, u32[]{:S(2)}) collective-permute-start(bf16[128,512]{1,0:T(8,128)(2,1)} %refs_0_.1), channel_id=1, source_target_pairs={{0,16},{1,17},{2,18},{3,19},{4,20},{5,21},{6,22},{7,23},{8,24},{9,... | collective-permute-start | bytes 393224 | tf_op jit(solution)/shard_map/ppermute | solution.py:195
  4.8 9.3 %collective-permute-start.1 = (bf16[128,512]{1,0:T(8,128)(2,1)}, bf16[128,512]{1,0:T(8,128)(2,1)S(1)}, u32[]{:S(2)}, u32[]{:S(2)}) collective-permute-start(bf16[128,512]{1,0:T(8,128)(2,1)} %refs_0_.1), channel_id=1, source_target_pairs={{0,8},{1,9},{2,10},{3,11},{4,12},{5,13},{6,14},{7,15},{8,0},{9,1},... | collective-permute-start | bytes 393224 | tf_op jit(solution)/shard_map/ppermute | solution.py:195
  6.3 6.3 %collective-permute-start.3 = (s32[1,128]{1,0:T(1,128)}, s32[1,128]{1,0:T(1,128)S(1)}, u32[]{:S(2)}, u32[]{:S(2)}) collective-permute-start(s32[1,128]{1,0:T(1,128)} %bitcast.8), channel_id=1, source_target_pairs={{0,16},{1,17},{2,18},{3,19},{4,20},{5,21},{6,22},{7,23},{8,24},{9,... | collective-permute-start | bytes 1544 | tf_op jit(solution)/shard_map/ppermute | solution.py:195
  9.5 6.4 %collective-permute-start.8 = (bf16[136,512]{1,0:T(8,128)(2,1)S(1)}, bf16[136,512]{1,0:T(8,128)(2,1)S(1)}, u32[]{:S(2)}, u32[]{:S(2)}) collective-permute-start(bf16[136,512]{1,0:T(8,128)(2,1)S(1)} %get-tuple-element.45.refs_3_), channel_id=1, source_target_pairs={{0,2},{1,3},{2,0},{3,1},{4,6},{5,7},{6,4},{7,5},{8,10},{9,11},{10,... | collective-permute-start | bytes 417800 | tf_op jit(solution)/shard_map/ppermute | solution.py:195
  11.1 8.0 %collective-permute-start.7 = (bf16[136,512]{1,0:T(8,128)(2,1)S(1)}, bf16[136,512]{1,0:T(8,128)(2,1)S(1)}, u32[]{:S(2)}, u32[]{:S(2)}) collective-permute-start(bf16[136,512]{1,0:T(8,128)(2,1)S(1)} %get-tuple-element.45.refs_3_), channel_id=1, source_target_pairs={{0,4},{1,5},{2,6},{3,7},{4,0},{5,1},{6,2},{7,3},{8,12},{9,13},{10,... | collective-permute-start | bytes 417800 | tf_op jit(solution)/shard_map/ppermute | solution.py:195
  12.6 6.5 %collective-permute-start.6 = (bf16[136,512]{1,0:T(8,128)(2,1)S(1)}, bf16[136,512]{1,0:T(8,128)(2,1)S(1)}, u32[]{:S(2)}, u32[]{:S(2)}) collective-permute-start(bf16[136,512]{1,0:T(8,128)(2,1)S(1)} %get-tuple-element.45.refs_3_), channel_id=1, source_target_pairs={{0,6},{1,7},{2,4},{3,5},{4,2},{5,3},{6,0},{7,1},{8,14},{9,15},{10,... | collective-permute-start | bytes 417800 | tf_op jit(solution)/shard_map/ppermute | solution.py:195
  14.1 5.1 %collective-permute-start.5 = (bf16[136,512]{1,0:T(8,128)(2,1)S(1)}, bf16[136,512]{1,0:T(8,128)(2,1)S(1)}, u32[]{:S(2)}, u32[]{:S(2)}) collective-permute-start(bf16[136,512]{1,0:T(8,128)(2,1)S(1)} %pack.1.refs_1_), channel_id=1, source_target_pairs={{0,8},{1,9},{2,10},{3,11},{4,12},{5,13},{6,14},{7,15},{8,0},{9,1},... | collective-permute-start | bytes 417800 | tf_op jit(solution)/shard_map/ppermute | solution.py:195
  15.9 4.6 %collective-permute-start.2 = (bf16[256,512]{1,0:T(8,128)(2,1)S(1)}, bf16[256,512]{1,0:T(8,128)(2,1)S(1)}, u32[]{:S(2)}, u32[]{:S(2)}) collective-permute-start(bf16[256,512]{1,0:T(8,128)(2,1)S(1)} %normalize.1.refs_0_), channel_id=1, source_target_pairs={{0,1},{1,0},{2,3},{3,2},{4,5},{5,4},{6,7},{7,6},{8,9},{9,8},{10,11... | collective-permute-start | bytes 786440 | tf_op jit(solution)/shard_map/ppermute | solution.py:195
  16.0 4.5 %collective-permute-start.4 = (bf16[136,512]{1,0:T(8,128)(2,1)S(1)}, bf16[136,512]{1,0:T(8,128)(2,1)S(1)}, u32[]{:S(2)}, u32[]{:S(2)}) collective-permute-start(bf16[136,512]{1,0:T(8,128)(2,1)S(1)} %pack.1.refs_1_), channel_id=1, source_target_pairs={{0,1},{1,0},{2,3},{3,2},{4,5},{5,4},{6,7},{7,6},{8,9},{9,8},{10,11... | collective-permute-start | bytes 417800 | tf_op jit(solution)/shard_map/ppermute | solution.py:195
  19.3 1.4 %collective-permute-start.9 = (bf16[136,512]{1,0:T(8,128)(2,1)S(1)}, bf16[136,512]{1,0:T(8,128)(2,1)S(1)}, u32[]{:S(2)}, u32[]{:S(2)}) collective-permute-start(bf16[136,512]{1,0:T(8,128)(2,1)S(1)} %collective-permute-done.5.refs_2_), channel_id=1, source_target_pairs={{0,1},{1,0},{2,3},{3,2},{4,5},{5,4},{6,7},{7,6},{8,9},{9,8},{10,11... | collective-permute-start | bytes 417800 | tf_op jit(solution)/shard_map/ppermute | solution.py:195
  21.8 1.3 %collective-permute-start.10 = (f32[16,128]{1,0:T(8,128)S(1)}, f32[16,128]{1,0:T(8,128)S(1)}, u32[]{:S(2)}, u32[]{:S(2)}) collective-permute-start(f32[16,128]{1,0:T(8,128)S(1)} %get-tuple-element.51), channel_id=1, source_target_pairs={{0,1},{1,0},{2,3},{3,2},{4,5},{5,4},{6,7},{7,6},{8,9},{9,8},{10,11... | collective-permute-start | bytes 24584 | tf_op jit(solution)/shard_map/ppermute | solution.py:195
  23.1 5.4 %collective-permute-start.13 = (f32[16,128]{1,0:T(8,128)S(1)}, f32[16,128]{1,0:T(8,128)S(1)}, u32[]{:S(2)}, u32[]{:S(2)}) collective-permute-start(f32[16,128]{1,0:T(8,128)S(1)} %add.37), channel_id=1, source_target_pairs={{0,24},{1,25},{2,26},{3,27},{4,28},{5,29},{6,30},{7,31},{8,16},{9,... | collective-permute-start | bytes 24584 | tf_op jit(solution)/shard_map/ppermute | solution.py:195
  26.7 4.5 %collective-permute-start.12 = (f32[16,128]{1,0:T(8,128)S(1)}, f32[16,128]{1,0:T(8,128)S(1)}, u32[]{:S(2)}, u32[]{:S(2)}) collective-permute-start(f32[16,128]{1,0:T(8,128)S(1)} %add.37), channel_id=1, source_target_pairs={{0,16},{1,17},{2,18},{3,19},{4,20},{5,21},{6,22},{7,23},{8,24},{9,... | collective-permute-start | bytes 24584 | tf_op jit(solution)/shard_map/ppermute | solution.py:195
  26.7 4.5 %collective-permute-start.11 = (f32[16,128]{1,0:T(8,128)S(1)}, f32[16,128]{1,0:T(8,128)S(1)}, u32[]{:S(2)}, u32[]{:S(2)}) collective-permute-start(f32[16,128]{1,0:T(8,128)S(1)} %add.37), channel_id=1, source_target_pairs={{0,8},{1,9},{2,10},{3,11},{4,12},{5,13},{6,14},{7,15},{8,0},{9,1},... | collective-permute-start | bytes 24584 | tf_op jit(solution)/shard_map/ppermute | solution.py:195
  32.4 5.9 %collective-permute-start.14 = (bf16[128,512]{1,0:T(8,128)(2,1)S(1)}, bf16[128,512]{1,0:T(8,128)(2,1)S(1)}, u32[]{:S(2)}, u32[]{:S(2)}) collective-permute-start(bf16[128,512]{1,0:T(8,128)(2,1)S(1)} %get-tuple-element.61), channel_id=1, source_target_pairs={{0,2},{1,3},{2,0},{3,1},{4,6},{5,7},{6,4},{7,5},{8,10},{9,11},{10,... | collective-permute-start | bytes 393224 | tf_op jit(solution)/shard_map/ppermute | solution.py:195
  33.0 7.4 %collective-permute-start.15 = (bf16[128,512]{1,0:T(8,128)(2,1)S(1)}, bf16[128,512]{1,0:T(8,128)(2,1)S(1)}, u32[]{:S(2)}, u32[]{:S(2)}) collective-permute-start(bf16[128,512]{1,0:T(8,128)(2,1)S(1)} %get-tuple-element.62), channel_id=1, source_target_pairs={{0,4},{1,5},{2,6},{3,7},{4,0},{5,1},{6,2},{7,3},{8,12},{9,13},{10,... | collective-permute-start | bytes 393224 | tf_op jit(solution)/shard_map/ppermute | solution.py:195
  34.1 6.4 %collective-permute-start.16 = (bf16[128,512]{1,0:T(8,128)(2,1)S(1)}, bf16[128,512]{1,0:T(8,128)(2,1)S(1)}, u32[]{:S(2)}, u32[]{:S(2)}) collective-permute-start(bf16[128,512]{1,0:T(8,128)(2,1)S(1)} %get-tuple-element.63), channel_id=1, source_target_pairs={{0,6},{1,7},{2,4},{3,5},{4,2},{5,3},{6,0},{7,1},{8,14},{9,15},{10,... | collective-permute-start | bytes 393224 | tf_op jit(solution)/shard_map/ppermute | solution.py:195
